TPU v7x, 32 devices: a whole 2x2x4 slice. The times are simulated.
32 devices in a mesh: blk: 8 (over z, core), user: 4 (over y, x).
Axes of the slice: x: 2, y: 2, z: 4, core: 2. Of those that a mesh axis runs over, the one named last changes fastest.
Arguments:
- user_factors: float32 [131072, 256], P(('blk', 'user')), may hold values from -2 to 2
- item_factors: float32 [8192, 256], P(('blk', 'user')), may hold values from -2 to 2
- block_index: int32 [3, 256, 2, 4], P(None, ('blk', 'user')), may hold values from 0 to 15, as said below
- block_count: int32 [3, 256, 2], P(None, ('blk', 'user')), may hold values from 1 to 4
- ratings: int32 [3, 256, 2, 4, 128, 128], P(None, ('blk', 'user')), may hold values from 0 to 10
Outputs:
- users_out: float32 [131072, 256], P(('blk', 'user'))
- items_out: float32 [8192, 256], P(('blk', 'user'))
Inputs may be any that keep to these rules, and one draw needn't show every extreme that they name: `block_index`: the 4 block numbers of one tile are distinct.
All inputs are finite; a program needn't handle non-finite values.
Results may differ from a plain program's by a relative error of at most 0.0003.
Values sent between devices are 32-bit elements; how exact they have to be, the bound alone decides.
No kernel may reach another device: no remote copies, remote signals or barrier semaphores. Data moves between devices by JAX's collectives and lax.ppermute only.
A program may use at most 128 MiB of HBM per device.

v0:
```python
import functools

import jax
import jax.numpy as jnp
from jax import lax
from jax.experimental import pallas as pl
from jax.experimental.pallas import tpu as pltpu
from jax.sharding import PartitionSpec as P

user_rate = 0.01
item_rate = 0.0015
decay_rate = 0.05
GROUPS = (8, 4)


def divided(x, n):
    return x >> (n.bit_length() - 1) if n & (n - 1) == 0 else lax.div(x, n)


def left_over(x, n):
    return x & (n - 1) if n & (n - 1) == 0 else lax.rem(x, n)


def partner(u, r, n):
    return u ^ r if n & (n - 1) == 0 else (u + r) % n


def source(u, r, n):
    return u ^ r if n & (n - 1) == 0 else (u - r + n) % n


def moved(x, step, r, nb, nu):
    route = [
        (b * nu + u, ((b + step) % nb) * nu + partner(u, r, nu))
        for b in range(nb)
        for u in range(nu)
    ]
    return lax.ppermute(x, ("blk", "user"), route)


def split(x):
    hi = x.astype(jnp.bfloat16)
    return hi, (x - hi.astype(jnp.float32)).astype(jnp.bfloat16)


def dot(a, b):
    return jnp.dot(a, b, preferred_element_type=jnp.float32)


def dot_rows(a, b):
    return lax.dot_general(a, b, (((1,), (1,)), ((), ())), preferred_element_type=jnp.float32)


def dot_split(x_hi, x_lo, y_hi, y_lo):
    wide = jnp.concatenate([x_hi, x_lo], axis=1)
    return dot(wide, jnp.concatenate([y_hi, y_hi], axis=0)) + dot(x_hi, y_lo)


def over_groups(count, body):
    first = 0
    for i, size in enumerate(GROUPS):
        groups = divided(count - first + (size - 1 if i + 1 == len(GROUPS) else 0), size)

        def step(g, carry, first=first, size=size):
            body(first + g * size, size)
            return carry

        lax.fori_loop(0, groups, step, 0)
        first = first + groups * size


class Shape:
    def __init__(self, user_factors, item_factors, block_index, ratings):
        self.steps, self.tile_rows, self.tile_cols, self.slots = block_index.shape
        self.block = ratings.shape[-1]
        self.rank = user_factors.shape[1]
        self.parts = user_factors.shape[0] // (self.tile_rows * self.block)
        self.chunks = item_factors.shape[0] // self.block
        self.total = self.tile_rows * self.tile_cols * self.slots
        self.user_blocks = self.tile_rows * self.parts

    def entry(self, packed):
        q = left_over(packed, self.parts * self.parts)
        slot = divided(packed, self.parts * self.parts)
        tile = divided(slot, self.slots)
        row = divided(tile, self.tile_cols) * self.parts + divided(q, self.parts)
        col = left_over(tile, self.tile_cols) * self.parts + left_over(q, self.parts)
        return slot, row, divided(col, self.chunks)


def load_kernel(sh, index_ref, count_ref, users_in, ratings_in, users, ratings, lists, sems):
    copies = [
        pltpu.make_async_copy(users_in, users, sems.at[0]),
        pltpu.make_async_copy(ratings_in.at[pl.ds(0, sh.total)], ratings, sems.at[1]),
    ]
    for copy in copies:
        copy.start()
    for s in range(sh.steps):

        def tile_row(t, found):
            for c in range(sh.tile_cols):
                count = count_ref[s, c, t]
                for k in range(sh.slots):
                    q = index_ref[s, c, k, t]
                    chunk = left_over(q + c * sh.parts, sh.chunks)
                    n = found[0]
                    for j in range(1, sh.chunks):
                        n = jnp.where(chunk == j, found[j], n)
                    slot = (t * sh.tile_cols + c) * sh.slots + k
                    lists[s * sh.chunks + chunk, n + 1] = slot * (sh.parts * sh.parts) + q
                    more = jnp.where(k < count, 1, 0)
                    found = tuple(
                        found[j] + jnp.where(chunk == j, more, 0) for j in range(sh.chunks)
                    )
            return found

        found = lax.fori_loop(0, sh.tile_rows, tile_row, (jnp.int32(0),) * sh.chunks)
        for j in range(sh.chunks):
            lists[s * sh.chunks + j, 0] = found[j]
    for copy in copies:
        copy.wait()


def item_kernel(sh, nu, row, *refs):
    list_ref, users, ratings = refs[:3]
    items = refs[3 : 3 + nu]
    terms = refs[3 + nu : 3 + 2 * nu]
    residuals, item_parts, grads, item_turned = refs[3 + 2 * nu :]
    block = sh.block
    me = lax.axis_index("user")
    for r in range(nu):
        hi, lo = split(items[r][...])
        at = source(me, r, nu)
        item_parts[at, :block] = hi
        item_parts[at, block:] = lo
        hi, lo = split(items[r][...].T)
        item_turned[at, :, :block] = hi
        item_turned[at, :, block:] = lo
    grads[...] = jnp.zeros_like(grads)
    count = list_ref[row, 0]

    def body(first, size):
        found = []
        for n in [first + j for j in range(size)]:
            slot, ub, ib = sh.entry(list_ref[row, jnp.minimum(n, count - 1) + 1])
            found.append((n, slot, ub, ib, jnp.where(n < count, 0, 1 << 30)))
        predicted = []
        for n, slot, ub, ib, least in found:
            u_hi, u_lo = split(users[ub])
            wide = dot(u_hi, item_turned[ib])
            narrow = dot(u_lo, item_turned[ib, :, :block])
            predicted.append((wide[:, block:] + narrow) + wide[:, :block])
        kept = []
        for (n, slot, ub, ib, least), p in zip(found, predicted):
            rating = ratings[slot]
            kept.append(jnp.where(rating > least, 0.5 * rating.astype(jnp.float32) - p, 0.0))
        sums = [
            dot_split(*split(residual.T), *split(users[ub]))
            for (n, slot, ub, ib, least), residual in zip(found, kept)
        ]
        for (n, slot, ub, ib, least), term in zip(found, sums):
            grads[ib] += term
        for (n, slot, ub, ib, least), residual in zip(found, kept):
            hi, lo = split(residual)
            residuals[n, :block] = hi
            residuals[n, block:] = lo

    over_groups(count, body)
    for r in range(nu):
        term = item_rate * grads[partner(me, r, nu)]
        if r == 0:
            term += items[0][...] * (1.0 - item_rate * decay_rate)
        terms[r][...] = term


def user_kernel(sh, step, *refs):
    list_ref, users = refs[:2]
    residuals = refs[2 : 2 + sh.chunks]
    item_parts = refs[2 + sh.chunks : 2 + 2 * sh.chunks]
    row = step * sh.chunks
    if step + 1 < sh.steps:
        ratings_in, users_next, ratings, sem = refs[2 + 2 * sh.chunks :]
        copy = pltpu.make_async_copy(
            ratings_in.at[pl.ds((step + 1) * sh.total, sh.total)], ratings, sem
        )
        copy.start()
    else:
        (users_next,) = refs[2 + 2 * sh.chunks :]
    block = sh.block

    def scale(i, carry):
        users_next[i] = users[i] * (1.0 - user_rate * decay_rate)
        return carry

    lax.fori_loop(0, sh.user_blocks, scale, 0)
    for k in range(sh.chunks):
        count = list_ref[row + k, 0]

        def body(first, size, k=k, count=count):
            found = []
            for n in [first + j for j in range(size)]:
                slot, ub, ib = sh.entry(list_ref[row + k, jnp.minimum(n, count - 1) + 1])
                found.append((n, ub, ib))
            terms = []
            for n, ub, ib in found:
                hi, lo = residuals[k][n, :block], residuals[k][n, block:]
                v_hi, v_lo = item_parts[k][ib, :block], item_parts[k][ib, block:]
                terms.append(user_rate * dot_split(hi, lo, v_hi, v_lo))
            for (n, ub, ib), term in zip(found, terms):
                users_next[ub] += term

        over_groups(count, body)
    if step + 1 < sh.steps:
        copy.wait()


def whole_in(space):
    return pl.BlockSpec(memory_space=space)


def in_vmem(x):
    return pltpu.with_memory_space_constraint(x, pltpu.VMEM)


def in_hbm(x):
    return pltpu.with_memory_space_constraint(x, pltpu.HBM)


def params():
    return pltpu.CompilerParams(vmem_limit_bytes=16 << 20)


def load(sh, index, count, users, blocks):
    return pl.pallas_call(
        functools.partial(load_kernel, sh),
        out_shape=[
            pltpu.VMEM(users.shape, users.dtype),
            pltpu.VMEM((sh.total, sh.block, sh.block), blocks.dtype),
            jax.ShapeDtypeStruct((sh.steps * sh.chunks, sh.total + 1), jnp.int32),
        ],
        in_specs=[whole_in(pltpu.SMEM)] * 2 + [whole_in(pl.ANY)] * 2,
        out_specs=[whole_in(pltpu.VMEM)] * 2 + [whole_in(pltpu.SMEM)],
        scratch_shapes=[pltpu.SemaphoreType.DMA((2,))],
        compiler_params=params(),
    )(*[in_hbm(x) for x in (index, count, users, blocks)])


def item_terms(sh, row, lists, users, ratings, items):
    nu = len(items)
    spec = whole_in(pltpu.VMEM)
    padded = -(-sh.total // GROUPS[0]) * GROUPS[0]
    outs = pl.pallas_call(
        functools.partial(item_kernel, sh, nu, row),
        out_shape=[pltpu.VMEM((sh.block, sh.rank), jnp.float32)] * nu
        + [
            pltpu.VMEM((padded, 2 * sh.block, sh.block), jnp.bfloat16),
            pltpu.VMEM((nu, 2 * sh.block, sh.rank), jnp.bfloat16),
        ],
        in_specs=[whole_in(pltpu.SMEM)] + [spec] * (2 + nu),
        out_specs=[spec] * (2 + nu),
        scratch_shapes=[
            pltpu.VMEM((nu, sh.block, sh.rank), jnp.float32),
            pltpu.VMEM((nu, sh.rank, 2 * sh.block), jnp.bfloat16),
        ],
        compiler_params=params(),
        cost_estimate=pl.CostEstimate(
            flops=sh.total * 8 * sh.block * sh.block * sh.rank // sh.chunks,
            bytes_accessed=8 * sh.total * sh.block * sh.block // sh.chunks,
            transcendentals=0,
        ),
    )(lists, *[in_vmem(x) for x in (users, ratings, *items)])
    return outs[:nu], outs[nu], outs[nu + 1]


def new_users(sh, step, lists, users, residuals, item_parts, blocks):
    spec = whole_in(pltpu.VMEM)
    more = step + 1 < sh.steps
    work = sh.total * 8 * sh.block * sh.block * sh.rank
    size = sh.block * sh.block
    out = pl.pallas_call(
        functools.partial(user_kernel, sh, step),
        out_shape=[pltpu.VMEM(users.shape, users.dtype)]
        + [pltpu.VMEM((sh.total, sh.block, sh.block), blocks.dtype)] * more,
        in_specs=[whole_in(pltpu.SMEM)]
        + [spec] * (1 + 2 * sh.chunks)
        + [whole_in(pl.ANY)] * more,
        out_specs=[spec] * (1 + more),
        scratch_shapes=[pltpu.SemaphoreType.DMA] * more,
        compiler_params=params(),
        cost_estimate=pl.CostEstimate(
            flops=work, bytes_accessed=8 * users.size + 8 * sh.total * size, transcendentals=0
        ),
    )(
        lists,
        *[in_vmem(x) for x in (users, *residuals, *item_parts)],
        *[in_hbm(blocks)] * more,
    )
    return out[0], out[1] if more else None


def local(nb, nu, user_factors, item_factors, block_index, block_count, ratings):
    sh = Shape(user_factors, item_factors, block_index, ratings)
    index = block_index.transpose(0, 2, 3, 1)
    count = block_count.transpose(0, 2, 1)
    users = user_factors.reshape(-1, sh.block, sh.rank)
    blocks = ratings.reshape(-1, sh.block, sh.block)
    own = [item_factors[k * sh.block : (k + 1) * sh.block] for k in range(sh.chunks)]
    users, step_ratings, lists = load(sh, index, count, users, blocks)
    for s in range(sh.steps):
        sent, residuals, item_parts = [], [], []
        for k in range(sh.chunks):
            items = [moved(own[k], 0, r, nb, nu) if r else own[k] for r in range(nu)]
            terms, residual, parts = item_terms(
                sh, s * sh.chunks + k, lists, users, step_ratings, items
            )
            residuals.append(residual)
            item_parts.append(parts)
            sent.append([moved(terms[r], 1, r, nb, nu) for r in range(nu)])
        own = [functools.reduce(jnp.add, x) for x in sent[:-1]]
        own, residuals = lax.optimization_barrier((own, residuals))
        users, step_ratings = new_users(
            sh, s, lists, users, residuals, item_parts, blocks
        )
        sent, users = lax.optimization_barrier((sent[-1], users))
        own.append(functools.reduce(jnp.add, sent))
    return (users.reshape(user_factors.shape), jnp.concatenate(own, axis=0))


def solution(mesh):
    in_specs = (
        P(("blk", "user"), None),
        P(("blk", "user"), None),
        P(None, ("blk", "user"), None, None),
        P(None, ("blk", "user"), None),
        P(None, ("blk", "user"), None, None, None, None),
    )
    out_specs = (P(("blk", "user"), None), P(("blk", "user"), None))
    return jax.shard_map(
        functools.partial(local, mesh.shape["blk"], mesh.shape["user"]),
        mesh=mesh,
        in_specs=in_specs,
        out_specs=out_specs,
        check_vma=False,
    )
```

profile of v0, /device:TPU:0, one launch (start us, length us, event | category | flops | bytes accessed | tf_op | source)
XLA Modules:
  0.0 100.0 jit_solution(16375100546255760308)
XLA Ops:
  0.6 1.0 fusion
  1.6 4.0 %collective-permute-start.9 = (f32[128,256]{1,0:T(8,128)S(1)}, f32[128,256]{1,0:T(8,128)S(1)}, u32[]{:S(2)}, u32[]{:S(2)}) collective-permute-start(f32[128,256]{1,0:T(8,128)S(1)} %get-tuple-element.136.refs_3_), channel_id=1, source_target_pairs={{0,3},{1,2},{2,1},{3,0},{4,7},{5,6},{6,5},{7,4},{8,11},{9,10},{10,... | collective-permute-start | bytes 393224 | tf_op jit(solution)/shard_map/ppermute | solution.py:38
  5.6 0.5 collective-permute-start.8
  6.1 0.1 collective-permute-start.7
  6.2 2.8 %collective-permute-start.2 = (f32[128,256]{1,0:T(8,128)S(1)}, f32[128,256]{1,0:T(8,128)S(1)}, u32[]{:S(2)}, u32[]{:S(2)}) collective-permute-start(f32[128,256]{1,0:T(8,128)S(1)} %get-tuple-element.137.refs_3_), channel_id=1, source_target_pairs={{0,3},{1,2},{2,1},{3,0},{4,7},{5,6},{6,5},{7,4},{8,11},{9,10},{10,... | collective-permute-start | bytes 393224 | tf_op jit(solution)/shard_map/ppermute | solution.py:38
  9.1 0.5 collective-permute-start.1
  9.6 5.0 %shard_map.68 = (f32[32,128,256]{2,1,0:T(8,128)S(1)}, s32[64,128,128]{2,1,0:T(8,128)S(1)}, s32[6,65]{1,0:T(8,128)S(1)}) custom-call(s32[3,2,4,8]{3,2,1,0:T(4,128)} %bitcast.10, s32[3,2,8]{2,1,0:T(2,128)} %bitcast.11, f32[32,128,256]{2,1,0:T(8,128)} %bitcast.9, s32[192,128,128]{2,1,0:T(8,128)} %bitcast.6), custom_call_target="tpu_custom_call" | custom-call | tf_op jit(solution)/shard_map/pallas_call | solution.py:234
  14.6 0.0 collective-permute-done.9.refs_6_
  14.6 0.2 collective-permute-start
  14.8 0.0 collective-permute-done.8.refs_5_
  14.8 0.0 collective-permute-done.7.refs_4_
  14.8 2.6 %shard_map.70 = (f32[128,256]{1,0:T(8,128)S(1)}, f32[128,256]{1,0:T(8,128)S(1)}, f32[128,256]{1,0:T(8,128)S(1)}, f32[128,256]{1,0:T(8,128)S(1)}, bf16[64,256,128...) custom-call(s32[6,65]{1,0:T(8,128)S(1)} %get-tuple-element.69.refs_0_, ...), custom_call_target="tpu_custom_call" | custom-call | flops 1073741824 | bytes 4194304 | tf_op jit(solution)/shard_map/pallas_call | solution.py:252
  17.4 0.1 collective-permute-start.10
  17.5 2.6 %collective-permute-start.11 = (f32[128,256]{1,0:T(8,128)S(1)}, f32[128,256]{1,0:T(8,128)S(1)}, u32[]{:S(2)}, u32[]{:S(2)}) collective-permute-start(f32[128,256]{1,0:T(8,128)S(1)} %get-tuple-element.77), channel_id=1, source_target_pairs={{0,5},{1,4},{2,7},{3,6},{4,9},{5,8},{6,11},{7,10},{8,13},{9,12},{1... | collective-permute-start | bytes 393224 | tf_op jit(solution)/shard_map/ppermute | solution.py:38
  20.1 1.8 %collective-permute-start.12 = (f32[128,256]{1,0:T(8,128)S(1)}, f32[128,256]{1,0:T(8,128)S(1)}, u32[]{:S(2)}, u32[]{:S(2)}) collective-permute-start(f32[128,256]{1,0:T(8,128)S(1)} %get-tuple-element.78), channel_id=1, source_target_pairs={{0,6},{1,7},{2,4},{3,5},{4,10},{5,11},{6,8},{7,9},{8,14},{9,15},{1... | collective-permute-start | bytes 393224 | tf_op jit(solution)/shard_map/ppermute | solution.py:38
  21.9 0.0 collective-permute-done.1.refs_5_
  21.9 1.2 %collective-permute-start.13 = (f32[128,256]{1,0:T(8,128)S(1)}, f32[128,256]{1,0:T(8,128)S(1)}, u32[]{:S(2)}, u32[]{:S(2)}) collective-permute-start(f32[128,256]{1,0:T(8,128)S(1)} %get-tuple-element.79), channel_id=1, source_target_pairs={{0,7},{1,6},{2,5},{3,4},{4,11},{5,10},{6,9},{7,8},{8,15},{9,14},{1... | collective-permute-start | bytes 393224 | tf_op jit(solution)/shard_map/ppermute | solution.py:38
  23.1 2.0 %shard_map.69 = (f32[128,256]{1,0:T(8,128)S(1)}, f32[128,256]{1,0:T(8,128)S(1)}, f32[128,256]{1,0:T(8,128)S(1)}, f32[128,256]{1,0:T(8,128)S(1)}, bf16[64,256,128...) custom-call(s32[6,65]{1,0:T(8,128)S(1)} %get-tuple-element.69.refs_0_, ...), custom_call_target="tpu_custom_call" | custom-call | flops 1073741824 | bytes 4194304 | tf_op jit(solution)/shard_map/pallas_call | solution.py:252
  25.1 1.1 %collective-permute-start.3 = (f32[128,256]{1,0:T(8,128)S(1)}, f32[128,256]{1,0:T(8,128)S(1)}, u32[]{:S(2)}, u32[]{:S(2)}) collective-permute-start(f32[128,256]{1,0:T(8,128)S(1)} %get-tuple-element.72), channel_id=1, source_target_pairs={{0,4},{1,5},{2,6},{3,7},{4,8},{5,9},{6,10},{7,11},{8,12},{9,13},{1... | collective-permute-start | bytes 393224 | tf_op jit(solution)/shard_map/ppermute | solution.py:38
  26.2 0.0 collective-permute-done.10
  26.2 2.6 %collective-permute-start.4 = (f32[128,256]{1,0:T(8,128)S(1)}, f32[128,256]{1,0:T(8,128)S(1)}, u32[]{:S(2)}, u32[]{:S(2)}) collective-permute-start(f32[128,256]{1,0:T(8,128)S(1)} %get-tuple-element.73), channel_id=1, source_target_pairs={{0,5},{1,4},{2,7},{3,6},{4,9},{5,8},{6,11},{7,10},{8,13},{9,12},{1... | collective-permute-start | bytes 393224 | tf_op jit(solution)/shard_map/ppermute | solution.py:38
  28.8 1.6 %collective-permute-start.5 = (f32[128,256]{1,0:T(8,128)S(1)}, f32[128,256]{1,0:T(8,128)S(1)}, u32[]{:S(2)}, u32[]{:S(2)}) collective-permute-start(f32[128,256]{1,0:T(8,128)S(1)} %get-tuple-element.74), channel_id=1, source_target_pairs={{0,6},{1,7},{2,4},{3,5},{4,10},{5,11},{6,8},{7,9},{8,14},{9,15},{1... | collective-permute-start | bytes 393224 | tf_op jit(solution)/shard_map/ppermute | solution.py:38
  30.3 0.1 collective-permute-start.6
  30.4 2.0 %collective-permute-start.23 = (f32[128,256]{1,0:T(8,128)S(1)}, f32[128,256]{1,0:T(8,128)S(1)}, u32[]{:S(2)}, u32[]{:S(2)}) collective-permute-start(f32[128,256]{1,0:T(8,128)S(1)} %add_add_fusion.5.refs_3_), channel_id=1, source_target_pairs={{0,3},{1,2},{2,1},{3,0},{4,7},{5,6},{6,5},{7,4},{8,11},{9,10},{10,... | collective-permute-start | bytes 393224 | tf_op jit(solution)/shard_map/ppermute | solution.py:38
  32.5 2.8 %shard_map.71 = (f32[32,128,256]{2,1,0:T(8,128)S(1)}, s32[64,128,128]{2,1,0:T(8,128)S(1)}) custom-call(s32[6,65]{1,0:T(8,128)S(1)} %get-tuple-element.69.refs_0_, f32[32,128,256]{2,1,0:T(8,128)S(1)} %get-tuple-element.70.refs_1_, bf16[64,256,128]{2,1,0:T(8,128)(2,1)S(1)} %get-tuple-element.82.refs_2_, bf16[64,256,128]{2,1,0:T(8,128)(2,1)S(1)} %get-tuple-element.83.refs_3_, ...), custom_call_target="tpu_custom_call" | custom-call | flops 2147483648 | bytes 16777216 | tf_op jit(solution)/shard_map/pallas_call | solution.py:280
  35.3 2.1 %collective-permute-start.22 = (f32[128,256]{1,0:T(8,128)S(1)}, f32[128,256]{1,0:T(8,128)S(1)}, u32[]{:S(2)}, u32[]{:S(2)}) collective-permute-start(f32[128,256]{1,0:T(8,128)S(1)} %add_add_fusion.5.refs_3_), channel_id=1, source_target_pairs={{0,2},{1,3},{2,0},{3,1},{4,6},{5,7},{6,4},{7,5},{8,10},{9,11},{10,... | collective-permute-start | bytes 393224 | tf_op jit(solution)/shard_map/ppermute | solution.py:38
  37.4 2.3 %collective-permute-done.6 = f32[128,256]{1,0:T(8,128)S(1)} collective-permute-done((f32[128,256]{1,0:T(8,128)S(1)}, f32[128,256]{1,0:T(8,128)S(1)}, u32[]{:S(2)}, u32[]{:S(2)}) %collective-permute-start.6) | collective-permute-done | bytes 131104 | tf_op jit(solution)/shard_map/ppermute | solution.py:38
  39.8 1.7 %collective-permute-start.16 = (f32[128,256]{1,0:T(8,128)S(1)}, f32[128,256]{1,0:T(8,128)S(1)}, u32[]{:S(2)}, u32[]{:S(2)}) collective-permute-start(f32[128,256]{1,0:T(8,128)S(1)} %add_add_fusion.4.refs_3_), channel_id=1, source_target_pairs={{0,3},{1,2},{2,1},{3,0},{4,7},{5,6},{6,5},{7,4},{8,11},{9,10},{10,... | collective-permute-start | bytes 393224 | tf_op jit(solution)/shard_map/ppermute | solution.py:38
  41.5 1.0 %collective-permute-start.15 = (f32[128,256]{1,0:T(8,128)S(1)}, f32[128,256]{1,0:T(8,128)S(1)}, u32[]{:S(2)}, u32[]{:S(2)}) collective-permute-start(f32[128,256]{1,0:T(8,128)S(1)} %add_add_fusion.4.refs_3_), channel_id=1, source_target_pairs={{0,2},{1,3},{2,0},{3,1},{4,6},{5,7},{6,4},{7,5},{8,10},{9,11},{10,... | collective-permute-start | bytes 393224 | tf_op jit(solution)/shard_map/ppermute | solution.py:38
  42.5 2.5 %collective-permute-start.14 = (f32[128,256]{1,0:T(8,128)S(1)}, f32[128,256]{1,0:T(8,128)S(1)}, u32[]{:S(2)}, u32[]{:S(2)}) collective-permute-start(f32[128,256]{1,0:T(8,128)S(1)} %add_add_fusion.4.refs_3_), channel_id=1, source_target_pairs={{0,1},{1,0},{2,3},{3,2},{4,5},{5,4},{6,7},{7,6},{8,9},{9,8},{10,11... | collective-permute-start | bytes 393224 | tf_op jit(solution)/shard_map/ppermute | solution.py:38
  45.0 3.1 %shard_map.73 = (f32[128,256]{1,0:T(8,128)S(1)}, f32[128,256]{1,0:T(8,128)S(1)}, f32[128,256]{1,0:T(8,128)S(1)}, f32[128,256]{1,0:T(8,128)S(1)}, bf16[64,256,128...) custom-call(s32[6,65]{1,0:T(8,128)S(1)} %get-tuple-element.69.refs_0_, ...), custom_call_target="tpu_custom_call" | custom-call | flops 1073741824 | bytes 4194304 | tf_op jit(solution)/shard_map/pallas_call | solution.py:252
  48.2 0.1 collective-permute-start.24
  48.2 2.9 %collective-permute-start.25 = (f32[128,256]{1,0:T(8,128)S(1)}, f32[128,256]{1,0:T(8,128)S(1)}, u32[]{:S(2)}, u32[]{:S(2)}) collective-permute-start(f32[128,256]{1,0:T(8,128)S(1)} %get-tuple-element.99), channel_id=1, source_target_pairs={{0,5},{1,4},{2,7},{3,6},{4,9},{5,8},{6,11},{7,10},{8,13},{9,12},{1... | collective-permute-start | bytes 393224 | tf_op jit(solution)/shard_map/ppermute | solution.py:38
  51.1 1.0 %collective-permute-start.27 = (f32[128,256]{1,0:T(8,128)S(1)}, f32[128,256]{1,0:T(8,128)S(1)}, u32[]{:S(2)}, u32[]{:S(2)}) collective-permute-start(f32[128,256]{1,0:T(8,128)S(1)} %get-tuple-element.101), channel_id=1, source_target_pairs={{0,7},{1,6},{2,5},{3,4},{4,11},{5,10},{6,9},{7,8},{8,15},{9,14},{1... | collective-permute-start | bytes 393224 | tf_op jit(solution)/shard_map/ppermute | solution.py:38
  52.2 3.1 %shard_map.72 = (f32[128,256]{1,0:T(8,128)S(1)}, f32[128,256]{1,0:T(8,128)S(1)}, f32[128,256]{1,0:T(8,128)S(1)}, f32[128,256]{1,0:T(8,128)S(1)}, bf16[64,256,128...) custom-call(s32[6,65]{1,0:T(8,128)S(1)} %get-tuple-element.69.refs_0_, ...), custom_call_target="tpu_custom_call" | custom-call | flops 1073741824 | bytes 4194304 | tf_op jit(solution)/shard_map/pallas_call | solution.py:252
  55.3 0.1 collective-permute-start.17
  55.4 0.3 collective-permute-start.18
  55.7 1.1 %collective-permute-done.25 = f32[128,256]{1,0:T(8,128)S(1)} collective-permute-done((f32[128,256]{1,0:T(8,128)S(1)}, f32[128,256]{1,0:T(8,128)S(1)}, u32[]{:S(2)}, u32[]{:S(2)}) %collective-permute-start.25) | collective-permute-done | bytes 131104 | tf_op jit(solution)/shard_map/ppermute | solution.py:38
  56.8 3.2 %collective-permute-start.19 = (f32[128,256]{1,0:T(8,128)S(1)}, f32[128,256]{1,0:T(8,128)S(1)}, u32[]{:S(2)}, u32[]{:S(2)}) collective-permute-start(f32[128,256]{1,0:T(8,128)S(1)} %get-tuple-element.95), channel_id=1, source_target_pairs={{0,6},{1,7},{2,4},{3,5},{4,10},{5,11},{6,8},{7,9},{8,14},{9,15},{1... | collective-permute-start | bytes 393224 | tf_op jit(solution)/shard_map/ppermute | solution.py:38
  60.0 1.0 %collective-permute-start.20 = (f32[128,256]{1,0:T(8,128)S(1)}, f32[128,256]{1,0:T(8,128)S(1)}, u32[]{:S(2)}, u32[]{:S(2)}) collective-permute-start(f32[128,256]{1,0:T(8,128)S(1)} %get-tuple-element.96), channel_id=1, source_target_pairs={{0,7},{1,6},{2,5},{3,4},{4,11},{5,10},{6,9},{7,8},{8,15},{9,14},{1... | collective-permute-start | bytes 393224 | tf_op jit(solution)/shard_map/ppermute | solution.py:38
  61.1 1.7 %collective-permute-start.37 = (f32[128,256]{1,0:T(8,128)S(1)}, f32[128,256]{1,0:T(8,128)S(1)}, u32[]{:S(2)}, u32[]{:S(2)}) collective-permute-start(f32[128,256]{1,0:T(8,128)S(1)} %add_add_fusion.3.refs_3_), channel_id=1, source_target_pairs={{0,3},{1,2},{2,1},{3,0},{4,7},{5,6},{6,5},{7,4},{8,11},{9,10},{10,... | collective-permute-start | bytes 393224 | tf_op jit(solution)/shard_map/ppermute | solution.py:38
  62.8 3.7 %shard_map.74 = (f32[32,128,256]{2,1,0:T(8,128)S(1)}, s32[64,128,128]{2,1,0:T(8,128)S(1)}) custom-call(s32[6,65]{1,0:T(8,128)S(1)} %get-tuple-element.69.refs_0_, f32[32,128,256]{2,1,0:T(8,128)S(1)} %get-tuple-element.87.refs_1_, bf16[64,256,128]{2,1,0:T(8,128)(2,1)S(1)} %get-tuple-element.104.refs_2_, bf16[64,256,128]{2,1,0:T(8,128)(2,1)S(1)} %get-tuple-element.105.refs_3_, ...), custom_call_target="tpu_custom_call" | custom-call | flops 2147483648 | bytes 16777216 | tf_op jit(solution)/shard_map/pallas_call | solution.py:280
  66.6 0.1 collective-permute-start.36
  66.7 1.5 %collective-permute-start.35 = (f32[128,256]{1,0:T(8,128)S(1)}, f32[128,256]{1,0:T(8,128)S(1)}, u32[]{:S(2)}, u32[]{:S(2)}) collective-permute-start(f32[128,256]{1,0:T(8,128)S(1)} %add_add_fusion.3.refs_3_), channel_id=1, source_target_pairs={{0,1},{1,0},{2,3},{3,2},{4,5},{5,4},{6,7},{7,6},{8,9},{9,8},{10,11... | collective-permute-start | bytes 393224 | tf_op jit(solution)/shard_map/ppermute | solution.py:38
  68.2 1.3 %collective-permute-done.19 = f32[128,256]{1,0:T(8,128)S(1)} collective-permute-done((f32[128,256]{1,0:T(8,128)S(1)}, f32[128,256]{1,0:T(8,128)S(1)}, u32[]{:S(2)}, u32[]{:S(2)}) %collective-permute-start.19) | collective-permute-done | bytes 131104 | tf_op jit(solution)/shard_map/ppermute | solution.py:38
  69.6 1.1 %collective-permute-start.30 = (f32[128,256]{1,0:T(8,128)S(1)}, f32[128,256]{1,0:T(8,128)S(1)}, u32[]{:S(2)}, u32[]{:S(2)}) collective-permute-start(f32[128,256]{1,0:T(8,128)S(1)} %add_add_fusion.2.refs_3_), channel_id=1, source_target_pairs={{0,3},{1,2},{2,1},{3,0},{4,7},{5,6},{6,5},{7,4},{8,11},{9,10},{10,... | collective-permute-start | bytes 393224 | tf_op jit(solution)/shard_map/ppermute | solution.py:38
  70.7 1.8 %collective-permute-start.29 = (f32[128,256]{1,0:T(8,128)S(1)}, f32[128,256]{1,0:T(8,128)S(1)}, u32[]{:S(2)}, u32[]{:S(2)}) collective-permute-start(f32[128,256]{1,0:T(8,128)S(1)} %add_add_fusion.2.refs_3_), channel_id=1, source_target_pairs={{0,2},{1,3},{2,0},{3,1},{4,6},{5,7},{6,4},{7,5},{8,10},{9,11},{10,... | collective-permute-start | bytes 393224 | tf_op jit(solution)/shard_map/ppermute | solution.py:38
  72.5 0.9 collective-permute-start.28
  73.4 0.4 collective-permute-done.36.refs_5_
  73.8 2.3 %shard_map.76 = (f32[128,256]{1,0:T(8,128)S(1)}, f32[128,256]{1,0:T(8,128)S(1)}, f32[128,256]{1,0:T(8,128)S(1)}, f32[128,256]{1,0:T(8,128)S(1)}, bf16[64,256,128...) custom-call(s32[6,65]{1,0:T(8,128)S(1)} %get-tuple-element.69.refs_0_, ...), custom_call_target="tpu_custom_call" | custom-call | flops 1073741824 | bytes 4194304 | tf_op jit(solution)/shard_map/pallas_call | solution.py:252
  76.1 0.1 collective-permute-start.38
  76.2 3.9 %collective-permute-start.39 = (f32[128,256]{1,0:T(8,128)S(1)}, f32[128,256]{1,0:T(8,128)S(1)}, u32[]{:S(2)}, u32[]{:S(2)}) collective-permute-start(f32[128,256]{1,0:T(8,128)S(1)} %get-tuple-element.121), channel_id=1, source_target_pairs={{0,5},{1,4},{2,7},{3,6},{4,9},{5,8},{6,11},{7,10},{8,13},{9,12},{1... | collective-permute-start | bytes 393224 | tf_op jit(solution)/shard_map/ppermute | solution.py:38
  80.1 1.0 %collective-permute-start.41 = (f32[128,256]{1,0:T(8,128)S(1)}, f32[128,256]{1,0:T(8,128)S(1)}, u32[]{:S(2)}, u32[]{:S(2)}) collective-permute-start(f32[128,256]{1,0:T(8,128)S(1)} %get-tuple-element.123), channel_id=1, source_target_pairs={{0,7},{1,6},{2,5},{3,4},{4,11},{5,10},{6,9},{7,8},{8,15},{9,14},{1... | collective-permute-start | bytes 393224 | tf_op jit(solution)/shard_map/ppermute | solution.py:38
  81.1 2.8 %shard_map.75 = (f32[128,256]{1,0:T(8,128)S(1)}, f32[128,256]{1,0:T(8,128)S(1)}, f32[128,256]{1,0:T(8,128)S(1)}, f32[128,256]{1,0:T(8,128)S(1)}, bf16[64,256,128...) custom-call(s32[6,65]{1,0:T(8,128)S(1)} %get-tuple-element.69.refs_0_, ...), custom_call_target="tpu_custom_call" | custom-call | flops 1073741824 | bytes 4194304 | tf_op jit(solution)/shard_map/pallas_call | solution.py:252
  83.9 0.1 collective-permute-start.31
  84.0 2.8 %collective-permute-start.32 = (f32[128,256]{1,0:T(8,128)S(1)}, f32[128,256]{1,0:T(8,128)S(1)}, u32[]{:S(2)}, u32[]{:S(2)}) collective-permute-start(f32[128,256]{1,0:T(8,128)S(1)} %get-tuple-element.116), channel_id=1, source_target_pairs={{0,5},{1,4},{2,7},{3,6},{4,9},{5,8},{6,11},{7,10},{8,13},{9,12},{1... | collective-permute-start | bytes 393224 | tf_op jit(solution)/shard_map/ppermute | solution.py:38
  86.8 0.9 collective-permute-start.33
  87.6 1.5 %collective-permute-done.40 = f32[128,256]{1,0:T(8,128)S(1)} collective-permute-done((f32[128,256]{1,0:T(8,128)S(1)}, f32[128,256]{1,0:T(8,128)S(1)}, u32[]{:S(2)}, u32[]{:S(2)}) %collective-permute-start.40) | collective-permute-done | bytes 131104 | tf_op jit(solution)/shard_map/ppermute | solution.py:38
  89.1 2.1 %collective-permute-done.41 = f32[128,256]{1,0:T(8,128)S(1)} collective-permute-done((f32[128,256]{1,0:T(8,128)S(1)}, f32[128,256]{1,0:T(8,128)S(1)}, u32[]{:S(2)}, u32[]{:S(2)}) %collective-permute-start.41) | collective-permute-done | bytes 131104 | tf_op jit(solution)/shard_map/ppermute | solution.py:38
  91.3 3.0 %shard_map.77 = f32[32,128,256]{2,1,0:T(8,128)S(1)} custom-call(s32[6,65]{1,0:T(8,128)S(1)} %get-tuple-element.69.refs_0_, f32[32,128,256]{2,1,0:T(8,128)S(1)} %get-tuple-element.109.refs_1_, bf16[64,256,128]{2,1,0:T(8,128)(2,1)S(1)} %get-tuple-element.126.refs_2_, bf16[64,256,128]{2,1,0:T(8,128)(2,1)S(1)} %get-tuple-element.127.refs_3_, ...), custom_call_target="tpu_custom_call" | custom-call | flops 2147483648 | bytes 16777216 | tf_op jit(solution)/shard_map/pallas_call | solution.py:280
  94.3 0.4 collective-permute-done.33
  94.7 2.5 %collective-permute-done.34 = f32[128,256]{1,0:T(8,128)S(1)} collective-permute-done((f32[128,256]{1,0:T(8,128)S(1)}, f32[128,256]{1,0:T(8,128)S(1)}, u32[]{:S(2)}, u32[]{:S(2)}) %collective-permute-start.34) | collective-permute-done | bytes 131104 | tf_op jit(solution)/shard_map/ppermute | solution.py:38
  97.2 2.0 %copy.7 = f32[4096,256]{1,0:T(8,128)} copy(f32[4096,256]{1,0:T(8,128)S(1)} %bitcast.5) | data formatting | bytes 8388608
  99.2 0.7 pad_maximum_fusion
  (39 shorter events, 0.3 us)
Async XLA Ops:
  1.6 13.0 %collective-permute-start.9 = (f32[128,256]{1,0:T(8,128)S(1)}, f32[128,256]{1,0:T(8,128)S(1)}, u32[]{:S(2)}, u32[]{:S(2)}) collective-permute-start(f32[128,256]{1,0:T(8,128)S(1)} %get-tuple-element.136.refs_3_), channel_id=1, source_target_pairs={{0,3},{1,2},{2,1},{3,0},{4,7},{5,6},{6,5},{7,4},{8,11},{9,10},{10,... | collective-permute-start | bytes 393224 | tf_op jit(solution)/shard_map/ppermute | solution.py:38
  5.6 9.3 %collective-permute-start.8 = (f32[128,256]{1,0:T(8,128)S(1)}, f32[128,256]{1,0:T(8,128)S(1)}, u32[]{:S(2)}, u32[]{:S(2)}) collective-permute-start(f32[128,256]{1,0:T(8,128)S(1)} %get-tuple-element.136.refs_3_), channel_id=1, source_target_pairs={{0,2},{1,3},{2,0},{3,1},{4,6},{5,7},{6,4},{7,5},{8,10},{9,11},{10,... | collective-permute-start | bytes 393224 | tf_op jit(solution)/shard_map/ppermute | solution.py:38
  6.1 8.8 %collective-permute-start.7 = (f32[128,256]{1,0:T(8,128)S(1)}, f32[128,256]{1,0:T(8,128)S(1)}, u32[]{:S(2)}, u32[]{:S(2)}) collective-permute-start(f32[128,256]{1,0:T(8,128)S(1)} %get-tuple-element.136.refs_3_), channel_id=1, source_target_pairs={{0,1},{1,0},{2,3},{3,2},{4,5},{5,4},{6,7},{7,6},{8,9},{9,8},{10,11... | collective-permute-start | bytes 393224 | tf_op jit(solution)/shard_map/ppermute | solution.py:38
  6.2 13.9 %collective-permute-start.2 = (f32[128,256]{1,0:T(8,128)S(1)}, f32[128,256]{1,0:T(8,128)S(1)}, u32[]{:S(2)}, u32[]{:S(2)}) collective-permute-start(f32[128,256]{1,0:T(8,128)S(1)} %get-tuple-element.137.refs_3_), channel_id=1, source_target_pairs={{0,3},{1,2},{2,1},{3,0},{4,7},{5,6},{6,5},{7,4},{8,11},{9,10},{10,... | collective-permute-start | bytes 393224 | tf_op jit(solution)/shard_map/ppermute | solution.py:38
  9.1 12.8 %collective-permute-start.1 = (f32[128,256]{1,0:T(8,128)S(1)}, f32[128,256]{1,0:T(8,128)S(1)}, u32[]{:S(2)}, u32[]{:S(2)}) collective-permute-start(f32[128,256]{1,0:T(8,128)S(1)} %get-tuple-element.137.refs_3_), channel_id=1, source_target_pairs={{0,2},{1,3},{2,0},{3,1},{4,6},{5,7},{6,4},{7,5},{8,10},{9,11},{10,... | collective-permute-start | bytes 393224 | tf_op jit(solution)/shard_map/ppermute | solution.py:38
  14.6 8.5 %collective-permute-start = (f32[128,256]{1,0:T(8,128)S(1)}, f32[128,256]{1,0:T(8,128)S(1)}, u32[]{:S(2)}, u32[]{:S(2)}) collective-permute-start(f32[128,256]{1,0:T(8,128)S(1)} %get-tuple-element.137.refs_3_), channel_id=1, source_target_pairs={{0,1},{1,0},{2,3},{3,2},{4,5},{5,4},{6,7},{7,6},{8,9},{9,8},{10,11... | collective-permute-start | bytes 393224 | tf_op jit(solution)/shard_map/ppermute | solution.py:38
  17.4 8.8 %collective-permute-start.10 = (f32[128,256]{1,0:T(8,128)S(1)}, f32[128,256]{1,0:T(8,128)S(1)}, u32[]{:S(2)}, u32[]{:S(2)}) collective-permute-start(f32[128,256]{1,0:T(8,128)S(1)} %get-tuple-element.76), channel_id=1, source_target_pairs={{0,4},{1,5},{2,6},{3,7},{4,8},{5,9},{6,10},{7,11},{8,12},{9,13},{1... | collective-permute-start | bytes 393224 | tf_op jit(solution)/shard_map/ppermute | solution.py:38
  17.5 11.3 %collective-permute-start.11 = (f32[128,256]{1,0:T(8,128)S(1)}, f32[128,256]{1,0:T(8,128)S(1)}, u32[]{:S(2)}, u32[]{:S(2)}) collective-permute-start(f32[128,256]{1,0:T(8,128)S(1)} %get-tuple-element.77), channel_id=1, source_target_pairs={{0,5},{1,4},{2,7},{3,6},{4,9},{5,8},{6,11},{7,10},{8,13},{9,12},{1... | collective-permute-start | bytes 393224 | tf_op jit(solution)/shard_map/ppermute | solution.py:38
  20.1 10.2 %collective-permute-start.12 = (f32[128,256]{1,0:T(8,128)S(1)}, f32[128,256]{1,0:T(8,128)S(1)}, u32[]{:S(2)}, u32[]{:S(2)}) collective-permute-start(f32[128,256]{1,0:T(8,128)S(1)} %get-tuple-element.78), channel_id=1, source_target_pairs={{0,6},{1,7},{2,4},{3,5},{4,10},{5,11},{6,8},{7,9},{8,14},{9,15},{1... | collective-permute-start | bytes 393224 | tf_op jit(solution)/shard_map/ppermute | solution.py:38
  21.9 8.5 %collective-permute-start.13 = (f32[128,256]{1,0:T(8,128)S(1)}, f32[128,256]{1,0:T(8,128)S(1)}, u32[]{:S(2)}, u32[]{:S(2)}) collective-permute-start(f32[128,256]{1,0:T(8,128)S(1)} %get-tuple-element.79), channel_id=1, source_target_pairs={{0,7},{1,6},{2,5},{3,4},{4,11},{5,10},{6,9},{7,8},{8,15},{9,14},{1... | collective-permute-start | bytes 393224 | tf_op jit(solution)/shard_map/ppermute | solution.py:38
  25.1 10.2 %collective-permute-start.3 = (f32[128,256]{1,0:T(8,128)S(1)}, f32[128,256]{1,0:T(8,128)S(1)}, u32[]{:S(2)}, u32[]{:S(2)}) collective-permute-start(f32[128,256]{1,0:T(8,128)S(1)} %get-tuple-element.72), channel_id=1, source_target_pairs={{0,4},{1,5},{2,6},{3,7},{4,8},{5,9},{6,10},{7,11},{8,12},{9,13},{1... | collective-permute-start | bytes 393224 | tf_op jit(solution)/shard_map/ppermute | solution.py:38
  26.2 11.2 %collective-permute-start.4 = (f32[128,256]{1,0:T(8,128)S(1)}, f32[128,256]{1,0:T(8,128)S(1)}, u32[]{:S(2)}, u32[]{:S(2)}) collective-permute-start(f32[128,256]{1,0:T(8,128)S(1)} %get-tuple-element.73), channel_id=1, source_target_pairs={{0,5},{1,4},{2,7},{3,6},{4,9},{5,8},{6,11},{7,10},{8,13},{9,12},{1... | collective-permute-start | bytes 393224 | tf_op jit(solution)/shard_map/ppermute | solution.py:38
  28.8 8.6 %collective-permute-start.5 = (f32[128,256]{1,0:T(8,128)S(1)}, f32[128,256]{1,0:T(8,128)S(1)}, u32[]{:S(2)}, u32[]{:S(2)}) collective-permute-start(f32[128,256]{1,0:T(8,128)S(1)} %get-tuple-element.74), channel_id=1, source_target_pairs={{0,6},{1,7},{2,4},{3,5},{4,10},{5,11},{6,8},{7,9},{8,14},{9,15},{1... | collective-permute-start | bytes 393224 | tf_op jit(solution)/shard_map/ppermute | solution.py:38
  30.3 9.4 %collective-permute-start.6 = (f32[128,256]{1,0:T(8,128)S(1)}, f32[128,256]{1,0:T(8,128)S(1)}, u32[]{:S(2)}, u32[]{:S(2)}) collective-permute-start(f32[128,256]{1,0:T(8,128)S(1)} %get-tuple-element.75), channel_id=1, source_target_pairs={{0,7},{1,6},{2,5},{3,4},{4,11},{5,10},{6,9},{7,8},{8,15},{9,14},{1... | collective-permute-start | bytes 393224 | tf_op jit(solution)/shard_map/ppermute | solution.py:38
  30.4 12.1 %collective-permute-start.23 = (f32[128,256]{1,0:T(8,128)S(1)}, f32[128,256]{1,0:T(8,128)S(1)}, u32[]{:S(2)}, u32[]{:S(2)}) collective-permute-start(f32[128,256]{1,0:T(8,128)S(1)} %add_add_fusion.5.refs_3_), channel_id=1, source_target_pairs={{0,3},{1,2},{2,1},{3,0},{4,7},{5,6},{6,5},{7,4},{8,11},{9,10},{10,... | collective-permute-start | bytes 393224 | tf_op jit(solution)/shard_map/ppermute | solution.py:38
  35.3 9.8 %collective-permute-start.22 = (f32[128,256]{1,0:T(8,128)S(1)}, f32[128,256]{1,0:T(8,128)S(1)}, u32[]{:S(2)}, u32[]{:S(2)}) collective-permute-start(f32[128,256]{1,0:T(8,128)S(1)} %add_add_fusion.5.refs_3_), channel_id=1, source_target_pairs={{0,2},{1,3},{2,0},{3,1},{4,6},{5,7},{6,4},{7,5},{8,10},{9,11},{10,... | collective-permute-start | bytes 393224 | tf_op jit(solution)/shard_map/ppermute | solution.py:38
  37.4 7.6 %collective-permute-start.21 = (f32[128,256]{1,0:T(8,128)S(1)}, f32[128,256]{1,0:T(8,128)S(1)}, u32[]{:S(2)}, u32[]{:S(2)}) collective-permute-start(f32[128,256]{1,0:T(8,128)S(1)} %add_add_fusion.5.refs_3_), channel_id=1, source_target_pairs={{0,1},{1,0},{2,3},{3,2},{4,5},{5,4},{6,7},{7,6},{8,9},{9,8},{10,11... | collective-permute-start | bytes 393224 | tf_op jit(solution)/shard_map/ppermute | solution.py:38
  39.8 11.3 %collective-permute-start.16 = (f32[128,256]{1,0:T(8,128)S(1)}, f32[128,256]{1,0:T(8,128)S(1)}, u32[]{:S(2)}, u32[]{:S(2)}) collective-permute-start(f32[128,256]{1,0:T(8,128)S(1)} %add_add_fusion.4.refs_3_), channel_id=1, source_target_pairs={{0,3},{1,2},{2,1},{3,0},{4,7},{5,6},{6,5},{7,4},{8,11},{9,10},{10,... | collective-permute-start | bytes 393224 | tf_op jit(solution)/shard_map/ppermute | solution.py:38
  41.5 9.7 %collective-permute-start.15 = (f32[128,256]{1,0:T(8,128)S(1)}, f32[128,256]{1,0:T(8,128)S(1)}, u32[]{:S(2)}, u32[]{:S(2)}) collective-permute-start(f32[128,256]{1,0:T(8,128)S(1)} %add_add_fusion.4.refs_3_), channel_id=1, source_target_pairs={{0,2},{1,3},{2,0},{3,1},{4,6},{5,7},{6,4},{7,5},{8,10},{9,11},{10,... | collective-permute-start | bytes 393224 | tf_op jit(solution)/shard_map/ppermute | solution.py:38
  42.5 9.7 %collective-permute-start.14 = (f32[128,256]{1,0:T(8,128)S(1)}, f32[128,256]{1,0:T(8,128)S(1)}, u32[]{:S(2)}, u32[]{:S(2)}) collective-permute-start(f32[128,256]{1,0:T(8,128)S(1)} %add_add_fusion.4.refs_3_), channel_id=1, source_target_pairs={{0,1},{1,0},{2,3},{3,2},{4,5},{5,4},{6,7},{7,6},{8,9},{9,8},{10,11... | collective-permute-start | bytes 393224 | tf_op jit(solution)/shard_map/ppermute | solution.py:38
  48.2 7.2 %collective-permute-start.24 = (f32[128,256]{1,0:T(8,128)S(1)}, f32[128,256]{1,0:T(8,128)S(1)}, u32[]{:S(2)}, u32[]{:S(2)}) collective-permute-start(f32[128,256]{1,0:T(8,128)S(1)} %get-tuple-element.98), channel_id=1, source_target_pairs={{0,4},{1,5},{2,6},{3,7},{4,8},{5,9},{6,10},{7,11},{8,12},{9,13},{1... | collective-permute-start | bytes 393224 | tf_op jit(solution)/shard_map/ppermute | solution.py:38
  48.2 8.5 %collective-permute-start.25 = (f32[128,256]{1,0:T(8,128)S(1)}, f32[128,256]{1,0:T(8,128)S(1)}, u32[]{:S(2)}, u32[]{:S(2)}) collective-permute-start(f32[128,256]{1,0:T(8,128)S(1)} %get-tuple-element.99), channel_id=1, source_target_pairs={{0,5},{1,4},{2,7},{3,6},{4,9},{5,8},{6,11},{7,10},{8,13},{9,12},{1... | collective-permute-start | bytes 393224 | tf_op jit(solution)/shard_map/ppermute | solution.py:38
  51.1 8.9 %collective-permute-start.26 = (f32[128,256]{1,0:T(8,128)S(1)}, f32[128,256]{1,0:T(8,128)S(1)}, u32[]{:S(2)}, u32[]{:S(2)}) collective-permute-start(f32[128,256]{1,0:T(8,128)S(1)} %get-tuple-element.100), channel_id=1, source_target_pairs={{0,6},{1,7},{2,4},{3,5},{4,10},{5,11},{6,8},{7,9},{8,14},{9,15},{1... | collective-permute-start | bytes 393224 | tf_op jit(solution)/shard_map/ppermute | solution.py:38
  51.1 9.9 %collective-permute-start.27 = (f32[128,256]{1,0:T(8,128)S(1)}, f32[128,256]{1,0:T(8,128)S(1)}, u32[]{:S(2)}, u32[]{:S(2)}) collective-permute-start(f32[128,256]{1,0:T(8,128)S(1)} %get-tuple-element.101), channel_id=1, source_target_pairs={{0,7},{1,6},{2,5},{3,4},{4,11},{5,10},{6,9},{7,8},{8,15},{9,14},{1... | collective-permute-start | bytes 393224 | tf_op jit(solution)/shard_map/ppermute | solution.py:38
  55.3 11.3 %collective-permute-start.17 = (f32[128,256]{1,0:T(8,128)S(1)}, f32[128,256]{1,0:T(8,128)S(1)}, u32[]{:S(2)}, u32[]{:S(2)}) collective-permute-start(f32[128,256]{1,0:T(8,128)S(1)} %get-tuple-element.93), channel_id=1, source_target_pairs={{0,4},{1,5},{2,6},{3,7},{4,8},{5,9},{6,10},{7,11},{8,12},{9,13},{1... | collective-permute-start | bytes 393224 | tf_op jit(solution)/shard_map/ppermute | solution.py:38
  55.4 11.3 %collective-permute-start.18 = (f32[128,256]{1,0:T(8,128)S(1)}, f32[128,256]{1,0:T(8,128)S(1)}, u32[]{:S(2)}, u32[]{:S(2)}) collective-permute-start(f32[128,256]{1,0:T(8,128)S(1)} %get-tuple-element.94), channel_id=1, source_target_pairs={{0,5},{1,4},{2,7},{3,6},{4,9},{5,8},{6,11},{7,10},{8,13},{9,12},{1... | collective-permute-start | bytes 393224 | tf_op jit(solution)/shard_map/ppermute | solution.py:38
  56.8 12.8 %collective-permute-start.19 = (f32[128,256]{1,0:T(8,128)S(1)}, f32[128,256]{1,0:T(8,128)S(1)}, u32[]{:S(2)}, u32[]{:S(2)}) collective-permute-start(f32[128,256]{1,0:T(8,128)S(1)} %get-tuple-element.95), channel_id=1, source_target_pairs={{0,6},{1,7},{2,4},{3,5},{4,10},{5,11},{6,8},{7,9},{8,14},{9,15},{1... | collective-permute-start | bytes 393224 | tf_op jit(solution)/shard_map/ppermute | solution.py:38
  60.0 9.5 %collective-permute-start.20 = (f32[128,256]{1,0:T(8,128)S(1)}, f32[128,256]{1,0:T(8,128)S(1)}, u32[]{:S(2)}, u32[]{:S(2)}) collective-permute-start(f32[128,256]{1,0:T(8,128)S(1)} %get-tuple-element.96), channel_id=1, source_target_pairs={{0,7},{1,6},{2,5},{3,4},{4,11},{5,10},{6,9},{7,8},{8,15},{9,14},{1... | collective-permute-start | bytes 393224 | tf_op jit(solution)/shard_map/ppermute | solution.py:38
  61.1 11.4 %collective-permute-start.37 = (f32[128,256]{1,0:T(8,128)S(1)}, f32[128,256]{1,0:T(8,128)S(1)}, u32[]{:S(2)}, u32[]{:S(2)}) collective-permute-start(f32[128,256]{1,0:T(8,128)S(1)} %add_add_fusion.3.refs_3_), channel_id=1, source_target_pairs={{0,3},{1,2},{2,1},{3,0},{4,7},{5,6},{6,5},{7,4},{8,11},{9,10},{10,... | collective-permute-start | bytes 393224 | tf_op jit(solution)/shard_map/ppermute | solution.py:38
  66.6 7.2 %collective-permute-start.36 = (f32[128,256]{1,0:T(8,128)S(1)}, f32[128,256]{1,0:T(8,128)S(1)}, u32[]{:S(2)}, u32[]{:S(2)}) collective-permute-start(f32[128,256]{1,0:T(8,128)S(1)} %add_add_fusion.3.refs_3_), channel_id=1, source_target_pairs={{0,2},{1,3},{2,0},{3,1},{4,6},{5,7},{6,4},{7,5},{8,10},{9,11},{10,... | collective-permute-start | bytes 393224 | tf_op jit(solution)/shard_map/ppermute | solution.py:38
  66.7 7.1 %collective-permute-start.35 = (f32[128,256]{1,0:T(8,128)S(1)}, f32[128,256]{1,0:T(8,128)S(1)}, u32[]{:S(2)}, u32[]{:S(2)}) collective-permute-start(f32[128,256]{1,0:T(8,128)S(1)} %add_add_fusion.3.refs_3_), channel_id=1, source_target_pairs={{0,1},{1,0},{2,3},{3,2},{4,5},{5,4},{6,7},{7,6},{8,9},{9,8},{10,11... | collective-permute-start | bytes 393224 | tf_op jit(solution)/shard_map/ppermute | solution.py:38
  69.6 10.5 %collective-permute-start.30 = (f32[128,256]{1,0:T(8,128)S(1)}, f32[128,256]{1,0:T(8,128)S(1)}, u32[]{:S(2)}, u32[]{:S(2)}) collective-permute-start(f32[128,256]{1,0:T(8,128)S(1)} %add_add_fusion.2.refs_3_), channel_id=1, source_target_pairs={{0,3},{1,2},{2,1},{3,0},{4,7},{5,6},{6,5},{7,4},{8,11},{9,10},{10,... | collective-permute-start | bytes 393224 | tf_op jit(solution)/shard_map/ppermute | solution.py:38
  70.7 9.4 %collective-permute-start.29 = (f32[128,256]{1,0:T(8,128)S(1)}, f32[128,256]{1,0:T(8,128)S(1)}, u32[]{:S(2)}, u32[]{:S(2)}) collective-permute-start(f32[128,256]{1,0:T(8,128)S(1)} %add_add_fusion.2.refs_3_), channel_id=1, source_target_pairs={{0,2},{1,3},{2,0},{3,1},{4,6},{5,7},{6,4},{7,5},{8,10},{9,11},{10,... | collective-permute-start | bytes 393224 | tf_op jit(solution)/shard_map/ppermute | solution.py:38
  72.5 8.6 %collective-permute-start.28 = (f32[128,256]{1,0:T(8,128)S(1)}, f32[128,256]{1,0:T(8,128)S(1)}, u32[]{:S(2)}, u32[]{:S(2)}) collective-permute-start(f32[128,256]{1,0:T(8,128)S(1)} %add_add_fusion.2.refs_3_), channel_id=1, source_target_pairs={{0,1},{1,0},{2,3},{3,2},{4,5},{5,4},{6,7},{7,6},{8,9},{9,8},{10,11... | collective-permute-start | bytes 393224 | tf_op jit(solution)/shard_map/ppermute | solution.py:38
  76.1 7.9 %collective-permute-start.38 = (f32[128,256]{1,0:T(8,128)S(1)}, f32[128,256]{1,0:T(8,128)S(1)}, u32[]{:S(2)}, u32[]{:S(2)}) collective-permute-start(f32[128,256]{1,0:T(8,128)S(1)} %get-tuple-element.120), channel_id=1, source_target_pairs={{0,4},{1,5},{2,6},{3,7},{4,8},{5,9},{6,10},{7,11},{8,12},{9,13},{1... | collective-permute-start | bytes 393224 | tf_op jit(solution)/shard_map/ppermute | solution.py:38
  76.2 10.6 %collective-permute-start.39 = (f32[128,256]{1,0:T(8,128)S(1)}, f32[128,256]{1,0:T(8,128)S(1)}, u32[]{:S(2)}, u32[]{:S(2)}) collective-permute-start(f32[128,256]{1,0:T(8,128)S(1)} %get-tuple-element.121), channel_id=1, source_target_pairs={{0,5},{1,4},{2,7},{3,6},{4,9},{5,8},{6,11},{7,10},{8,13},{9,12},{1... | collective-permute-start | bytes 393224 | tf_op jit(solution)/shard_map/ppermute | solution.py:38
  80.1 9.0 %collective-permute-start.40 = (f32[128,256]{1,0:T(8,128)S(1)}, f32[128,256]{1,0:T(8,128)S(1)}, u32[]{:S(2)}, u32[]{:S(2)}) collective-permute-start(f32[128,256]{1,0:T(8,128)S(1)} %get-tuple-element.122), channel_id=1, source_target_pairs={{0,6},{1,7},{2,4},{3,5},{4,10},{5,11},{6,8},{7,9},{8,14},{9,15},{1... | collective-permute-start | bytes 393224 | tf_op jit(solution)/shard_map/ppermute | solution.py:38
  80.1 11.2 %collective-permute-start.41 = (f32[128,256]{1,0:T(8,128)S(1)}, f32[128,256]{1,0:T(8,128)S(1)}, u32[]{:S(2)}, u32[]{:S(2)}) collective-permute-start(f32[128,256]{1,0:T(8,128)S(1)} %get-tuple-element.123), channel_id=1, source_target_pairs={{0,7},{1,6},{2,5},{3,4},{4,11},{5,10},{6,9},{7,8},{8,15},{9,14},{1... | collective-permute-start | bytes 393224 | tf_op jit(solution)/shard_map/ppermute | solution.py:38
  83.9 10.3 %collective-permute-start.31 = (f32[128,256]{1,0:T(8,128)S(1)}, f32[128,256]{1,0:T(8,128)S(1)}, u32[]{:S(2)}, u32[]{:S(2)}) collective-permute-start(f32[128,256]{1,0:T(8,128)S(1)} %get-tuple-element.115), channel_id=1, source_target_pairs={{0,4},{1,5},{2,6},{3,7},{4,8},{5,9},{6,10},{7,11},{8,12},{9,13},{1... | collective-permute-start | bytes 393224 | tf_op jit(solution)/shard_map/ppermute | solution.py:38
  84.0 10.3 %collective-permute-start.32 = (f32[128,256]{1,0:T(8,128)S(1)}, f32[128,256]{1,0:T(8,128)S(1)}, u32[]{:S(2)}, u32[]{:S(2)}) collective-permute-start(f32[128,256]{1,0:T(8,128)S(1)} %get-tuple-element.116), channel_id=1, source_target_pairs={{0,5},{1,4},{2,7},{3,6},{4,9},{5,8},{6,11},{7,10},{8,13},{9,12},{1... | collective-permute-start | bytes 393224 | tf_op jit(solution)/shard_map/ppermute | solution.py:38
  86.8 7.9 %collective-permute-start.33 = (f32[128,256]{1,0:T(8,128)S(1)}, f32[128,256]{1,0:T(8,128)S(1)}, u32[]{:S(2)}, u32[]{:S(2)}) collective-permute-start(f32[128,256]{1,0:T(8,128)S(1)} %get-tuple-element.117), channel_id=1, source_target_pairs={{0,6},{1,7},{2,4},{3,5},{4,10},{5,11},{6,8},{7,9},{8,14},{9,15},{1... | collective-permute-start | bytes 393224 | tf_op jit(solution)/shard_map/ppermute | solution.py:38
  89.1 8.1 %collective-permute-start.34 = (f32[128,256]{1,0:T(8,128)S(1)}, f32[128,256]{1,0:T(8,128)S(1)}, u32[]{:S(2)}, u32[]{:S(2)}) collective-permute-start(f32[128,256]{1,0:T(8,128)S(1)} %get-tuple-element.118), channel_id=1, source_target_pairs={{0,7},{1,6},{2,5},{3,4},{4,11},{5,10},{6,9},{7,8},{8,15},{9,14},{1... | collective-permute-start | bytes 393224 | tf_op jit(solution)/shard_map/ppermute | solution.py:38
where the time goes:
time: 100 us
  starting transfers between devices  53 us (53%)
  Pallas kernels  30.4 us (30%)
  waiting for transfers between devices  11.7 us (12%)
  local copies, waits for them, and re-layouts  3 us (3%)
    ppermute x42, starting transfers between devices, moved(): return lax.ppermute(x, ('blk', 'user'), route)  53 us
    pallas_call x6, Pallas kernels, item_terms(): pl.pallas_call(functools.partial(item_kernel, sh, nu, row), out_shape=[pl...  15.9 us
    ppermute x42, waiting for transfers between devices, moved(): return lax.ppermute(x, ('blk', 'user'), route)  11.7 us
    pallas_call x3, Pallas kernels, new_users(): pl.pallas_call(functools.partial(user_kernel, sh, step), out_shape=[pltpu...  9.5 us
    pallas_call x1, Pallas kernels, load(): pl.pallas_call(functools.partial(load_kernel, sh), out_shape=[pltpu.VMEM(...  5.04 us
    unnamed x1, local copies, waits for them, and re-layouts  2.01 us
  transfers between devices with their start and end apart: 42, of which 8 were waited for; matrix products, arithmetic and copies ran while one was open for 0% of the time, Pallas kernels for 30%

commit v1 on v0

--- a/solution.py
+++ b/solution.py
@@ -185,7 +185,7 @@
         )
         copy.start()
     else:
-        (users_next,) = refs[2 + 2 * sh.chunks :]
+        users_out, users_next, sem = refs[2 + 2 * sh.chunks :]
     block = sh.block
 
     def scale(i, carry):
@@ -210,8 +210,10 @@
                 users_next[ub] += term
 
         over_groups(count, body)
-    if step + 1 < sh.steps:
-        copy.wait()
+    if step + 1 == sh.steps:
+        copy = pltpu.make_async_copy(users_next, users_out, sem)
+        copy.start()
+    copy.wait()
 
 
 def whole_in(space):
@@ -277,15 +279,25 @@
     more = step + 1 < sh.steps
     work = sh.total * 8 * sh.block * sh.block * sh.rank
     size = sh.block * sh.block
+    if more:
+        out_shape = [
+            pltpu.VMEM(users.shape, users.dtype),
+            pltpu.VMEM((sh.total, sh.block, sh.block), blocks.dtype),
+        ]
+        out_specs = [spec, spec]
+        scratch = []
+    else:
+        out_shape = [jax.ShapeDtypeStruct(users.shape, users.dtype)]
+        out_specs = [whole_in(pl.ANY)]
+        scratch = [pltpu.VMEM(users.shape, users.dtype)]
     out = pl.pallas_call(
         functools.partial(user_kernel, sh, step),
-        out_shape=[pltpu.VMEM(users.shape, users.dtype)]
-        + [pltpu.VMEM((sh.total, sh.block, sh.block), blocks.dtype)] * more,
+        out_shape=out_shape,
         in_specs=[whole_in(pltpu.SMEM)]
         + [spec] * (1 + 2 * sh.chunks)
         + [whole_in(pl.ANY)] * more,
-        out_specs=[spec] * (1 + more),
-        scratch_shapes=[pltpu.SemaphoreType.DMA] * more,
+        out_specs=out_specs,
+        scratch_shapes=scratch + [pltpu.SemaphoreType.DMA],
         compiler_params=params(),
         cost_estimate=pl.CostEstimate(
             flops=work, bytes_accessed=8 * users.size + 8 * sh.total * size, transcendentals=0
@@ -315,7 +327,7 @@
             )
             residuals.append(residual)
             item_parts.append(parts)
-            sent.append([moved(terms[r], 1, r, nb, nu) for r in range(nu)])
+            sent.append([moved(terms[r], 1, r, nb, nu) for r in reversed(range(nu))])
         own = [functools.reduce(jnp.add, x) for x in sent[:-1]]
         own, residuals = lax.optimization_barrier((own, residuals))
         users, step_ratings = new_users(

time: 100 us -> 94.9 us (0.949)
  starting transfers between devices: 53 us -> 49 us
  Pallas kernels: 30.4 us -> 32.8 us
  local copies, waits for them, and re-layouts: 3 us -> 0.99 us
  waiting for transfers between devices: 11.7 us -> 10.1 us
    ppermute x42, starting transfers between devices: 53 us -> 49 us  [moved(): return lax.ppermute(x, ('blk', 'user'), route)]
    pallas_call x3, Pallas kernels: 9.5 us -> 11.5 us  [new_users(): pl.pallas_call(functools.partial(user_kernel, sh, step), out_shape=out_sh...]
    unnamed x1 -> x0, local copies, waits for them, and re-layouts: 2.01 us -> none
    ppermute x42, waiting for transfers between devices: 11.7 us -> 10.1 us  [moved(): return lax.ppermute(x, ('blk', 'user'), route)]
  transfers between devices with their start and end apart: 42 -> 42, of which waited for: 8 -> 13; matrix products, arithmetic and copies ran while one was open for 0% -> 0% of each run, Pallas kernels for 30% -> 35%
where the time goes in v1:
time: 94.9 us; the launch traced here: 94.6 us
  starting transfers between devices  49 us (52%)
  Pallas kernels  32.8 us (35%)
  waiting for transfers between devices  10.1 us (11%)
  local copies, waits for them, and re-layouts  0.99 us (1%)
    ppermute x42, starting transfers between devices, moved(): return lax.ppermute(x, ('blk', 'user'), route)  49 us
    pallas_call x6, Pallas kernels, item_terms(): pl.pallas_call(functools.partial(item_kernel, sh, nu, row), out_shape=[pl...  16.2 us
    pallas_call x3, Pallas kernels, new_users(): pl.pallas_call(functools.partial(user_kernel, sh, step), out_shape=out_sh...  11.5 us
    ppermute x42, waiting for transfers between devices, moved(): return lax.ppermute(x, ('blk', 'user'), route)  10.1 us
    pallas_call x1, Pallas kernels, load(): pl.pallas_call(functools.partial(load_kernel, sh), out_shape=[pltpu.VMEM(...  5.04 us
  transfers between devices with their start and end apart: 42, of which 13 were waited for; matrix products, arithmetic and copies ran while one was open for 0% of the time, Pallas kernels for 35%

profile of v1, /device:TPU:0, one launch (start us, length us, event | category | flops | bytes accessed | tf_op | source)
XLA Modules:
  0.0 94.6 jit_solution(9301868522366071724)
XLA Ops:
  0.6 1.0 %fusion = (f32[128,256]{1,0:T(8,128)S(1)}, f32[128,256]{1,0:T(8,128)S(1)}) fusion(f32[256,256]{1,0:T(8,128)} %param.6), kind=kLoop, calls=%fused_computation.7 | loop fusion | bytes 524288 | tf_op jit(solution)/shard_map/slice | solution.py:319
  1.6 4.0 %collective-permute-start.9 = (f32[128,256]{1,0:T(8,128)S(1)}, f32[128,256]{1,0:T(8,128)S(1)}, u32[]{:S(2)}, u32[]{:S(2)}) collective-permute-start(f32[128,256]{1,0:T(8,128)S(1)} %get-tuple-element.136.refs_3_), channel_id=1, source_target_pairs={{0,3},{1,2},{2,1},{3,0},{4,7},{5,6},{6,5},{7,4},{8,11},{9,10},{10,... | collective-permute-start | bytes 393224 | tf_op jit(solution)/shard_map/ppermute | solution.py:38
  5.6 0.5 collective-permute-start.8
  6.1 0.1 collective-permute-start.7
  6.2 2.8 %collective-permute-start.2 = (f32[128,256]{1,0:T(8,128)S(1)}, f32[128,256]{1,0:T(8,128)S(1)}, u32[]{:S(2)}, u32[]{:S(2)}) collective-permute-start(f32[128,256]{1,0:T(8,128)S(1)} %get-tuple-element.137.refs_3_), channel_id=1, source_target_pairs={{0,3},{1,2},{2,1},{3,0},{4,7},{5,6},{6,5},{7,4},{8,11},{9,10},{10,... | collective-permute-start | bytes 393224 | tf_op jit(solution)/shard_map/ppermute | solution.py:38
  9.1 0.5 collective-permute-start.1
  9.6 5.0 %shard_map.68 = (f32[32,128,256]{2,1,0:T(8,128)S(1)}, s32[64,128,128]{2,1,0:T(8,128)S(1)}, s32[6,65]{1,0:T(8,128)S(1)}) custom-call(s32[3,2,4,8]{3,2,1,0:T(4,128)} %bitcast.10, s32[3,2,8]{2,1,0:T(2,128)} %bitcast.11, f32[32,128,256]{2,1,0:T(8,128)} %bitcast.8, s32[192,128,128]{2,1,0:T(8,128)} %bitcast.5), custom_call_target="tpu_custom_call" | custom-call | tf_op jit(solution)/shard_map/pallas_call | solution.py:236
  14.6 0.2 collective-permute-start
  14.8 3.1 %shard_map.70 = (f32[128,256]{1,0:T(8,128)S(1)}, f32[128,256]{1,0:T(8,128)S(1)}, f32[128,256]{1,0:T(8,128)S(1)}, f32[128,256]{1,0:T(8,128)S(1)}, bf16[64,256,128...) custom-call(s32[6,65]{1,0:T(8,128)S(1)} %get-tuple-element.69.refs_0_, ...), custom_call_target="tpu_custom_call" | custom-call | flops 1073741824 | bytes 4194304 | tf_op jit(solution)/shard_map/pallas_call | solution.py:254
  17.9 0.7 collective-permute-start.10
  18.6 3.2 %collective-permute-start.11 = (f32[128,256]{1,0:T(8,128)S(1)}, f32[128,256]{1,0:T(8,128)S(1)}, u32[]{:S(2)}, u32[]{:S(2)}) collective-permute-start(f32[128,256]{1,0:T(8,128)S(1)} %get-tuple-element.77), channel_id=1, source_target_pairs={{0,6},{1,7},{2,4},{3,5},{4,10},{5,11},{6,8},{7,9},{8,14},{9,15},{1... | collective-permute-start | bytes 393224 | tf_op jit(solution)/shard_map/ppermute | solution.py:38
  21.8 0.0 collective-permute-start.12
  21.8 1.9 %collective-permute-start.13 = (f32[128,256]{1,0:T(8,128)S(1)}, f32[128,256]{1,0:T(8,128)S(1)}, u32[]{:S(2)}, u32[]{:S(2)}) collective-permute-start(f32[128,256]{1,0:T(8,128)S(1)} %get-tuple-element.79), channel_id=1, source_target_pairs={{0,4},{1,5},{2,6},{3,7},{4,8},{5,9},{6,10},{7,11},{8,12},{9,13},{1... | collective-permute-start | bytes 393224 | tf_op jit(solution)/shard_map/ppermute | solution.py:38
  23.8 2.3 %shard_map.69 = (f32[128,256]{1,0:T(8,128)S(1)}, f32[128,256]{1,0:T(8,128)S(1)}, f32[128,256]{1,0:T(8,128)S(1)}, f32[128,256]{1,0:T(8,128)S(1)}, bf16[64,256,128...) custom-call(s32[6,65]{1,0:T(8,128)S(1)} %get-tuple-element.69.refs_0_, ...), custom_call_target="tpu_custom_call" | custom-call | flops 1073741824 | bytes 4194304 | tf_op jit(solution)/shard_map/pallas_call | solution.py:254
  26.0 2.7 %collective-permute-start.3 = (f32[128,256]{1,0:T(8,128)S(1)}, f32[128,256]{1,0:T(8,128)S(1)}, u32[]{:S(2)}, u32[]{:S(2)}) collective-permute-start(f32[128,256]{1,0:T(8,128)S(1)} %get-tuple-element.72), channel_id=1, source_target_pairs={{0,7},{1,6},{2,5},{3,4},{4,11},{5,10},{6,9},{7,8},{8,15},{9,14},{1... | collective-permute-start | bytes 393224 | tf_op jit(solution)/shard_map/ppermute | solution.py:38
  28.7 0.6 collective-permute-start.4
  29.3 1.3 %collective-permute-start.5 = (f32[128,256]{1,0:T(8,128)S(1)}, f32[128,256]{1,0:T(8,128)S(1)}, u32[]{:S(2)}, u32[]{:S(2)}) collective-permute-start(f32[128,256]{1,0:T(8,128)S(1)} %get-tuple-element.74), channel_id=1, source_target_pairs={{0,5},{1,4},{2,7},{3,6},{4,9},{5,8},{6,11},{7,10},{8,13},{9,12},{1... | collective-permute-start | bytes 393224 | tf_op jit(solution)/shard_map/ppermute | solution.py:38
  30.5 0.2 collective-permute-done.13
  30.8 1.8 %collective-permute-start.23 = (f32[128,256]{1,0:T(8,128)S(1)}, f32[128,256]{1,0:T(8,128)S(1)}, u32[]{:S(2)}, u32[]{:S(2)}) collective-permute-start(f32[128,256]{1,0:T(8,128)S(1)} %add_add_fusion.5.refs_3_), channel_id=1, source_target_pairs={{0,3},{1,2},{2,1},{3,0},{4,7},{5,6},{6,5},{7,4},{8,11},{9,10},{10,... | collective-permute-start | bytes 393224 | tf_op jit(solution)/shard_map/ppermute | solution.py:38
  32.7 3.1 %shard_map.71 = (f32[32,128,256]{2,1,0:T(8,128)S(1)}, s32[64,128,128]{2,1,0:T(8,128)S(1)}) custom-call(s32[6,65]{1,0:T(8,128)S(1)} %get-tuple-element.69.refs_0_, f32[32,128,256]{2,1,0:T(8,128)S(1)} %get-tuple-element.70.refs_1_, bf16[64,256,128]{2,1,0:T(8,128)(2,1)S(1)} %get-tuple-element.82.refs_2_, bf16[64,256,128]{2,1,0:T(8,128)(2,1)S(1)} %get-tuple-element.83.refs_3_, ...), custom_call_target="tpu_custom_call" | custom-call | flops 2147483648 | bytes 16777216 | tf_op jit(solution)/shard_map/pallas_call | solution.py:293
  35.8 0.7 collective-permute-start.22
  36.5 0.4 collective-permute-done.4
  36.9 1.3 %collective-permute-start.21 = (f32[128,256]{1,0:T(8,128)S(1)}, f32[128,256]{1,0:T(8,128)S(1)}, u32[]{:S(2)}, u32[]{:S(2)}) collective-permute-start(f32[128,256]{1,0:T(8,128)S(1)} %add_add_fusion.5.refs_3_), channel_id=1, source_target_pairs={{0,1},{1,0},{2,3},{3,2},{4,5},{5,4},{6,7},{7,6},{8,9},{9,8},{10,11... | collective-permute-start | bytes 393224 | tf_op jit(solution)/shard_map/ppermute | solution.py:38
  38.3 0.8 collective-permute-done.6
  39.1 1.0 %collective-permute-start.16 = (f32[128,256]{1,0:T(8,128)S(1)}, f32[128,256]{1,0:T(8,128)S(1)}, u32[]{:S(2)}, u32[]{:S(2)}) collective-permute-start(f32[128,256]{1,0:T(8,128)S(1)} %add_add_fusion.4.refs_3_), channel_id=1, source_target_pairs={{0,3},{1,2},{2,1},{3,0},{4,7},{5,6},{6,5},{7,4},{8,11},{9,10},{10,... | collective-permute-start | bytes 393224 | tf_op jit(solution)/shard_map/ppermute | solution.py:38
  40.1 1.5 %collective-permute-start.15 = (f32[128,256]{1,0:T(8,128)S(1)}, f32[128,256]{1,0:T(8,128)S(1)}, u32[]{:S(2)}, u32[]{:S(2)}) collective-permute-start(f32[128,256]{1,0:T(8,128)S(1)} %add_add_fusion.4.refs_3_), channel_id=1, source_target_pairs={{0,2},{1,3},{2,0},{3,1},{4,6},{5,7},{6,4},{7,5},{8,10},{9,11},{10,... | collective-permute-start | bytes 393224 | tf_op jit(solution)/shard_map/ppermute | solution.py:38
  41.6 1.1 %collective-permute-start.14 = (f32[128,256]{1,0:T(8,128)S(1)}, f32[128,256]{1,0:T(8,128)S(1)}, u32[]{:S(2)}, u32[]{:S(2)}) collective-permute-start(f32[128,256]{1,0:T(8,128)S(1)} %add_add_fusion.4.refs_3_), channel_id=1, source_target_pairs={{0,1},{1,0},{2,3},{3,2},{4,5},{5,4},{6,7},{7,6},{8,9},{9,8},{10,11... | collective-permute-start | bytes 393224 | tf_op jit(solution)/shard_map/ppermute | solution.py:38
  42.7 0.4 collective-permute-done.21.refs_4_
  43.1 2.6 %shard_map.73 = (f32[128,256]{1,0:T(8,128)S(1)}, f32[128,256]{1,0:T(8,128)S(1)}, f32[128,256]{1,0:T(8,128)S(1)}, f32[128,256]{1,0:T(8,128)S(1)}, bf16[64,256,128...) custom-call(s32[6,65]{1,0:T(8,128)S(1)} %get-tuple-element.69.refs_0_, ...), custom_call_target="tpu_custom_call" | custom-call | flops 1073741824 | bytes 4194304 | tf_op jit(solution)/shard_map/pallas_call | solution.py:254
  45.7 1.3 %collective-permute-start.24 = (f32[128,256]{1,0:T(8,128)S(1)}, f32[128,256]{1,0:T(8,128)S(1)}, u32[]{:S(2)}, u32[]{:S(2)}) collective-permute-start(f32[128,256]{1,0:T(8,128)S(1)} %get-tuple-element.98), channel_id=1, source_target_pairs={{0,7},{1,6},{2,5},{3,4},{4,11},{5,10},{6,9},{7,8},{8,15},{9,14},{1... | collective-permute-start | bytes 393224 | tf_op jit(solution)/shard_map/ppermute | solution.py:38
  47.0 1.0 %collective-permute-start.25 = (f32[128,256]{1,0:T(8,128)S(1)}, f32[128,256]{1,0:T(8,128)S(1)}, u32[]{:S(2)}, u32[]{:S(2)}) collective-permute-start(f32[128,256]{1,0:T(8,128)S(1)} %get-tuple-element.99), channel_id=1, source_target_pairs={{0,6},{1,7},{2,4},{3,5},{4,10},{5,11},{6,8},{7,9},{8,14},{9,15},{1... | collective-permute-start | bytes 393224 | tf_op jit(solution)/shard_map/ppermute | solution.py:38
  48.0 2.1 %collective-permute-start.26 = (f32[128,256]{1,0:T(8,128)S(1)}, f32[128,256]{1,0:T(8,128)S(1)}, u32[]{:S(2)}, u32[]{:S(2)}) collective-permute-start(f32[128,256]{1,0:T(8,128)S(1)} %get-tuple-element.100), channel_id=1, source_target_pairs={{0,5},{1,4},{2,7},{3,6},{4,9},{5,8},{6,11},{7,10},{8,13},{9,12},{1... | collective-permute-start | bytes 393224 | tf_op jit(solution)/shard_map/ppermute | solution.py:38
  50.2 2.8 %shard_map.72 = (f32[128,256]{1,0:T(8,128)S(1)}, f32[128,256]{1,0:T(8,128)S(1)}, f32[128,256]{1,0:T(8,128)S(1)}, f32[128,256]{1,0:T(8,128)S(1)}, bf16[64,256,128...) custom-call(s32[6,65]{1,0:T(8,128)S(1)} %get-tuple-element.69.refs_0_, ...), custom_call_target="tpu_custom_call" | custom-call | flops 1073741824 | bytes 4194304 | tf_op jit(solution)/shard_map/pallas_call | solution.py:254
  53.0 1.9 %collective-permute-start.17 = (f32[128,256]{1,0:T(8,128)S(1)}, f32[128,256]{1,0:T(8,128)S(1)}, u32[]{:S(2)}, u32[]{:S(2)}) collective-permute-start(f32[128,256]{1,0:T(8,128)S(1)} %get-tuple-element.93), channel_id=1, source_target_pairs={{0,7},{1,6},{2,5},{3,4},{4,11},{5,10},{6,9},{7,8},{8,15},{9,14},{1... | collective-permute-start | bytes 393224 | tf_op jit(solution)/shard_map/ppermute | solution.py:38
  54.9 1.6 %collective-permute-start.18 = (f32[128,256]{1,0:T(8,128)S(1)}, f32[128,256]{1,0:T(8,128)S(1)}, u32[]{:S(2)}, u32[]{:S(2)}) collective-permute-start(f32[128,256]{1,0:T(8,128)S(1)} %get-tuple-element.94), channel_id=1, source_target_pairs={{0,6},{1,7},{2,4},{3,5},{4,10},{5,11},{6,8},{7,9},{8,14},{9,15},{1... | collective-permute-start | bytes 393224 | tf_op jit(solution)/shard_map/ppermute | solution.py:38
  56.4 1.4 %collective-permute-start.19 = (f32[128,256]{1,0:T(8,128)S(1)}, f32[128,256]{1,0:T(8,128)S(1)}, u32[]{:S(2)}, u32[]{:S(2)}) collective-permute-start(f32[128,256]{1,0:T(8,128)S(1)} %get-tuple-element.95), channel_id=1, source_target_pairs={{0,5},{1,4},{2,7},{3,6},{4,9},{5,8},{6,11},{7,10},{8,13},{9,12},{1... | collective-permute-start | bytes 393224 | tf_op jit(solution)/shard_map/ppermute | solution.py:38
  57.9 0.1 collective-permute-start.20
  58.0 0.8 collective-permute-done.27
  58.8 1.2 %collective-permute-start.37 = (f32[128,256]{1,0:T(8,128)S(1)}, f32[128,256]{1,0:T(8,128)S(1)}, u32[]{:S(2)}, u32[]{:S(2)}) collective-permute-start(f32[128,256]{1,0:T(8,128)S(1)} %add_add_fusion.3.refs_3_), channel_id=1, source_target_pairs={{0,3},{1,2},{2,1},{3,0},{4,7},{5,6},{6,5},{7,4},{8,11},{9,10},{10,... | collective-permute-start | bytes 393224 | tf_op jit(solution)/shard_map/ppermute | solution.py:38
  60.0 3.3 %shard_map.74 = (f32[32,128,256]{2,1,0:T(8,128)S(1)}, s32[64,128,128]{2,1,0:T(8,128)S(1)}) custom-call(s32[6,65]{1,0:T(8,128)S(1)} %get-tuple-element.69.refs_0_, f32[32,128,256]{2,1,0:T(8,128)S(1)} %get-tuple-element.87.refs_1_, bf16[64,256,128]{2,1,0:T(8,128)(2,1)S(1)} %get-tuple-element.104.refs_2_, bf16[64,256,128]{2,1,0:T(8,128)(2,1)S(1)} %get-tuple-element.105.refs_3_, ...), custom_call_target="tpu_custom_call" | custom-call | flops 2147483648 | bytes 16777216 | tf_op jit(solution)/shard_map/pallas_call | solution.py:293
  63.3 2.2 %collective-permute-start.36 = (f32[128,256]{1,0:T(8,128)S(1)}, f32[128,256]{1,0:T(8,128)S(1)}, u32[]{:S(2)}, u32[]{:S(2)}) collective-permute-start(f32[128,256]{1,0:T(8,128)S(1)} %add_add_fusion.3.refs_3_), channel_id=1, source_target_pairs={{0,2},{1,3},{2,0},{3,1},{4,6},{5,7},{6,4},{7,5},{8,10},{9,11},{10,... | collective-permute-start | bytes 393224 | tf_op jit(solution)/shard_map/ppermute | solution.py:38
  65.5 0.3 collective-permute-start.35
  65.8 0.1 collective-permute-done.20
  65.9 1.3 %collective-permute-start.30 = (f32[128,256]{1,0:T(8,128)S(1)}, f32[128,256]{1,0:T(8,128)S(1)}, u32[]{:S(2)}, u32[]{:S(2)}) collective-permute-start(f32[128,256]{1,0:T(8,128)S(1)} %add_add_fusion.2.refs_3_), channel_id=1, source_target_pairs={{0,3},{1,2},{2,1},{3,0},{4,7},{5,6},{6,5},{7,4},{8,11},{9,10},{10,... | collective-permute-start | bytes 393224 | tf_op jit(solution)/shard_map/ppermute | solution.py:38
  67.2 1.8 %collective-permute-start.29 = (f32[128,256]{1,0:T(8,128)S(1)}, f32[128,256]{1,0:T(8,128)S(1)}, u32[]{:S(2)}, u32[]{:S(2)}) collective-permute-start(f32[128,256]{1,0:T(8,128)S(1)} %add_add_fusion.2.refs_3_), channel_id=1, source_target_pairs={{0,2},{1,3},{2,0},{3,1},{4,6},{5,7},{6,4},{7,5},{8,10},{9,11},{10,... | collective-permute-start | bytes 393224 | tf_op jit(solution)/shard_map/ppermute | solution.py:38
  69.1 0.4 collective-permute-start.28
  69.5 1.3 %collective-permute-done.36.refs_5_ = f32[128,256]{1,0:T(8,128)S(1)} collective-permute-done((f32[128,256]{1,0:T(8,128)S(1)}, f32[128,256]{1,0:T(8,128)S(1)}, u32[]{:S(2)}, u32[]{:S(2)}) %collective-permute-start.36) | collective-permute-done | bytes 131104 | tf_op jit(solution)/shard_map/ppermute | solution.py:38
  70.8 1.0 %collective-permute-done.35.refs_4_ = f32[128,256]{1,0:T(8,128)S(1)} collective-permute-done((f32[128,256]{1,0:T(8,128)S(1)}, f32[128,256]{1,0:T(8,128)S(1)}, u32[]{:S(2)}, u32[]{:S(2)}) %collective-permute-start.35) | collective-permute-done | bytes 131104 | tf_op jit(solution)/shard_map/ppermute | solution.py:38
  71.9 2.8 %shard_map.76 = (f32[128,256]{1,0:T(8,128)S(1)}, f32[128,256]{1,0:T(8,128)S(1)}, f32[128,256]{1,0:T(8,128)S(1)}, f32[128,256]{1,0:T(8,128)S(1)}, bf16[64,256,128...) custom-call(s32[6,65]{1,0:T(8,128)S(1)} %get-tuple-element.69.refs_0_, ...), custom_call_target="tpu_custom_call" | custom-call | flops 1073741824 | bytes 4194304 | tf_op jit(solution)/shard_map/pallas_call | solution.py:254
  74.7 0.5 collective-permute-start.38
  75.2 1.5 %collective-permute-start.39 = (f32[128,256]{1,0:T(8,128)S(1)}, f32[128,256]{1,0:T(8,128)S(1)}, u32[]{:S(2)}, u32[]{:S(2)}) collective-permute-start(f32[128,256]{1,0:T(8,128)S(1)} %get-tuple-element.121), channel_id=1, source_target_pairs={{0,6},{1,7},{2,4},{3,5},{4,10},{5,11},{6,8},{7,9},{8,14},{9,15},{1... | collective-permute-start | bytes 393224 | tf_op jit(solution)/shard_map/ppermute | solution.py:38
  76.7 0.1 collective-permute-start.40
  76.8 1.2 %collective-permute-start.41 = (f32[128,256]{1,0:T(8,128)S(1)}, f32[128,256]{1,0:T(8,128)S(1)}, u32[]{:S(2)}, u32[]{:S(2)}) collective-permute-start(f32[128,256]{1,0:T(8,128)S(1)} %get-tuple-element.123), channel_id=1, source_target_pairs={{0,4},{1,5},{2,6},{3,7},{4,8},{5,9},{6,10},{7,11},{8,12},{9,13},{1... | collective-permute-start | bytes 393224 | tf_op jit(solution)/shard_map/ppermute | solution.py:38
  78.0 2.6 %shard_map.75 = (f32[128,256]{1,0:T(8,128)S(1)}, f32[128,256]{1,0:T(8,128)S(1)}, f32[128,256]{1,0:T(8,128)S(1)}, f32[128,256]{1,0:T(8,128)S(1)}, bf16[64,256,128...) custom-call(s32[6,65]{1,0:T(8,128)S(1)} %get-tuple-element.69.refs_0_, ...), custom_call_target="tpu_custom_call" | custom-call | flops 1073741824 | bytes 4194304 | tf_op jit(solution)/shard_map/pallas_call | solution.py:254
  80.6 2.1 %collective-permute-start.31 = (f32[128,256]{1,0:T(8,128)S(1)}, f32[128,256]{1,0:T(8,128)S(1)}, u32[]{:S(2)}, u32[]{:S(2)}) collective-permute-start(f32[128,256]{1,0:T(8,128)S(1)} %get-tuple-element.115), channel_id=1, source_target_pairs={{0,7},{1,6},{2,5},{3,4},{4,11},{5,10},{6,9},{7,8},{8,15},{9,14},{1... | collective-permute-start | bytes 393224 | tf_op jit(solution)/shard_map/ppermute | solution.py:38
  82.7 1.6 %collective-permute-done.38 = f32[128,256]{1,0:T(8,128)S(1)} collective-permute-done((f32[128,256]{1,0:T(8,128)S(1)}, f32[128,256]{1,0:T(8,128)S(1)}, u32[]{:S(2)}, u32[]{:S(2)}) %collective-permute-start.38) | collective-permute-done | bytes 131104 | tf_op jit(solution)/shard_map/ppermute | solution.py:38
  84.2 0.6 collective-permute-start.33
  84.9 1.1 %collective-permute-done.40 = f32[128,256]{1,0:T(8,128)S(1)} collective-permute-done((f32[128,256]{1,0:T(8,128)S(1)}, f32[128,256]{1,0:T(8,128)S(1)}, u32[]{:S(2)}, u32[]{:S(2)}) %collective-permute-start.40) | collective-permute-done | bytes 131104 | tf_op jit(solution)/shard_map/ppermute | solution.py:38
  86.0 0.5 collective-permute-start.34
  86.5 0.5 collective-permute-done.41
  87.0 5.1 %shard_map.77 = f32[32,128,256]{2,1,0:T(8,128)} custom-call(s32[6,65]{1,0:T(8,128)S(1)} %get-tuple-element.69.refs_0_, f32[32,128,256]{2,1,0:T(8,128)S(1)} %get-tuple-element.109.refs_1_, bf16[64,256,128]{2,1,0:T(8,128)(2,1)S(1)} %get-tuple-element.126.refs_2_, bf16[64,256,128]{2,1,0:T(8,128)(2,1)S(1)} %get-tuple-element.127.refs_3_, ...), custom_call_target="tpu_custom_call" | custom-call | flops 2147483648 | bytes 16777216 | tf_op jit(solution)/shard_map/pallas_call | solution.py:293
  92.2 1.1 %collective-permute-done.33 = f32[128,256]{1,0:T(8,128)S(1)} collective-permute-done((f32[128,256]{1,0:T(8,128)S(1)}, f32[128,256]{1,0:T(8,128)S(1)}, u32[]{:S(2)}, u32[]{:S(2)}) %collective-permute-start.33) | collective-permute-done | bytes 131104 | tf_op jit(solution)/shard_map/ppermute | solution.py:38
  93.3 0.6 collective-permute-done.34
  93.9 0.7 pad_maximum_fusion
  (38 shorter events, 0.3 us)
Async XLA Ops:
  1.6 13.0 %collective-permute-start.9 = (f32[128,256]{1,0:T(8,128)S(1)}, f32[128,256]{1,0:T(8,128)S(1)}, u32[]{:S(2)}, u32[]{:S(2)}) collective-permute-start(f32[128,256]{1,0:T(8,128)S(1)} %get-tuple-element.136.refs_3_), channel_id=1, source_target_pairs={{0,3},{1,2},{2,1},{3,0},{4,7},{5,6},{6,5},{7,4},{8,11},{9,10},{10,... | collective-permute-start | bytes 393224 | tf_op jit(solution)/shard_map/ppermute | solution.py:38
  5.6 9.3 %collective-permute-start.8 = (f32[128,256]{1,0:T(8,128)S(1)}, f32[128,256]{1,0:T(8,128)S(1)}, u32[]{:S(2)}, u32[]{:S(2)}) collective-permute-start(f32[128,256]{1,0:T(8,128)S(1)} %get-tuple-element.136.refs_3_), channel_id=1, source_target_pairs={{0,2},{1,3},{2,0},{3,1},{4,6},{5,7},{6,4},{7,5},{8,10},{9,11},{10,... | collective-permute-start | bytes 393224 | tf_op jit(solution)/shard_map/ppermute | solution.py:38
  6.1 8.8 %collective-permute-start.7 = (f32[128,256]{1,0:T(8,128)S(1)}, f32[128,256]{1,0:T(8,128)S(1)}, u32[]{:S(2)}, u32[]{:S(2)}) collective-permute-start(f32[128,256]{1,0:T(8,128)S(1)} %get-tuple-element.136.refs_3_), channel_id=1, source_target_pairs={{0,1},{1,0},{2,3},{3,2},{4,5},{5,4},{6,7},{7,6},{8,9},{9,8},{10,11... | collective-permute-start | bytes 393224 | tf_op jit(solution)/shard_map/ppermute | solution.py:38
  6.2 15.6 %collective-permute-start.2 = (f32[128,256]{1,0:T(8,128)S(1)}, f32[128,256]{1,0:T(8,128)S(1)}, u32[]{:S(2)}, u32[]{:S(2)}) collective-permute-start(f32[128,256]{1,0:T(8,128)S(1)} %get-tuple-element.137.refs_3_), channel_id=1, source_target_pairs={{0,3},{1,2},{2,1},{3,0},{4,7},{5,6},{6,5},{7,4},{8,11},{9,10},{10,... | collective-permute-start | bytes 393224 | tf_op jit(solution)/shard_map/ppermute | solution.py:38
  9.1 12.8 %collective-permute-start.1 = (f32[128,256]{1,0:T(8,128)S(1)}, f32[128,256]{1,0:T(8,128)S(1)}, u32[]{:S(2)}, u32[]{:S(2)}) collective-permute-start(f32[128,256]{1,0:T(8,128)S(1)} %get-tuple-element.137.refs_3_), channel_id=1, source_target_pairs={{0,2},{1,3},{2,0},{3,1},{4,6},{5,7},{6,4},{7,5},{8,10},{9,11},{10,... | collective-permute-start | bytes 393224 | tf_op jit(solution)/shard_map/ppermute | solution.py:38
  14.6 9.1 %collective-permute-start = (f32[128,256]{1,0:T(8,128)S(1)}, f32[128,256]{1,0:T(8,128)S(1)}, u32[]{:S(2)}, u32[]{:S(2)}) collective-permute-start(f32[128,256]{1,0:T(8,128)S(1)} %get-tuple-element.137.refs_3_), channel_id=1, source_target_pairs={{0,1},{1,0},{2,3},{3,2},{4,5},{5,4},{6,7},{7,6},{8,9},{9,8},{10,11... | collective-permute-start | bytes 393224 | tf_op jit(solution)/shard_map/ppermute | solution.py:38
  17.9 10.7 %collective-permute-start.10 = (f32[128,256]{1,0:T(8,128)S(1)}, f32[128,256]{1,0:T(8,128)S(1)}, u32[]{:S(2)}, u32[]{:S(2)}) collective-permute-start(f32[128,256]{1,0:T(8,128)S(1)} %get-tuple-element.76), channel_id=1, source_target_pairs={{0,7},{1,6},{2,5},{3,4},{4,11},{5,10},{6,9},{7,8},{8,15},{9,14},{1... | collective-permute-start | bytes 393224 | tf_op jit(solution)/shard_map/ppermute | solution.py:38
  18.6 10.7 %collective-permute-start.11 = (f32[128,256]{1,0:T(8,128)S(1)}, f32[128,256]{1,0:T(8,128)S(1)}, u32[]{:S(2)}, u32[]{:S(2)}) collective-permute-start(f32[128,256]{1,0:T(8,128)S(1)} %get-tuple-element.77), channel_id=1, source_target_pairs={{0,6},{1,7},{2,4},{3,5},{4,10},{5,11},{6,8},{7,9},{8,14},{9,15},{1... | collective-permute-start | bytes 393224 | tf_op jit(solution)/shard_map/ppermute | solution.py:38
  21.8 8.7 %collective-permute-start.12 = (f32[128,256]{1,0:T(8,128)S(1)}, f32[128,256]{1,0:T(8,128)S(1)}, u32[]{:S(2)}, u32[]{:S(2)}) collective-permute-start(f32[128,256]{1,0:T(8,128)S(1)} %get-tuple-element.78), channel_id=1, source_target_pairs={{0,5},{1,4},{2,7},{3,6},{4,9},{5,8},{6,11},{7,10},{8,13},{9,12},{1... | collective-permute-start | bytes 393224 | tf_op jit(solution)/shard_map/ppermute | solution.py:38
  21.8 8.9 %collective-permute-start.13 = (f32[128,256]{1,0:T(8,128)S(1)}, f32[128,256]{1,0:T(8,128)S(1)}, u32[]{:S(2)}, u32[]{:S(2)}) collective-permute-start(f32[128,256]{1,0:T(8,128)S(1)} %get-tuple-element.79), channel_id=1, source_target_pairs={{0,4},{1,5},{2,6},{3,7},{4,8},{5,9},{6,10},{7,11},{8,12},{9,13},{1... | collective-permute-start | bytes 393224 | tf_op jit(solution)/shard_map/ppermute | solution.py:38
  26.0 9.7 %collective-permute-start.3 = (f32[128,256]{1,0:T(8,128)S(1)}, f32[128,256]{1,0:T(8,128)S(1)}, u32[]{:S(2)}, u32[]{:S(2)}) collective-permute-start(f32[128,256]{1,0:T(8,128)S(1)} %get-tuple-element.72), channel_id=1, source_target_pairs={{0,7},{1,6},{2,5},{3,4},{4,11},{5,10},{6,9},{7,8},{8,15},{9,14},{1... | collective-permute-start | bytes 393224 | tf_op jit(solution)/shard_map/ppermute | solution.py:38
  28.7 8.2 %collective-permute-start.4 = (f32[128,256]{1,0:T(8,128)S(1)}, f32[128,256]{1,0:T(8,128)S(1)}, u32[]{:S(2)}, u32[]{:S(2)}) collective-permute-start(f32[128,256]{1,0:T(8,128)S(1)} %get-tuple-element.73), channel_id=1, source_target_pairs={{0,6},{1,7},{2,4},{3,5},{4,10},{5,11},{6,8},{7,9},{8,14},{9,15},{1... | collective-permute-start | bytes 393224 | tf_op jit(solution)/shard_map/ppermute | solution.py:38
  29.3 9.0 %collective-permute-start.5 = (f32[128,256]{1,0:T(8,128)S(1)}, f32[128,256]{1,0:T(8,128)S(1)}, u32[]{:S(2)}, u32[]{:S(2)}) collective-permute-start(f32[128,256]{1,0:T(8,128)S(1)} %get-tuple-element.74), channel_id=1, source_target_pairs={{0,5},{1,4},{2,7},{3,6},{4,9},{5,8},{6,11},{7,10},{8,13},{9,12},{1... | collective-permute-start | bytes 393224 | tf_op jit(solution)/shard_map/ppermute | solution.py:38
  30.5 8.6 %collective-permute-start.6 = (f32[128,256]{1,0:T(8,128)S(1)}, f32[128,256]{1,0:T(8,128)S(1)}, u32[]{:S(2)}, u32[]{:S(2)}) collective-permute-start(f32[128,256]{1,0:T(8,128)S(1)} %get-tuple-element.75), channel_id=1, source_target_pairs={{0,4},{1,5},{2,6},{3,7},{4,8},{5,9},{6,10},{7,11},{8,12},{9,13},{1... | collective-permute-start | bytes 393224 | tf_op jit(solution)/shard_map/ppermute | solution.py:38
  30.8 10.8 %collective-permute-start.23 = (f32[128,256]{1,0:T(8,128)S(1)}, f32[128,256]{1,0:T(8,128)S(1)}, u32[]{:S(2)}, u32[]{:S(2)}) collective-permute-start(f32[128,256]{1,0:T(8,128)S(1)} %add_add_fusion.5.refs_3_), channel_id=1, source_target_pairs={{0,3},{1,2},{2,1},{3,0},{4,7},{5,6},{6,5},{7,4},{8,11},{9,10},{10,... | collective-permute-start | bytes 393224 | tf_op jit(solution)/shard_map/ppermute | solution.py:38
  35.8 6.9 %collective-permute-start.22 = (f32[128,256]{1,0:T(8,128)S(1)}, f32[128,256]{1,0:T(8,128)S(1)}, u32[]{:S(2)}, u32[]{:S(2)}) collective-permute-start(f32[128,256]{1,0:T(8,128)S(1)} %add_add_fusion.5.refs_3_), channel_id=1, source_target_pairs={{0,2},{1,3},{2,0},{3,1},{4,6},{5,7},{6,4},{7,5},{8,10},{9,11},{10,... | collective-permute-start | bytes 393224 | tf_op jit(solution)/shard_map/ppermute | solution.py:38
  36.9 6.2 %collective-permute-start.21 = (f32[128,256]{1,0:T(8,128)S(1)}, f32[128,256]{1,0:T(8,128)S(1)}, u32[]{:S(2)}, u32[]{:S(2)}) collective-permute-start(f32[128,256]{1,0:T(8,128)S(1)} %add_add_fusion.5.refs_3_), channel_id=1, source_target_pairs={{0,1},{1,0},{2,3},{3,2},{4,5},{5,4},{6,7},{7,6},{8,9},{9,8},{10,11... | collective-permute-start | bytes 393224 | tf_op jit(solution)/shard_map/ppermute | solution.py:38
  39.1 8.9 %collective-permute-start.16 = (f32[128,256]{1,0:T(8,128)S(1)}, f32[128,256]{1,0:T(8,128)S(1)}, u32[]{:S(2)}, u32[]{:S(2)}) collective-permute-start(f32[128,256]{1,0:T(8,128)S(1)} %add_add_fusion.4.refs_3_), channel_id=1, source_target_pairs={{0,3},{1,2},{2,1},{3,0},{4,7},{5,6},{6,5},{7,4},{8,11},{9,10},{10,... | collective-permute-start | bytes 393224 | tf_op jit(solution)/shard_map/ppermute | solution.py:38
  40.1 10.0 %collective-permute-start.15 = (f32[128,256]{1,0:T(8,128)S(1)}, f32[128,256]{1,0:T(8,128)S(1)}, u32[]{:S(2)}, u32[]{:S(2)}) collective-permute-start(f32[128,256]{1,0:T(8,128)S(1)} %add_add_fusion.4.refs_3_), channel_id=1, source_target_pairs={{0,2},{1,3},{2,0},{3,1},{4,6},{5,7},{6,4},{7,5},{8,10},{9,11},{10,... | collective-permute-start | bytes 393224 | tf_op jit(solution)/shard_map/ppermute | solution.py:38
  41.6 8.6 %collective-permute-start.14 = (f32[128,256]{1,0:T(8,128)S(1)}, f32[128,256]{1,0:T(8,128)S(1)}, u32[]{:S(2)}, u32[]{:S(2)}) collective-permute-start(f32[128,256]{1,0:T(8,128)S(1)} %add_add_fusion.4.refs_3_), channel_id=1, source_target_pairs={{0,1},{1,0},{2,3},{3,2},{4,5},{5,4},{6,7},{7,6},{8,9},{9,8},{10,11... | collective-permute-start | bytes 393224 | tf_op jit(solution)/shard_map/ppermute | solution.py:38
  45.7 9.2 %collective-permute-start.24 = (f32[128,256]{1,0:T(8,128)S(1)}, f32[128,256]{1,0:T(8,128)S(1)}, u32[]{:S(2)}, u32[]{:S(2)}) collective-permute-start(f32[128,256]{1,0:T(8,128)S(1)} %get-tuple-element.98), channel_id=1, source_target_pairs={{0,7},{1,6},{2,5},{3,4},{4,11},{5,10},{6,9},{7,8},{8,15},{9,14},{1... | collective-permute-start | bytes 393224 | tf_op jit(solution)/shard_map/ppermute | solution.py:38
  47.0 9.5 %collective-permute-start.25 = (f32[128,256]{1,0:T(8,128)S(1)}, f32[128,256]{1,0:T(8,128)S(1)}, u32[]{:S(2)}, u32[]{:S(2)}) collective-permute-start(f32[128,256]{1,0:T(8,128)S(1)} %get-tuple-element.99), channel_id=1, source_target_pairs={{0,6},{1,7},{2,4},{3,5},{4,10},{5,11},{6,8},{7,9},{8,14},{9,15},{1... | collective-permute-start | bytes 393224 | tf_op jit(solution)/shard_map/ppermute | solution.py:38
  48.0 9.9 %collective-permute-start.26 = (f32[128,256]{1,0:T(8,128)S(1)}, f32[128,256]{1,0:T(8,128)S(1)}, u32[]{:S(2)}, u32[]{:S(2)}) collective-permute-start(f32[128,256]{1,0:T(8,128)S(1)} %get-tuple-element.100), channel_id=1, source_target_pairs={{0,5},{1,4},{2,7},{3,6},{4,9},{5,8},{6,11},{7,10},{8,13},{9,12},{1... | collective-permute-start | bytes 393224 | tf_op jit(solution)/shard_map/ppermute | solution.py:38
  50.1 8.6 %collective-permute-start.27 = (f32[128,256]{1,0:T(8,128)S(1)}, f32[128,256]{1,0:T(8,128)S(1)}, u32[]{:S(2)}, u32[]{:S(2)}) collective-permute-start(f32[128,256]{1,0:T(8,128)S(1)} %get-tuple-element.101), channel_id=1, source_target_pairs={{0,4},{1,5},{2,6},{3,7},{4,8},{5,9},{6,10},{7,11},{8,12},{9,13},{1... | collective-permute-start | bytes 393224 | tf_op jit(solution)/shard_map/ppermute | solution.py:38
  53.0 10.3 %collective-permute-start.17 = (f32[128,256]{1,0:T(8,128)S(1)}, f32[128,256]{1,0:T(8,128)S(1)}, u32[]{:S(2)}, u32[]{:S(2)}) collective-permute-start(f32[128,256]{1,0:T(8,128)S(1)} %get-tuple-element.93), channel_id=1, source_target_pairs={{0,7},{1,6},{2,5},{3,4},{4,11},{5,10},{6,9},{7,8},{8,15},{9,14},{1... | collective-permute-start | bytes 393224 | tf_op jit(solution)/shard_map/ppermute | solution.py:38
  54.9 10.6 %collective-permute-start.18 = (f32[128,256]{1,0:T(8,128)S(1)}, f32[128,256]{1,0:T(8,128)S(1)}, u32[]{:S(2)}, u32[]{:S(2)}) collective-permute-start(f32[128,256]{1,0:T(8,128)S(1)} %get-tuple-element.94), channel_id=1, source_target_pairs={{0,6},{1,7},{2,4},{3,5},{4,10},{5,11},{6,8},{7,9},{8,14},{9,15},{1... | collective-permute-start | bytes 393224 | tf_op jit(solution)/shard_map/ppermute | solution.py:38
  56.4 9.3 %collective-permute-start.19 = (f32[128,256]{1,0:T(8,128)S(1)}, f32[128,256]{1,0:T(8,128)S(1)}, u32[]{:S(2)}, u32[]{:S(2)}) collective-permute-start(f32[128,256]{1,0:T(8,128)S(1)} %get-tuple-element.95), channel_id=1, source_target_pairs={{0,5},{1,4},{2,7},{3,6},{4,9},{5,8},{6,11},{7,10},{8,13},{9,12},{1... | collective-permute-start | bytes 393224 | tf_op jit(solution)/shard_map/ppermute | solution.py:38
  57.9 8.0 %collective-permute-start.20 = (f32[128,256]{1,0:T(8,128)S(1)}, f32[128,256]{1,0:T(8,128)S(1)}, u32[]{:S(2)}, u32[]{:S(2)}) collective-permute-start(f32[128,256]{1,0:T(8,128)S(1)} %get-tuple-element.96), channel_id=1, source_target_pairs={{0,4},{1,5},{2,6},{3,7},{4,8},{5,9},{6,10},{7,11},{8,12},{9,13},{1... | collective-permute-start | bytes 393224 | tf_op jit(solution)/shard_map/ppermute | solution.py:38
  58.8 10.3 %collective-permute-start.37 = (f32[128,256]{1,0:T(8,128)S(1)}, f32[128,256]{1,0:T(8,128)S(1)}, u32[]{:S(2)}, u32[]{:S(2)}) collective-permute-start(f32[128,256]{1,0:T(8,128)S(1)} %add_add_fusion.3.refs_3_), channel_id=1, source_target_pairs={{0,3},{1,2},{2,1},{3,0},{4,7},{5,6},{6,5},{7,4},{8,11},{9,10},{10,... | collective-permute-start | bytes 393224 | tf_op jit(solution)/shard_map/ppermute | solution.py:38
  63.3 7.5 %collective-permute-start.36 = (f32[128,256]{1,0:T(8,128)S(1)}, f32[128,256]{1,0:T(8,128)S(1)}, u32[]{:S(2)}, u32[]{:S(2)}) collective-permute-start(f32[128,256]{1,0:T(8,128)S(1)} %add_add_fusion.3.refs_3_), channel_id=1, source_target_pairs={{0,2},{1,3},{2,0},{3,1},{4,6},{5,7},{6,4},{7,5},{8,10},{9,11},{10,... | collective-permute-start | bytes 393224 | tf_op jit(solution)/shard_map/ppermute | solution.py:38
  65.5 6.4 %collective-permute-start.35 = (f32[128,256]{1,0:T(8,128)S(1)}, f32[128,256]{1,0:T(8,128)S(1)}, u32[]{:S(2)}, u32[]{:S(2)}) collective-permute-start(f32[128,256]{1,0:T(8,128)S(1)} %add_add_fusion.3.refs_3_), channel_id=1, source_target_pairs={{0,1},{1,0},{2,3},{3,2},{4,5},{5,4},{6,7},{7,6},{8,9},{9,8},{10,11... | collective-permute-start | bytes 393224 | tf_op jit(solution)/shard_map/ppermute | solution.py:38
  65.9 10.8 %collective-permute-start.30 = (f32[128,256]{1,0:T(8,128)S(1)}, f32[128,256]{1,0:T(8,128)S(1)}, u32[]{:S(2)}, u32[]{:S(2)}) collective-permute-start(f32[128,256]{1,0:T(8,128)S(1)} %add_add_fusion.2.refs_3_), channel_id=1, source_target_pairs={{0,3},{1,2},{2,1},{3,0},{4,7},{5,6},{6,5},{7,4},{8,11},{9,10},{10,... | collective-permute-start | bytes 393224 | tf_op jit(solution)/shard_map/ppermute | solution.py:38
  67.2 9.6 %collective-permute-start.29 = (f32[128,256]{1,0:T(8,128)S(1)}, f32[128,256]{1,0:T(8,128)S(1)}, u32[]{:S(2)}, u32[]{:S(2)}) collective-permute-start(f32[128,256]{1,0:T(8,128)S(1)} %add_add_fusion.2.refs_3_), channel_id=1, source_target_pairs={{0,2},{1,3},{2,0},{3,1},{4,6},{5,7},{6,4},{7,5},{8,10},{9,11},{10,... | collective-permute-start | bytes 393224 | tf_op jit(solution)/shard_map/ppermute | solution.py:38
  69.1 8.9 %collective-permute-start.28 = (f32[128,256]{1,0:T(8,128)S(1)}, f32[128,256]{1,0:T(8,128)S(1)}, u32[]{:S(2)}, u32[]{:S(2)}) collective-permute-start(f32[128,256]{1,0:T(8,128)S(1)} %add_add_fusion.2.refs_3_), channel_id=1, source_target_pairs={{0,1},{1,0},{2,3},{3,2},{4,5},{5,4},{6,7},{7,6},{8,9},{9,8},{10,11... | collective-permute-start | bytes 393224 | tf_op jit(solution)/shard_map/ppermute | solution.py:38
  74.7 9.5 %collective-permute-start.38 = (f32[128,256]{1,0:T(8,128)S(1)}, f32[128,256]{1,0:T(8,128)S(1)}, u32[]{:S(2)}, u32[]{:S(2)}) collective-permute-start(f32[128,256]{1,0:T(8,128)S(1)} %get-tuple-element.120), channel_id=1, source_target_pairs={{0,7},{1,6},{2,5},{3,4},{4,11},{5,10},{6,9},{7,8},{8,15},{9,14},{1... | collective-permute-start | bytes 393224 | tf_op jit(solution)/shard_map/ppermute | solution.py:38
  75.2 9.0 %collective-permute-start.39 = (f32[128,256]{1,0:T(8,128)S(1)}, f32[128,256]{1,0:T(8,128)S(1)}, u32[]{:S(2)}, u32[]{:S(2)}) collective-permute-start(f32[128,256]{1,0:T(8,128)S(1)} %get-tuple-element.121), channel_id=1, source_target_pairs={{0,6},{1,7},{2,4},{3,5},{4,10},{5,11},{6,8},{7,9},{8,14},{9,15},{1... | collective-permute-start | bytes 393224 | tf_op jit(solution)/shard_map/ppermute | solution.py:38
  76.7 9.2 %collective-permute-start.40 = (f32[128,256]{1,0:T(8,128)S(1)}, f32[128,256]{1,0:T(8,128)S(1)}, u32[]{:S(2)}, u32[]{:S(2)}) collective-permute-start(f32[128,256]{1,0:T(8,128)S(1)} %get-tuple-element.122), channel_id=1, source_target_pairs={{0,5},{1,4},{2,7},{3,6},{4,9},{5,8},{6,11},{7,10},{8,13},{9,12},{1... | collective-permute-start | bytes 393224 | tf_op jit(solution)/shard_map/ppermute | solution.py:38
  76.8 10.2 %collective-permute-start.41 = (f32[128,256]{1,0:T(8,128)S(1)}, f32[128,256]{1,0:T(8,128)S(1)}, u32[]{:S(2)}, u32[]{:S(2)}) collective-permute-start(f32[128,256]{1,0:T(8,128)S(1)} %get-tuple-element.123), channel_id=1, source_target_pairs={{0,4},{1,5},{2,6},{3,7},{4,8},{5,9},{6,10},{7,11},{8,12},{9,13},{1... | collective-permute-start | bytes 393224 | tf_op jit(solution)/shard_map/ppermute | solution.py:38
  80.6 11.6 %collective-permute-start.31 = (f32[128,256]{1,0:T(8,128)S(1)}, f32[128,256]{1,0:T(8,128)S(1)}, u32[]{:S(2)}, u32[]{:S(2)}) collective-permute-start(f32[128,256]{1,0:T(8,128)S(1)} %get-tuple-element.115), channel_id=1, source_target_pairs={{0,7},{1,6},{2,5},{3,4},{4,11},{5,10},{6,9},{7,8},{8,15},{9,14},{1... | collective-permute-start | bytes 393224 | tf_op jit(solution)/shard_map/ppermute | solution.py:38
  84.2 8.0 %collective-permute-start.32 = (f32[128,256]{1,0:T(8,128)S(1)}, f32[128,256]{1,0:T(8,128)S(1)}, u32[]{:S(2)}, u32[]{:S(2)}) collective-permute-start(f32[128,256]{1,0:T(8,128)S(1)} %get-tuple-element.116), channel_id=1, source_target_pairs={{0,6},{1,7},{2,4},{3,5},{4,10},{5,11},{6,8},{7,9},{8,14},{9,15},{1... | collective-permute-start | bytes 393224 | tf_op jit(solution)/shard_map/ppermute | solution.py:38
  84.2 9.1 %collective-permute-start.33 = (f32[128,256]{1,0:T(8,128)S(1)}, f32[128,256]{1,0:T(8,128)S(1)}, u32[]{:S(2)}, u32[]{:S(2)}) collective-permute-start(f32[128,256]{1,0:T(8,128)S(1)} %get-tuple-element.117), channel_id=1, source_target_pairs={{0,5},{1,4},{2,7},{3,6},{4,9},{5,8},{6,11},{7,10},{8,13},{9,12},{1... | collective-permute-start | bytes 393224 | tf_op jit(solution)/shard_map/ppermute | solution.py:38
  86.0 7.9 %collective-permute-start.34 = (f32[128,256]{1,0:T(8,128)S(1)}, f32[128,256]{1,0:T(8,128)S(1)}, u32[]{:S(2)}, u32[]{:S(2)}) collective-permute-start(f32[128,256]{1,0:T(8,128)S(1)} %get-tuple-element.118), channel_id=1, source_target_pairs={{0,4},{1,5},{2,6},{3,7},{4,8},{5,9},{6,10},{7,11},{8,12},{9,13},{1... | collective-permute-start | bytes 393224 | tf_op jit(solution)/shard_map/ppermute | solution.py:38

commit v2 on v1

--- a/solution.py
+++ b/solution.py
@@ -224,6 +224,10 @@
     return pltpu.with_memory_space_constraint(x, pltpu.VMEM)
 
 
+def in_smem(x):
+    return pltpu.with_memory_space_constraint(x, pltpu.SMEM)
+
+
 def in_hbm(x):
     return pltpu.with_memory_space_constraint(x, pltpu.HBM)
 
@@ -238,7 +242,7 @@
         out_shape=[
             pltpu.VMEM(users.shape, users.dtype),
             pltpu.VMEM((sh.total, sh.block, sh.block), blocks.dtype),
-            jax.ShapeDtypeStruct((sh.steps * sh.chunks, sh.total + 1), jnp.int32),
+            pltpu.SMEM((sh.steps * sh.chunks, sh.total + 1), jnp.int32),
         ],
         in_specs=[whole_in(pltpu.SMEM)] * 2 + [whole_in(pl.ANY)] * 2,
         out_specs=[whole_in(pltpu.VMEM)] * 2 + [whole_in(pltpu.SMEM)],
@@ -270,7 +274,7 @@
             bytes_accessed=8 * sh.total * sh.block * sh.block // sh.chunks,
             transcendentals=0,
         ),
-    )(lists, *[in_vmem(x) for x in (users, ratings, *items)])
+    )(in_smem(lists), *[in_vmem(x) for x in (users, ratings, *items)])
     return outs[:nu], outs[nu], outs[nu + 1]
 
 
@@ -303,7 +307,7 @@
             flops=work, bytes_accessed=8 * users.size + 8 * sh.total * size, transcendentals=0
         ),
     )(
-        lists,
+        in_smem(lists),
         *[in_vmem(x) for x in (users, *residuals, *item_parts)],
         *[in_hbm(blocks)] * more,
     )

time: 94.9 us -> 89.2 us (0.940)
  Pallas kernels: 32.8 us -> 27.7 us
  waiting for transfers between devices: 10.1 us -> 6.4 us
  starting transfers between devices: 49 us -> 51.7 us
    ppermute x42, waiting for transfers between devices: 10.1 us -> 6.4 us  [moved(): return lax.ppermute(x, ('blk', 'user'), route)]
    pallas_call x6, Pallas kernels: 16.2 us -> 13.1 us  [item_terms(): pl.pallas_call(functools.partial(item_kernel, sh, nu, row), out_shape=[pl...]
    ppermute x42, starting transfers between devices: 49 us -> 51.7 us  [moved(): return lax.ppermute(x, ('blk', 'user'), route)]
    pallas_call x3, Pallas kernels: 11.5 us -> 10.2 us  [new_users(): pl.pallas_call(functools.partial(user_kernel, sh, step), out_shape=out_sh...]
  transfers between devices with their start and end apart: 42 -> 42, of which waited for: 13 -> 15; matrix products, arithmetic and copies ran while one was open for 0% -> 0% of each run, Pallas kernels for 35% -> 31%
where the time goes in v2:
time: 89.2 us; the launch traced here: 88.6 us
  starting transfers between devices  51.7 us (58%)
  Pallas kernels  27.7 us (31%)
  waiting for transfers between devices  6.4 us (7%)
  local copies, waits for them, and re-layouts  0.99 us (1%)
  other arithmetic  0.92 us (1%)
    ppermute x42, starting transfers between devices, moved(): return lax.ppermute(x, ('blk', 'user'), route)  51.7 us
    pallas_call x6, Pallas kernels, item_terms(): pl.pallas_call(functools.partial(item_kernel, sh, nu, row), out_shape=[pl...  13.1 us
    pallas_call x3, Pallas kernels, new_users(): pl.pallas_call(functools.partial(user_kernel, sh, step), out_shape=out_sh...  10.2 us
    ppermute x42, waiting for transfers between devices, moved(): return lax.ppermute(x, ('blk', 'user'), route)  6.4 us
    pallas_call x1, Pallas kernels, load(): pl.pallas_call(functools.partial(load_kernel, sh), out_shape=[pltpu.VMEM(...  4.39 us
  transfers between devices with their start and end apart: 42, of which 15 were waited for; matrix products, arithmetic and copies ran while one was open for 0% of the time, Pallas kernels for 31%

profile of v2, /device:TPU:0, one launch (start us, length us, event | category | flops | bytes accessed | tf_op | source)
XLA Modules:
  0.0 88.6 jit_solution(9217662875952186655)
XLA Ops:
  0.6 1.0 %fusion = (f32[128,256]{1,0:T(8,128)S(1)}, f32[128,256]{1,0:T(8,128)S(1)}) fusion(f32[256,256]{1,0:T(8,128)} %param.6), kind=kLoop, calls=%fused_computation.7 | loop fusion | bytes 524288 | tf_op jit(solution)/shard_map/slice | solution.py:323
  1.6 4.0 %collective-permute-start.9 = (f32[128,256]{1,0:T(8,128)S(1)}, f32[128,256]{1,0:T(8,128)S(1)}, u32[]{:S(2)}, u32[]{:S(2)}) collective-permute-start(f32[128,256]{1,0:T(8,128)S(1)} %get-tuple-element.136.refs_3_), channel_id=1, source_target_pairs={{0,3},{1,2},{2,1},{3,0},{4,7},{5,6},{6,5},{7,4},{8,11},{9,10},{10,... | collective-permute-start | bytes 393224 | tf_op jit(solution)/shard_map/ppermute | solution.py:38
  5.6 0.5 collective-permute-start.8
  6.1 0.1 collective-permute-start.7
  6.2 2.8 %collective-permute-start.2 = (f32[128,256]{1,0:T(8,128)S(1)}, f32[128,256]{1,0:T(8,128)S(1)}, u32[]{:S(2)}, u32[]{:S(2)}) collective-permute-start(f32[128,256]{1,0:T(8,128)S(1)} %get-tuple-element.137.refs_3_), channel_id=1, source_target_pairs={{0,3},{1,2},{2,1},{3,0},{4,7},{5,6},{6,5},{7,4},{8,11},{9,10},{10,... | collective-permute-start | bytes 393224 | tf_op jit(solution)/shard_map/ppermute | solution.py:38
  9.1 0.5 collective-permute-start.1
  9.6 4.4 %shard_map.68 = (f32[32,128,256]{2,1,0:T(8,128)S(1)}, s32[64,128,128]{2,1,0:T(8,128)S(1)}, s32[6,65]{1,0:T(8,128)S(4)}) custom-call(s32[3,2,4,8]{3,2,1,0:T(4,128)} %bitcast.10, s32[3,2,8]{2,1,0:T(2,128)} %bitcast.11, f32[32,128,256]{2,1,0:T(8,128)} %bitcast.8, s32[192,128,128]{2,1,0:T(8,128)} %bitcast.5), custom_call_target="tpu_custom_call" | custom-call | tf_op jit(solution)/shard_map/pallas_call | solution.py:240
  14.0 0.2 collective-permute-start
  14.2 0.6 collective-permute-done.8.refs_5_
  14.8 2.4 %shard_map.70 = (f32[128,256]{1,0:T(8,128)S(1)}, f32[128,256]{1,0:T(8,128)S(1)}, f32[128,256]{1,0:T(8,128)S(1)}, f32[128,256]{1,0:T(8,128)S(1)}, bf16[64,256,128...) custom-call(s32[6,65]{1,0:T(8,128)S(4)} %get-tuple-element.69.refs_0_, ...), custom_call_target="tpu_custom_call" | custom-call | flops 1073741824 | bytes 4194304 | tf_op jit(solution)/shard_map/pallas_call | solution.py:258
  17.3 3.5 %collective-permute-start.11 = (f32[128,256]{1,0:T(8,128)S(1)}, f32[128,256]{1,0:T(8,128)S(1)}, u32[]{:S(2)}, u32[]{:S(2)}) collective-permute-start(f32[128,256]{1,0:T(8,128)S(1)} %get-tuple-element.77), channel_id=1, source_target_pairs={{0,6},{1,7},{2,4},{3,5},{4,10},{5,11},{6,8},{7,9},{8,14},{9,15},{1... | collective-permute-start | bytes 393224 | tf_op jit(solution)/shard_map/ppermute | solution.py:38
  20.8 1.7 %collective-permute-start.13 = (f32[128,256]{1,0:T(8,128)S(1)}, f32[128,256]{1,0:T(8,128)S(1)}, u32[]{:S(2)}, u32[]{:S(2)}) collective-permute-start(f32[128,256]{1,0:T(8,128)S(1)} %get-tuple-element.79), channel_id=1, source_target_pairs={{0,4},{1,5},{2,6},{3,7},{4,8},{5,9},{6,10},{7,11},{8,12},{9,13},{1... | collective-permute-start | bytes 393224 | tf_op jit(solution)/shard_map/ppermute | solution.py:38
  22.5 1.7 %shard_map.69 = (f32[128,256]{1,0:T(8,128)S(1)}, f32[128,256]{1,0:T(8,128)S(1)}, f32[128,256]{1,0:T(8,128)S(1)}, f32[128,256]{1,0:T(8,128)S(1)}, bf16[64,256,128...) custom-call(s32[6,65]{1,0:T(8,128)S(4)} %get-tuple-element.69.refs_0_, ...), custom_call_target="tpu_custom_call" | custom-call | flops 1073741824 | bytes 4194304 | tf_op jit(solution)/shard_map/pallas_call | solution.py:258
  24.1 2.4 %collective-permute-start.3 = (f32[128,256]{1,0:T(8,128)S(1)}, f32[128,256]{1,0:T(8,128)S(1)}, u32[]{:S(2)}, u32[]{:S(2)}) collective-permute-start(f32[128,256]{1,0:T(8,128)S(1)} %get-tuple-element.72), channel_id=1, source_target_pairs={{0,7},{1,6},{2,5},{3,4},{4,11},{5,10},{6,9},{7,8},{8,15},{9,14},{1... | collective-permute-start | bytes 393224 | tf_op jit(solution)/shard_map/ppermute | solution.py:38
  26.5 1.1 %collective-permute-start.4 = (f32[128,256]{1,0:T(8,128)S(1)}, f32[128,256]{1,0:T(8,128)S(1)}, u32[]{:S(2)}, u32[]{:S(2)}) collective-permute-start(f32[128,256]{1,0:T(8,128)S(1)} %get-tuple-element.73), channel_id=1, source_target_pairs={{0,6},{1,7},{2,4},{3,5},{4,10},{5,11},{6,8},{7,9},{8,14},{9,15},{1... | collective-permute-start | bytes 393224 | tf_op jit(solution)/shard_map/ppermute | solution.py:38
  27.6 0.8 collective-permute-start.5
  28.4 0.1 collective-permute-start.6
  28.5 0.7 collective-permute-done.13
  29.2 1.5 %collective-permute-start.23 = (f32[128,256]{1,0:T(8,128)S(1)}, f32[128,256]{1,0:T(8,128)S(1)}, u32[]{:S(2)}, u32[]{:S(2)}) collective-permute-start(f32[128,256]{1,0:T(8,128)S(1)} %add_add_fusion.5.refs_3_), channel_id=1, source_target_pairs={{0,3},{1,2},{2,1},{3,0},{4,7},{5,6},{6,5},{7,4},{8,11},{9,10},{10,... | collective-permute-start | bytes 393224 | tf_op jit(solution)/shard_map/ppermute | solution.py:38
  30.7 2.5 %shard_map.71 = (f32[32,128,256]{2,1,0:T(8,128)S(1)}, s32[64,128,128]{2,1,0:T(8,128)S(1)}) custom-call(s32[6,65]{1,0:T(8,128)S(4)} %get-tuple-element.69.refs_0_, f32[32,128,256]{2,1,0:T(8,128)S(1)} %get-tuple-element.70.refs_1_, bf16[64,256,128]{2,1,0:T(8,128)(2,1)S(1)} %get-tuple-element.82.refs_2_, bf16[64,256,128]{2,1,0:T(8,128)(2,1)S(1)} %get-tuple-element.83.refs_3_, ...), custom_call_target="tpu_custom_call" | custom-call | flops 2147483648 | bytes 16777216 | tf_op jit(solution)/shard_map/pallas_call | solution.py:297
  33.2 1.3 %collective-permute-start.22 = (f32[128,256]{1,0:T(8,128)S(1)}, f32[128,256]{1,0:T(8,128)S(1)}, u32[]{:S(2)}, u32[]{:S(2)}) collective-permute-start(f32[128,256]{1,0:T(8,128)S(1)} %add_add_fusion.5.refs_3_), channel_id=1, source_target_pairs={{0,2},{1,3},{2,0},{3,1},{4,6},{5,7},{6,4},{7,5},{8,10},{9,11},{10,... | collective-permute-start | bytes 393224 | tf_op jit(solution)/shard_map/ppermute | solution.py:38
  34.5 2.3 %collective-permute-start.21 = (f32[128,256]{1,0:T(8,128)S(1)}, f32[128,256]{1,0:T(8,128)S(1)}, u32[]{:S(2)}, u32[]{:S(2)}) collective-permute-start(f32[128,256]{1,0:T(8,128)S(1)} %add_add_fusion.5.refs_3_), channel_id=1, source_target_pairs={{0,1},{1,0},{2,3},{3,2},{4,5},{5,4},{6,7},{7,6},{8,9},{9,8},{10,11... | collective-permute-start | bytes 393224 | tf_op jit(solution)/shard_map/ppermute | solution.py:38
  36.8 0.5 collective-permute-done.6
  37.3 0.8 collective-permute-start.16
  38.1 1.5 %collective-permute-start.15 = (f32[128,256]{1,0:T(8,128)S(1)}, f32[128,256]{1,0:T(8,128)S(1)}, u32[]{:S(2)}, u32[]{:S(2)}) collective-permute-start(f32[128,256]{1,0:T(8,128)S(1)} %add_add_fusion.4.refs_3_), channel_id=1, source_target_pairs={{0,2},{1,3},{2,0},{3,1},{4,6},{5,7},{6,4},{7,5},{8,10},{9,11},{10,... | collective-permute-start | bytes 393224 | tf_op jit(solution)/shard_map/ppermute | solution.py:38
  39.6 1.3 %collective-permute-start.14 = (f32[128,256]{1,0:T(8,128)S(1)}, f32[128,256]{1,0:T(8,128)S(1)}, u32[]{:S(2)}, u32[]{:S(2)}) collective-permute-start(f32[128,256]{1,0:T(8,128)S(1)} %add_add_fusion.4.refs_3_), channel_id=1, source_target_pairs={{0,1},{1,0},{2,3},{3,2},{4,5},{5,4},{6,7},{7,6},{8,9},{9,8},{10,11... | collective-permute-start | bytes 393224 | tf_op jit(solution)/shard_map/ppermute | solution.py:38
  40.9 0.2 collective-permute-done.21.refs_4_
  41.1 2.5 %shard_map.73 = (f32[128,256]{1,0:T(8,128)S(1)}, f32[128,256]{1,0:T(8,128)S(1)}, f32[128,256]{1,0:T(8,128)S(1)}, f32[128,256]{1,0:T(8,128)S(1)}, bf16[64,256,128...) custom-call(s32[6,65]{1,0:T(8,128)S(4)} %get-tuple-element.69.refs_0_, ...), custom_call_target="tpu_custom_call" | custom-call | flops 1073741824 | bytes 4194304 | tf_op jit(solution)/shard_map/pallas_call | solution.py:258
  43.6 2.8 %collective-permute-start.25 = (f32[128,256]{1,0:T(8,128)S(1)}, f32[128,256]{1,0:T(8,128)S(1)}, u32[]{:S(2)}, u32[]{:S(2)}) collective-permute-start(f32[128,256]{1,0:T(8,128)S(1)} %get-tuple-element.99), channel_id=1, source_target_pairs={{0,6},{1,7},{2,4},{3,5},{4,10},{5,11},{6,8},{7,9},{8,14},{9,15},{1... | collective-permute-start | bytes 393224 | tf_op jit(solution)/shard_map/ppermute | solution.py:38
  46.4 0.5 collective-permute-start.26
  46.8 0.7 collective-permute-start.27
  47.5 1.7 %shard_map.72 = (f32[128,256]{1,0:T(8,128)S(1)}, f32[128,256]{1,0:T(8,128)S(1)}, f32[128,256]{1,0:T(8,128)S(1)}, f32[128,256]{1,0:T(8,128)S(1)}, bf16[64,256,128...) custom-call(s32[6,65]{1,0:T(8,128)S(4)} %get-tuple-element.69.refs_0_, ...), custom_call_target="tpu_custom_call" | custom-call | flops 1073741824 | bytes 4194304 | tf_op jit(solution)/shard_map/pallas_call | solution.py:258
  49.2 2.2 %collective-permute-start.17 = (f32[128,256]{1,0:T(8,128)S(1)}, f32[128,256]{1,0:T(8,128)S(1)}, u32[]{:S(2)}, u32[]{:S(2)}) collective-permute-start(f32[128,256]{1,0:T(8,128)S(1)} %get-tuple-element.93), channel_id=1, source_target_pairs={{0,7},{1,6},{2,5},{3,4},{4,11},{5,10},{6,9},{7,8},{8,15},{9,14},{1... | collective-permute-start | bytes 393224 | tf_op jit(solution)/shard_map/ppermute | solution.py:38
  51.4 0.4 collective-permute-done.24
  51.7 1.4 %collective-permute-start.18 = (f32[128,256]{1,0:T(8,128)S(1)}, f32[128,256]{1,0:T(8,128)S(1)}, u32[]{:S(2)}, u32[]{:S(2)}) collective-permute-start(f32[128,256]{1,0:T(8,128)S(1)} %get-tuple-element.94), channel_id=1, source_target_pairs={{0,6},{1,7},{2,4},{3,5},{4,10},{5,11},{6,8},{7,9},{8,14},{9,15},{1... | collective-permute-start | bytes 393224 | tf_op jit(solution)/shard_map/ppermute | solution.py:38
  53.2 0.1 collective-permute-done.25
  53.3 1.2 %collective-permute-start.19 = (f32[128,256]{1,0:T(8,128)S(1)}, f32[128,256]{1,0:T(8,128)S(1)}, u32[]{:S(2)}, u32[]{:S(2)}) collective-permute-start(f32[128,256]{1,0:T(8,128)S(1)} %get-tuple-element.95), channel_id=1, source_target_pairs={{0,5},{1,4},{2,7},{3,6},{4,9},{5,8},{6,11},{7,10},{8,13},{9,12},{1... | collective-permute-start | bytes 393224 | tf_op jit(solution)/shard_map/ppermute | solution.py:38
  54.5 0.7 collective-permute-start.20
  55.3 1.7 %collective-permute-start.37 = (f32[128,256]{1,0:T(8,128)S(1)}, f32[128,256]{1,0:T(8,128)S(1)}, u32[]{:S(2)}, u32[]{:S(2)}) collective-permute-start(f32[128,256]{1,0:T(8,128)S(1)} %add_add_fusion.3.refs_3_), channel_id=1, source_target_pairs={{0,3},{1,2},{2,1},{3,0},{4,7},{5,6},{6,5},{7,4},{8,11},{9,10},{10,... | collective-permute-start | bytes 393224 | tf_op jit(solution)/shard_map/ppermute | solution.py:38
  56.9 2.7 %shard_map.74 = (f32[32,128,256]{2,1,0:T(8,128)S(1)}, s32[64,128,128]{2,1,0:T(8,128)S(1)}) custom-call(s32[6,65]{1,0:T(8,128)S(4)} %get-tuple-element.69.refs_0_, f32[32,128,256]{2,1,0:T(8,128)S(1)} %get-tuple-element.87.refs_1_, bf16[64,256,128]{2,1,0:T(8,128)(2,1)S(1)} %get-tuple-element.104.refs_2_, bf16[64,256,128]{2,1,0:T(8,128)(2,1)S(1)} %get-tuple-element.105.refs_3_, ...), custom_call_target="tpu_custom_call" | custom-call | flops 2147483648 | bytes 16777216 | tf_op jit(solution)/shard_map/pallas_call | solution.py:297
  59.6 1.4 %collective-permute-start.36 = (f32[128,256]{1,0:T(8,128)S(1)}, f32[128,256]{1,0:T(8,128)S(1)}, u32[]{:S(2)}, u32[]{:S(2)}) collective-permute-start(f32[128,256]{1,0:T(8,128)S(1)} %add_add_fusion.3.refs_3_), channel_id=1, source_target_pairs={{0,2},{1,3},{2,0},{3,1},{4,6},{5,7},{6,4},{7,5},{8,10},{9,11},{10,... | collective-permute-start | bytes 393224 | tf_op jit(solution)/shard_map/ppermute | solution.py:38
  61.1 1.0 %collective-permute-start.35 = (f32[128,256]{1,0:T(8,128)S(1)}, f32[128,256]{1,0:T(8,128)S(1)}, u32[]{:S(2)}, u32[]{:S(2)}) collective-permute-start(f32[128,256]{1,0:T(8,128)S(1)} %add_add_fusion.3.refs_3_), channel_id=1, source_target_pairs={{0,1},{1,0},{2,3},{3,2},{4,5},{5,4},{6,7},{7,6},{8,9},{9,8},{10,11... | collective-permute-start | bytes 393224 | tf_op jit(solution)/shard_map/ppermute | solution.py:38
  62.1 0.1 collective-permute-done.20
  62.2 2.8 %collective-permute-start.30 = (f32[128,256]{1,0:T(8,128)S(1)}, f32[128,256]{1,0:T(8,128)S(1)}, u32[]{:S(2)}, u32[]{:S(2)}) collective-permute-start(f32[128,256]{1,0:T(8,128)S(1)} %add_add_fusion.2.refs_3_), channel_id=1, source_target_pairs={{0,3},{1,2},{2,1},{3,0},{4,7},{5,6},{6,5},{7,4},{8,11},{9,10},{10,... | collective-permute-start | bytes 393224 | tf_op jit(solution)/shard_map/ppermute | solution.py:38
  65.0 0.8 collective-permute-start.28
  65.8 0.3 collective-permute-done.36.refs_5_
  66.1 0.3 collective-permute-done.35.refs_4_
  66.4 2.5 %shard_map.76 = (f32[128,256]{1,0:T(8,128)S(1)}, f32[128,256]{1,0:T(8,128)S(1)}, f32[128,256]{1,0:T(8,128)S(1)}, f32[128,256]{1,0:T(8,128)S(1)}, bf16[64,256,128...) custom-call(s32[6,65]{1,0:T(8,128)S(4)} %get-tuple-element.69.refs_0_, ...), custom_call_target="tpu_custom_call" | custom-call | flops 1073741824 | bytes 4194304 | tf_op jit(solution)/shard_map/pallas_call | solution.py:258
  68.9 0.7 collective-permute-start.38
  69.6 2.8 %collective-permute-start.39 = (f32[128,256]{1,0:T(8,128)S(1)}, f32[128,256]{1,0:T(8,128)S(1)}, u32[]{:S(2)}, u32[]{:S(2)}) collective-permute-start(f32[128,256]{1,0:T(8,128)S(1)} %get-tuple-element.121), channel_id=1, source_target_pairs={{0,6},{1,7},{2,4},{3,5},{4,10},{5,11},{6,8},{7,9},{8,14},{9,15},{1... | collective-permute-start | bytes 393224 | tf_op jit(solution)/shard_map/ppermute | solution.py:38
  72.4 0.3 collective-permute-start.40
  72.6 1.5 %collective-permute-start.41 = (f32[128,256]{1,0:T(8,128)S(1)}, f32[128,256]{1,0:T(8,128)S(1)}, u32[]{:S(2)}, u32[]{:S(2)}) collective-permute-start(f32[128,256]{1,0:T(8,128)S(1)} %get-tuple-element.123), channel_id=1, source_target_pairs={{0,4},{1,5},{2,6},{3,7},{4,8},{5,9},{6,10},{7,11},{8,12},{9,13},{1... | collective-permute-start | bytes 393224 | tf_op jit(solution)/shard_map/ppermute | solution.py:38
  74.2 2.5 %shard_map.75 = (f32[128,256]{1,0:T(8,128)S(1)}, f32[128,256]{1,0:T(8,128)S(1)}, f32[128,256]{1,0:T(8,128)S(1)}, f32[128,256]{1,0:T(8,128)S(1)}, bf16[64,256,128...) custom-call(s32[6,65]{1,0:T(8,128)S(4)} %get-tuple-element.69.refs_0_, ...), custom_call_target="tpu_custom_call" | custom-call | flops 1073741824 | bytes 4194304 | tf_op jit(solution)/shard_map/pallas_call | solution.py:258
  76.6 0.4 collective-permute-start.31
  77.1 0.7 collective-permute-done.38
  77.7 2.1 %collective-permute-start.32 = (f32[128,256]{1,0:T(8,128)S(1)}, f32[128,256]{1,0:T(8,128)S(1)}, u32[]{:S(2)}, u32[]{:S(2)}) collective-permute-start(f32[128,256]{1,0:T(8,128)S(1)} %get-tuple-element.116), channel_id=1, source_target_pairs={{0,6},{1,7},{2,4},{3,5},{4,10},{5,11},{6,8},{7,9},{8,14},{9,15},{1... | collective-permute-start | bytes 393224 | tf_op jit(solution)/shard_map/ppermute | solution.py:38
  79.9 0.5 collective-permute-start.33
  80.3 0.2 collective-permute-done.40
  80.5 0.6 collective-permute-done.41
  81.1 5.0 %shard_map.77 = f32[32,128,256]{2,1,0:T(8,128)} custom-call(s32[6,65]{1,0:T(8,128)S(4)} %get-tuple-element.69.refs_0_, f32[32,128,256]{2,1,0:T(8,128)S(1)} %get-tuple-element.109.refs_1_, bf16[64,256,128]{2,1,0:T(8,128)(2,1)S(1)} %get-tuple-element.126.refs_2_, bf16[64,256,128]{2,1,0:T(8,128)(2,1)S(1)} %get-tuple-element.127.refs_3_, ...), custom_call_target="tpu_custom_call" | custom-call | flops 2147483648 | bytes 16777216 | tf_op jit(solution)/shard_map/pallas_call | solution.py:297
  86.1 0.1 collective-permute-done.32
  86.2 0.8 collective-permute-done.33
  87.0 0.9 collective-permute-done.34
  87.8 0.7 pad_maximum_fusion
  (38 shorter events, 0.4 us)
Async XLA Ops:
  1.6 12.4 %collective-permute-start.9 = (f32[128,256]{1,0:T(8,128)S(1)}, f32[128,256]{1,0:T(8,128)S(1)}, u32[]{:S(2)}, u32[]{:S(2)}) collective-permute-start(f32[128,256]{1,0:T(8,128)S(1)} %get-tuple-element.136.refs_3_), channel_id=1, source_target_pairs={{0,3},{1,2},{2,1},{3,0},{4,7},{5,6},{6,5},{7,4},{8,11},{9,10},{10,... | collective-permute-start | bytes 393224 | tf_op jit(solution)/shard_map/ppermute | solution.py:38
  5.6 9.2 %collective-permute-start.8 = (f32[128,256]{1,0:T(8,128)S(1)}, f32[128,256]{1,0:T(8,128)S(1)}, u32[]{:S(2)}, u32[]{:S(2)}) collective-permute-start(f32[128,256]{1,0:T(8,128)S(1)} %get-tuple-element.136.refs_3_), channel_id=1, source_target_pairs={{0,2},{1,3},{2,0},{3,1},{4,6},{5,7},{6,4},{7,5},{8,10},{9,11},{10,... | collective-permute-start | bytes 393224 | tf_op jit(solution)/shard_map/ppermute | solution.py:38
  6.1 8.7 %collective-permute-start.7 = (f32[128,256]{1,0:T(8,128)S(1)}, f32[128,256]{1,0:T(8,128)S(1)}, u32[]{:S(2)}, u32[]{:S(2)}) collective-permute-start(f32[128,256]{1,0:T(8,128)S(1)} %get-tuple-element.136.refs_3_), channel_id=1, source_target_pairs={{0,1},{1,0},{2,3},{3,2},{4,5},{5,4},{6,7},{7,6},{8,9},{9,8},{10,11... | collective-permute-start | bytes 393224 | tf_op jit(solution)/shard_map/ppermute | solution.py:38
  6.2 14.6 %collective-permute-start.2 = (f32[128,256]{1,0:T(8,128)S(1)}, f32[128,256]{1,0:T(8,128)S(1)}, u32[]{:S(2)}, u32[]{:S(2)}) collective-permute-start(f32[128,256]{1,0:T(8,128)S(1)} %get-tuple-element.137.refs_3_), channel_id=1, source_target_pairs={{0,3},{1,2},{2,1},{3,0},{4,7},{5,6},{6,5},{7,4},{8,11},{9,10},{10,... | collective-permute-start | bytes 393224 | tf_op jit(solution)/shard_map/ppermute | solution.py:38
  9.1 11.7 %collective-permute-start.1 = (f32[128,256]{1,0:T(8,128)S(1)}, f32[128,256]{1,0:T(8,128)S(1)}, u32[]{:S(2)}, u32[]{:S(2)}) collective-permute-start(f32[128,256]{1,0:T(8,128)S(1)} %get-tuple-element.137.refs_3_), channel_id=1, source_target_pairs={{0,2},{1,3},{2,0},{3,1},{4,6},{5,7},{6,4},{7,5},{8,10},{9,11},{10,... | collective-permute-start | bytes 393224 | tf_op jit(solution)/shard_map/ppermute | solution.py:38
  14.0 8.5 %collective-permute-start = (f32[128,256]{1,0:T(8,128)S(1)}, f32[128,256]{1,0:T(8,128)S(1)}, u32[]{:S(2)}, u32[]{:S(2)}) collective-permute-start(f32[128,256]{1,0:T(8,128)S(1)} %get-tuple-element.137.refs_3_), channel_id=1, source_target_pairs={{0,1},{1,0},{2,3},{3,2},{4,5},{5,4},{6,7},{7,6},{8,9},{9,8},{10,11... | collective-permute-start | bytes 393224 | tf_op jit(solution)/shard_map/ppermute | solution.py:38
  17.3 9.3 %collective-permute-start.10 = (f32[128,256]{1,0:T(8,128)S(1)}, f32[128,256]{1,0:T(8,128)S(1)}, u32[]{:S(2)}, u32[]{:S(2)}) collective-permute-start(f32[128,256]{1,0:T(8,128)S(1)} %get-tuple-element.76), channel_id=1, source_target_pairs={{0,7},{1,6},{2,5},{3,4},{4,11},{5,10},{6,9},{7,8},{8,15},{9,14},{1... | collective-permute-start | bytes 393224 | tf_op jit(solution)/shard_map/ppermute | solution.py:38
  17.3 10.3 %collective-permute-start.11 = (f32[128,256]{1,0:T(8,128)S(1)}, f32[128,256]{1,0:T(8,128)S(1)}, u32[]{:S(2)}, u32[]{:S(2)}) collective-permute-start(f32[128,256]{1,0:T(8,128)S(1)} %get-tuple-element.77), channel_id=1, source_target_pairs={{0,6},{1,7},{2,4},{3,5},{4,10},{5,11},{6,8},{7,9},{8,14},{9,15},{1... | collective-permute-start | bytes 393224 | tf_op jit(solution)/shard_map/ppermute | solution.py:38
  20.8 7.6 %collective-permute-start.12 = (f32[128,256]{1,0:T(8,128)S(1)}, f32[128,256]{1,0:T(8,128)S(1)}, u32[]{:S(2)}, u32[]{:S(2)}) collective-permute-start(f32[128,256]{1,0:T(8,128)S(1)} %get-tuple-element.78), channel_id=1, source_target_pairs={{0,5},{1,4},{2,7},{3,6},{4,9},{5,8},{6,11},{7,10},{8,13},{9,12},{1... | collective-permute-start | bytes 393224 | tf_op jit(solution)/shard_map/ppermute | solution.py:38
  20.8 8.4 %collective-permute-start.13 = (f32[128,256]{1,0:T(8,128)S(1)}, f32[128,256]{1,0:T(8,128)S(1)}, u32[]{:S(2)}, u32[]{:S(2)}) collective-permute-start(f32[128,256]{1,0:T(8,128)S(1)} %get-tuple-element.79), channel_id=1, source_target_pairs={{0,4},{1,5},{2,6},{3,7},{4,8},{5,9},{6,10},{7,11},{8,12},{9,13},{1... | collective-permute-start | bytes 393224 | tf_op jit(solution)/shard_map/ppermute | solution.py:38
  24.1 9.1 %collective-permute-start.3 = (f32[128,256]{1,0:T(8,128)S(1)}, f32[128,256]{1,0:T(8,128)S(1)}, u32[]{:S(2)}, u32[]{:S(2)}) collective-permute-start(f32[128,256]{1,0:T(8,128)S(1)} %get-tuple-element.72), channel_id=1, source_target_pairs={{0,7},{1,6},{2,5},{3,4},{4,11},{5,10},{6,9},{7,8},{8,15},{9,14},{1... | collective-permute-start | bytes 393224 | tf_op jit(solution)/shard_map/ppermute | solution.py:38
  26.5 8.0 %collective-permute-start.4 = (f32[128,256]{1,0:T(8,128)S(1)}, f32[128,256]{1,0:T(8,128)S(1)}, u32[]{:S(2)}, u32[]{:S(2)}) collective-permute-start(f32[128,256]{1,0:T(8,128)S(1)} %get-tuple-element.73), channel_id=1, source_target_pairs={{0,6},{1,7},{2,4},{3,5},{4,10},{5,11},{6,8},{7,9},{8,14},{9,15},{1... | collective-permute-start | bytes 393224 | tf_op jit(solution)/shard_map/ppermute | solution.py:38
  27.6 9.2 %collective-permute-start.5 = (f32[128,256]{1,0:T(8,128)S(1)}, f32[128,256]{1,0:T(8,128)S(1)}, u32[]{:S(2)}, u32[]{:S(2)}) collective-permute-start(f32[128,256]{1,0:T(8,128)S(1)} %get-tuple-element.74), channel_id=1, source_target_pairs={{0,5},{1,4},{2,7},{3,6},{4,9},{5,8},{6,11},{7,10},{8,13},{9,12},{1... | collective-permute-start | bytes 393224 | tf_op jit(solution)/shard_map/ppermute | solution.py:38
  28.4 8.9 %collective-permute-start.6 = (f32[128,256]{1,0:T(8,128)S(1)}, f32[128,256]{1,0:T(8,128)S(1)}, u32[]{:S(2)}, u32[]{:S(2)}) collective-permute-start(f32[128,256]{1,0:T(8,128)S(1)} %get-tuple-element.75), channel_id=1, source_target_pairs={{0,4},{1,5},{2,6},{3,7},{4,8},{5,9},{6,10},{7,11},{8,12},{9,13},{1... | collective-permute-start | bytes 393224 | tf_op jit(solution)/shard_map/ppermute | solution.py:38
  29.2 10.4 %collective-permute-start.23 = (f32[128,256]{1,0:T(8,128)S(1)}, f32[128,256]{1,0:T(8,128)S(1)}, u32[]{:S(2)}, u32[]{:S(2)}) collective-permute-start(f32[128,256]{1,0:T(8,128)S(1)} %add_add_fusion.5.refs_3_), channel_id=1, source_target_pairs={{0,3},{1,2},{2,1},{3,0},{4,7},{5,6},{6,5},{7,4},{8,11},{9,10},{10,... | collective-permute-start | bytes 393224 | tf_op jit(solution)/shard_map/ppermute | solution.py:38
  33.2 7.6 %collective-permute-start.22 = (f32[128,256]{1,0:T(8,128)S(1)}, f32[128,256]{1,0:T(8,128)S(1)}, u32[]{:S(2)}, u32[]{:S(2)}) collective-permute-start(f32[128,256]{1,0:T(8,128)S(1)} %add_add_fusion.5.refs_3_), channel_id=1, source_target_pairs={{0,2},{1,3},{2,0},{3,1},{4,6},{5,7},{6,4},{7,5},{8,10},{9,11},{10,... | collective-permute-start | bytes 393224 | tf_op jit(solution)/shard_map/ppermute | solution.py:38
  34.5 6.5 %collective-permute-start.21 = (f32[128,256]{1,0:T(8,128)S(1)}, f32[128,256]{1,0:T(8,128)S(1)}, u32[]{:S(2)}, u32[]{:S(2)}) collective-permute-start(f32[128,256]{1,0:T(8,128)S(1)} %add_add_fusion.5.refs_3_), channel_id=1, source_target_pairs={{0,1},{1,0},{2,3},{3,2},{4,5},{5,4},{6,7},{7,6},{8,9},{9,8},{10,11... | collective-permute-start | bytes 393224 | tf_op jit(solution)/shard_map/ppermute | solution.py:38
  37.3 9.1 %collective-permute-start.16 = (f32[128,256]{1,0:T(8,128)S(1)}, f32[128,256]{1,0:T(8,128)S(1)}, u32[]{:S(2)}, u32[]{:S(2)}) collective-permute-start(f32[128,256]{1,0:T(8,128)S(1)} %add_add_fusion.4.refs_3_), channel_id=1, source_target_pairs={{0,3},{1,2},{2,1},{3,0},{4,7},{5,6},{6,5},{7,4},{8,11},{9,10},{10,... | collective-permute-start | bytes 393224 | tf_op jit(solution)/shard_map/ppermute | solution.py:38
  38.1 8.8 %collective-permute-start.15 = (f32[128,256]{1,0:T(8,128)S(1)}, f32[128,256]{1,0:T(8,128)S(1)}, u32[]{:S(2)}, u32[]{:S(2)}) collective-permute-start(f32[128,256]{1,0:T(8,128)S(1)} %add_add_fusion.4.refs_3_), channel_id=1, source_target_pairs={{0,2},{1,3},{2,0},{3,1},{4,6},{5,7},{6,4},{7,5},{8,10},{9,11},{10,... | collective-permute-start | bytes 393224 | tf_op jit(solution)/shard_map/ppermute | solution.py:38
  39.6 7.9 %collective-permute-start.14 = (f32[128,256]{1,0:T(8,128)S(1)}, f32[128,256]{1,0:T(8,128)S(1)}, u32[]{:S(2)}, u32[]{:S(2)}) collective-permute-start(f32[128,256]{1,0:T(8,128)S(1)} %add_add_fusion.4.refs_3_), channel_id=1, source_target_pairs={{0,1},{1,0},{2,3},{3,2},{4,5},{5,4},{6,7},{7,6},{8,9},{9,8},{10,11... | collective-permute-start | bytes 393224 | tf_op jit(solution)/shard_map/ppermute | solution.py:38
  43.5 8.2 %collective-permute-start.24 = (f32[128,256]{1,0:T(8,128)S(1)}, f32[128,256]{1,0:T(8,128)S(1)}, u32[]{:S(2)}, u32[]{:S(2)}) collective-permute-start(f32[128,256]{1,0:T(8,128)S(1)} %get-tuple-element.98), channel_id=1, source_target_pairs={{0,7},{1,6},{2,5},{3,4},{4,11},{5,10},{6,9},{7,8},{8,15},{9,14},{1... | collective-permute-start | bytes 393224 | tf_op jit(solution)/shard_map/ppermute | solution.py:38
  43.6 9.7 %collective-permute-start.25 = (f32[128,256]{1,0:T(8,128)S(1)}, f32[128,256]{1,0:T(8,128)S(1)}, u32[]{:S(2)}, u32[]{:S(2)}) collective-permute-start(f32[128,256]{1,0:T(8,128)S(1)} %get-tuple-element.99), channel_id=1, source_target_pairs={{0,6},{1,7},{2,4},{3,5},{4,10},{5,11},{6,8},{7,9},{8,14},{9,15},{1... | collective-permute-start | bytes 393224 | tf_op jit(solution)/shard_map/ppermute | solution.py:38
  46.4 8.2 %collective-permute-start.26 = (f32[128,256]{1,0:T(8,128)S(1)}, f32[128,256]{1,0:T(8,128)S(1)}, u32[]{:S(2)}, u32[]{:S(2)}) collective-permute-start(f32[128,256]{1,0:T(8,128)S(1)} %get-tuple-element.100), channel_id=1, source_target_pairs={{0,5},{1,4},{2,7},{3,6},{4,9},{5,8},{6,11},{7,10},{8,13},{9,12},{1... | collective-permute-start | bytes 393224 | tf_op jit(solution)/shard_map/ppermute | solution.py:38
  46.8 8.4 %collective-permute-start.27 = (f32[128,256]{1,0:T(8,128)S(1)}, f32[128,256]{1,0:T(8,128)S(1)}, u32[]{:S(2)}, u32[]{:S(2)}) collective-permute-start(f32[128,256]{1,0:T(8,128)S(1)} %get-tuple-element.101), channel_id=1, source_target_pairs={{0,4},{1,5},{2,6},{3,7},{4,8},{5,9},{6,10},{7,11},{8,12},{9,13},{1... | collective-permute-start | bytes 393224 | tf_op jit(solution)/shard_map/ppermute | solution.py:38
  49.2 10.5 %collective-permute-start.17 = (f32[128,256]{1,0:T(8,128)S(1)}, f32[128,256]{1,0:T(8,128)S(1)}, u32[]{:S(2)}, u32[]{:S(2)}) collective-permute-start(f32[128,256]{1,0:T(8,128)S(1)} %get-tuple-element.93), channel_id=1, source_target_pairs={{0,7},{1,6},{2,5},{3,4},{4,11},{5,10},{6,9},{7,8},{8,15},{9,14},{1... | collective-permute-start | bytes 393224 | tf_op jit(solution)/shard_map/ppermute | solution.py:38
  51.7 9.3 %collective-permute-start.18 = (f32[128,256]{1,0:T(8,128)S(1)}, f32[128,256]{1,0:T(8,128)S(1)}, u32[]{:S(2)}, u32[]{:S(2)}) collective-permute-start(f32[128,256]{1,0:T(8,128)S(1)} %get-tuple-element.94), channel_id=1, source_target_pairs={{0,6},{1,7},{2,4},{3,5},{4,10},{5,11},{6,8},{7,9},{8,14},{9,15},{1... | collective-permute-start | bytes 393224 | tf_op jit(solution)/shard_map/ppermute | solution.py:38
  53.3 8.8 %collective-permute-start.19 = (f32[128,256]{1,0:T(8,128)S(1)}, f32[128,256]{1,0:T(8,128)S(1)}, u32[]{:S(2)}, u32[]{:S(2)}) collective-permute-start(f32[128,256]{1,0:T(8,128)S(1)} %get-tuple-element.95), channel_id=1, source_target_pairs={{0,5},{1,4},{2,7},{3,6},{4,9},{5,8},{6,11},{7,10},{8,13},{9,12},{1... | collective-permute-start | bytes 393224 | tf_op jit(solution)/shard_map/ppermute | solution.py:38
  54.5 7.6 %collective-permute-start.20 = (f32[128,256]{1,0:T(8,128)S(1)}, f32[128,256]{1,0:T(8,128)S(1)}, u32[]{:S(2)}, u32[]{:S(2)}) collective-permute-start(f32[128,256]{1,0:T(8,128)S(1)} %get-tuple-element.96), channel_id=1, source_target_pairs={{0,4},{1,5},{2,6},{3,7},{4,8},{5,9},{6,10},{7,11},{8,12},{9,13},{1... | collective-permute-start | bytes 393224 | tf_op jit(solution)/shard_map/ppermute | solution.py:38
  55.3 9.7 %collective-permute-start.37 = (f32[128,256]{1,0:T(8,128)S(1)}, f32[128,256]{1,0:T(8,128)S(1)}, u32[]{:S(2)}, u32[]{:S(2)}) collective-permute-start(f32[128,256]{1,0:T(8,128)S(1)} %add_add_fusion.3.refs_3_), channel_id=1, source_target_pairs={{0,3},{1,2},{2,1},{3,0},{4,7},{5,6},{6,5},{7,4},{8,11},{9,10},{10,... | collective-permute-start | bytes 393224 | tf_op jit(solution)/shard_map/ppermute | solution.py:38
  59.6 6.5 %collective-permute-start.36 = (f32[128,256]{1,0:T(8,128)S(1)}, f32[128,256]{1,0:T(8,128)S(1)}, u32[]{:S(2)}, u32[]{:S(2)}) collective-permute-start(f32[128,256]{1,0:T(8,128)S(1)} %add_add_fusion.3.refs_3_), channel_id=1, source_target_pairs={{0,2},{1,3},{2,0},{3,1},{4,6},{5,7},{6,4},{7,5},{8,10},{9,11},{10,... | collective-permute-start | bytes 393224 | tf_op jit(solution)/shard_map/ppermute | solution.py:38
  61.1 5.4 %collective-permute-start.35 = (f32[128,256]{1,0:T(8,128)S(1)}, f32[128,256]{1,0:T(8,128)S(1)}, u32[]{:S(2)}, u32[]{:S(2)}) collective-permute-start(f32[128,256]{1,0:T(8,128)S(1)} %add_add_fusion.3.refs_3_), channel_id=1, source_target_pairs={{0,1},{1,0},{2,3},{3,2},{4,5},{5,4},{6,7},{7,6},{8,9},{9,8},{10,11... | collective-permute-start | bytes 393224 | tf_op jit(solution)/shard_map/ppermute | solution.py:38
  62.2 10.2 %collective-permute-start.30 = (f32[128,256]{1,0:T(8,128)S(1)}, f32[128,256]{1,0:T(8,128)S(1)}, u32[]{:S(2)}, u32[]{:S(2)}) collective-permute-start(f32[128,256]{1,0:T(8,128)S(1)} %add_add_fusion.2.refs_3_), channel_id=1, source_target_pairs={{0,3},{1,2},{2,1},{3,0},{4,7},{5,6},{6,5},{7,4},{8,11},{9,10},{10,... | collective-permute-start | bytes 393224 | tf_op jit(solution)/shard_map/ppermute | solution.py:38
  65.0 7.7 %collective-permute-start.29 = (f32[128,256]{1,0:T(8,128)S(1)}, f32[128,256]{1,0:T(8,128)S(1)}, u32[]{:S(2)}, u32[]{:S(2)}) collective-permute-start(f32[128,256]{1,0:T(8,128)S(1)} %add_add_fusion.2.refs_3_), channel_id=1, source_target_pairs={{0,2},{1,3},{2,0},{3,1},{4,6},{5,7},{6,4},{7,5},{8,10},{9,11},{10,... | collective-permute-start | bytes 393224 | tf_op jit(solution)/shard_map/ppermute | solution.py:38
  65.0 9.2 %collective-permute-start.28 = (f32[128,256]{1,0:T(8,128)S(1)}, f32[128,256]{1,0:T(8,128)S(1)}, u32[]{:S(2)}, u32[]{:S(2)}) collective-permute-start(f32[128,256]{1,0:T(8,128)S(1)} %add_add_fusion.2.refs_3_), channel_id=1, source_target_pairs={{0,1},{1,0},{2,3},{3,2},{4,5},{5,4},{6,7},{7,6},{8,9},{9,8},{10,11... | collective-permute-start | bytes 393224 | tf_op jit(solution)/shard_map/ppermute | solution.py:38
  68.9 8.8 %collective-permute-start.38 = (f32[128,256]{1,0:T(8,128)S(1)}, f32[128,256]{1,0:T(8,128)S(1)}, u32[]{:S(2)}, u32[]{:S(2)}) collective-permute-start(f32[128,256]{1,0:T(8,128)S(1)} %get-tuple-element.120), channel_id=1, source_target_pairs={{0,7},{1,6},{2,5},{3,4},{4,11},{5,10},{6,9},{7,8},{8,15},{9,14},{1... | collective-permute-start | bytes 393224 | tf_op jit(solution)/shard_map/ppermute | solution.py:38
  69.6 10.3 %collective-permute-start.39 = (f32[128,256]{1,0:T(8,128)S(1)}, f32[128,256]{1,0:T(8,128)S(1)}, u32[]{:S(2)}, u32[]{:S(2)}) collective-permute-start(f32[128,256]{1,0:T(8,128)S(1)} %get-tuple-element.121), channel_id=1, source_target_pairs={{0,6},{1,7},{2,4},{3,5},{4,10},{5,11},{6,8},{7,9},{8,14},{9,15},{1... | collective-permute-start | bytes 393224 | tf_op jit(solution)/shard_map/ppermute | solution.py:38
  72.4 8.1 %collective-permute-start.40 = (f32[128,256]{1,0:T(8,128)S(1)}, f32[128,256]{1,0:T(8,128)S(1)}, u32[]{:S(2)}, u32[]{:S(2)}) collective-permute-start(f32[128,256]{1,0:T(8,128)S(1)} %get-tuple-element.122), channel_id=1, source_target_pairs={{0,5},{1,4},{2,7},{3,6},{4,9},{5,8},{6,11},{7,10},{8,13},{9,12},{1... | collective-permute-start | bytes 393224 | tf_op jit(solution)/shard_map/ppermute | solution.py:38
  72.6 8.5 %collective-permute-start.41 = (f32[128,256]{1,0:T(8,128)S(1)}, f32[128,256]{1,0:T(8,128)S(1)}, u32[]{:S(2)}, u32[]{:S(2)}) collective-permute-start(f32[128,256]{1,0:T(8,128)S(1)} %get-tuple-element.123), channel_id=1, source_target_pairs={{0,4},{1,5},{2,6},{3,7},{4,8},{5,9},{6,10},{7,11},{8,12},{9,13},{1... | collective-permute-start | bytes 393224 | tf_op jit(solution)/shard_map/ppermute | solution.py:38
  76.6 9.5 %collective-permute-start.31 = (f32[128,256]{1,0:T(8,128)S(1)}, f32[128,256]{1,0:T(8,128)S(1)}, u32[]{:S(2)}, u32[]{:S(2)}) collective-permute-start(f32[128,256]{1,0:T(8,128)S(1)} %get-tuple-element.115), channel_id=1, source_target_pairs={{0,7},{1,6},{2,5},{3,4},{4,11},{5,10},{6,9},{7,8},{8,15},{9,14},{1... | collective-permute-start | bytes 393224 | tf_op jit(solution)/shard_map/ppermute | solution.py:38
  77.7 8.5 %collective-permute-start.32 = (f32[128,256]{1,0:T(8,128)S(1)}, f32[128,256]{1,0:T(8,128)S(1)}, u32[]{:S(2)}, u32[]{:S(2)}) collective-permute-start(f32[128,256]{1,0:T(8,128)S(1)} %get-tuple-element.116), channel_id=1, source_target_pairs={{0,6},{1,7},{2,4},{3,5},{4,10},{5,11},{6,8},{7,9},{8,14},{9,15},{1... | collective-permute-start | bytes 393224 | tf_op jit(solution)/shard_map/ppermute | solution.py:38
  79.9 7.1 %collective-permute-start.33 = (f32[128,256]{1,0:T(8,128)S(1)}, f32[128,256]{1,0:T(8,128)S(1)}, u32[]{:S(2)}, u32[]{:S(2)}) collective-permute-start(f32[128,256]{1,0:T(8,128)S(1)} %get-tuple-element.117), channel_id=1, source_target_pairs={{0,5},{1,4},{2,7},{3,6},{4,9},{5,8},{6,11},{7,10},{8,13},{9,12},{1... | collective-permute-start | bytes 393224 | tf_op jit(solution)/shard_map/ppermute | solution.py:38
  80.5 7.3 %collective-permute-start.34 = (f32[128,256]{1,0:T(8,128)S(1)}, f32[128,256]{1,0:T(8,128)S(1)}, u32[]{:S(2)}, u32[]{:S(2)}) collective-permute-start(f32[128,256]{1,0:T(8,128)S(1)} %get-tuple-element.118), channel_id=1, source_target_pairs={{0,4},{1,5},{2,6},{3,7},{4,8},{5,9},{6,10},{7,11},{8,12},{9,13},{1... | collective-permute-start | bytes 393224 | tf_op jit(solution)/shard_map/ppermute | solution.py:38

commit v3 on v2

--- a/solution.py
+++ b/solution.py
@@ -36,6 +36,14 @@
         for u in range(nu)
     ]
     return lax.ppermute(x, ("blk", "user"), route)
+
+
+def sum_order(nu):
+    return [nu - 1, *range(1, nu - 1), 0]
+
+
+def gather_order(nu):
+    return [*range(1, nu), 0]
 
 
 def split(x):
@@ -123,7 +131,7 @@
 
 def item_kernel(sh, nu, row, *refs):
     list_ref, users, ratings = refs[:3]
-    items = refs[3 : 3 + nu]
+    items = dict(zip(gather_order(nu), refs[3 : 3 + nu]))
     terms = refs[3 + nu : 3 + 2 * nu]
     residuals, item_parts, grads, item_turned = refs[3 + 2 * nu :]
     block = sh.block
@@ -274,7 +282,7 @@
             bytes_accessed=8 * sh.total * sh.block * sh.block // sh.chunks,
             transcendentals=0,
         ),
-    )(in_smem(lists), *[in_vmem(x) for x in (users, ratings, *items)])
+    )(in_smem(lists), *[in_vmem(x) for x in (users, ratings, *[items[r] for r in gather_order(nu)])])
     return outs[:nu], outs[nu], outs[nu + 1]
 
 
@@ -331,7 +339,7 @@
             )
             residuals.append(residual)
             item_parts.append(parts)
-            sent.append([moved(terms[r], 1, r, nb, nu) for r in reversed(range(nu))])
+            sent.append([moved(terms[r], 1, r, nb, nu) for r in sum_order(nu)])
         own = [functools.reduce(jnp.add, x) for x in sent[:-1]]
         own, residuals = lax.optimization_barrier((own, residuals))
         users, step_ratings = new_users(

time: 89.2 us -> 89.2 us (level)
  waiting for transfers between devices: 6.4 us -> 10.7 us
  starting transfers between devices: 51.7 us -> 48.9 us
  Pallas kernels: 27.7 us -> 26.4 us
    ppermute x42, waiting for transfers between devices: 6.4 us -> 10.7 us  [moved(): return lax.ppermute(x, ('blk', 'user'), route)]
    ppermute x42, starting transfers between devices: 51.7 us -> 48.9 us  [moved(): return lax.ppermute(x, ('blk', 'user'), route)]
  transfers between devices with their start and end apart: 42 -> 42, of which waited for: 15 -> 13; matrix products, arithmetic and copies ran while one was open for 0% -> 0% of each run, Pallas kernels for 31% -> 30%
where the time goes in v3:
time: 89.2 us; the launch traced here: 88.8 us
  starting transfers between devices  48.9 us (55%)
  Pallas kernels  26.4 us (30%)
  waiting for transfers between devices  10.7 us (12%)
  local copies, waits for them, and re-layouts  0.99 us (1%)
  other arithmetic  0.92 us (1%)
    ppermute x42, starting transfers between devices, moved(): return lax.ppermute(x, ('blk', 'user'), route)  48.9 us
    pallas_call x6, Pallas kernels, item_terms(): pl.pallas_call(functools.partial(item_kernel, sh, nu, row), out_shape=[pl...  12.3 us
    ppermute x42, waiting for transfers between devices, moved(): return lax.ppermute(x, ('blk', 'user'), route)  10.7 us
    pallas_call x3, Pallas kernels, new_users(): pl.pallas_call(functools.partial(user_kernel, sh, step), out_shape=out_sh...  9.75 us
    pallas_call x1, Pallas kernels, load(): pl.pallas_call(functools.partial(load_kernel, sh), out_shape=[pltpu.VMEM(...  4.39 us
  transfers between devices with their start and end apart: 42, of which 13 were waited for; matrix products, arithmetic and copies ran while one was open for 0% of the time, Pallas kernels for 30%

profile of v3, /device:TPU:0, one launch (start us, length us, event | category | flops | bytes accessed | tf_op | source)
XLA Modules:
  0.0 88.8 jit_solution(18057888714706894744)
XLA Ops:
  0.6 1.0 %fusion = (f32[128,256]{1,0:T(8,128)S(1)}, f32[128,256]{1,0:T(8,128)S(1)}) fusion(f32[256,256]{1,0:T(8,128)} %param.6), kind=kLoop, calls=%fused_computation.7 | loop fusion | bytes 524288 | tf_op jit(solution)/shard_map/slice | solution.py:331
  1.6 4.0 %collective-permute-start.9 = (f32[128,256]{1,0:T(8,128)S(1)}, f32[128,256]{1,0:T(8,128)S(1)}, u32[]{:S(2)}, u32[]{:S(2)}) collective-permute-start(f32[128,256]{1,0:T(8,128)S(1)} %get-tuple-element.136.refs_6_), channel_id=1, source_target_pairs={{0,3},{1,2},{2,1},{3,0},{4,7},{5,6},{6,5},{7,4},{8,11},{9,10},{10,... | collective-permute-start | bytes 393224 | tf_op jit(solution)/shard_map/ppermute | solution.py:38
  5.6 0.5 collective-permute-start.8
  6.1 0.1 collective-permute-start.7
  6.2 2.8 %collective-permute-start.2 = (f32[128,256]{1,0:T(8,128)S(1)}, f32[128,256]{1,0:T(8,128)S(1)}, u32[]{:S(2)}, u32[]{:S(2)}) collective-permute-start(f32[128,256]{1,0:T(8,128)S(1)} %get-tuple-element.137.refs_6_), channel_id=1, source_target_pairs={{0,3},{1,2},{2,1},{3,0},{4,7},{5,6},{6,5},{7,4},{8,11},{9,10},{10,... | collective-permute-start | bytes 393224 | tf_op jit(solution)/shard_map/ppermute | solution.py:38
  9.1 0.5 collective-permute-start.1
  9.6 4.4 %shard_map.68 = (f32[32,128,256]{2,1,0:T(8,128)S(1)}, s32[64,128,128]{2,1,0:T(8,128)S(1)}, s32[6,65]{1,0:T(8,128)S(4)}) custom-call(s32[3,2,4,8]{3,2,1,0:T(4,128)} %bitcast.10, s32[3,2,8]{2,1,0:T(2,128)} %bitcast.11, f32[32,128,256]{2,1,0:T(8,128)} %bitcast.8, s32[192,128,128]{2,1,0:T(8,128)} %bitcast.5), custom_call_target="tpu_custom_call" | custom-call | tf_op jit(solution)/shard_map/pallas_call | solution.py:248
  14.0 0.2 collective-permute-start
  14.2 0.6 collective-permute-done.8.refs_4_
  14.8 1.6 %shard_map.70 = (f32[128,256]{1,0:T(8,128)S(1)}, f32[128,256]{1,0:T(8,128)S(1)}, f32[128,256]{1,0:T(8,128)S(1)}, f32[128,256]{1,0:T(8,128)S(1)}, bf16[64,256,128...) custom-call(s32[6,65]{1,0:T(8,128)S(4)} %get-tuple-element.69.refs_0_, ...), custom_call_target="tpu_custom_call" | custom-call | flops 1073741824 | bytes 4194304 | tf_op jit(solution)/shard_map/pallas_call | solution.py:266
  16.5 0.6 collective-permute-start.10
  17.0 3.2 %collective-permute-start.11 = (f32[128,256]{1,0:T(8,128)S(1)}, f32[128,256]{1,0:T(8,128)S(1)}, u32[]{:S(2)}, u32[]{:S(2)}) collective-permute-start(f32[128,256]{1,0:T(8,128)S(1)} %get-tuple-element.77), channel_id=1, source_target_pairs={{0,5},{1,4},{2,7},{3,6},{4,9},{5,8},{6,11},{7,10},{8,13},{9,12},{1... | collective-permute-start | bytes 393224 | tf_op jit(solution)/shard_map/ppermute | solution.py:38
  20.3 0.1 collective-permute-start.12
  20.4 0.7 collective-permute-start.13
  21.1 3.0 %shard_map.69 = (f32[128,256]{1,0:T(8,128)S(1)}, f32[128,256]{1,0:T(8,128)S(1)}, f32[128,256]{1,0:T(8,128)S(1)}, f32[128,256]{1,0:T(8,128)S(1)}, bf16[64,256,128...) custom-call(s32[6,65]{1,0:T(8,128)S(4)} %get-tuple-element.69.refs_0_, ...), custom_call_target="tpu_custom_call" | custom-call | flops 1073741824 | bytes 4194304 | tf_op jit(solution)/shard_map/pallas_call | solution.py:266
  24.1 2.4 %collective-permute-start.3 = (f32[128,256]{1,0:T(8,128)S(1)}, f32[128,256]{1,0:T(8,128)S(1)}, u32[]{:S(2)}, u32[]{:S(2)}) collective-permute-start(f32[128,256]{1,0:T(8,128)S(1)} %get-tuple-element.72), channel_id=1, source_target_pairs={{0,7},{1,6},{2,5},{3,4},{4,11},{5,10},{6,9},{7,8},{8,15},{9,14},{1... | collective-permute-start | bytes 393224 | tf_op jit(solution)/shard_map/ppermute | solution.py:38
  26.5 0.9 collective-permute-start.4
  27.4 0.6 collective-permute-start.5
  28.0 0.4 collective-permute-start.6
  28.4 1.0 %collective-permute-done.13 = f32[128,256]{1,0:T(8,128)S(1)} collective-permute-done((f32[128,256]{1,0:T(8,128)S(1)}, f32[128,256]{1,0:T(8,128)S(1)}, u32[]{:S(2)}, u32[]{:S(2)}) %collective-permute-start.13) | collective-permute-done | bytes 131104 | tf_op jit(solution)/shard_map/ppermute | solution.py:38
  29.4 1.8 %collective-permute-start.23 = (f32[128,256]{1,0:T(8,128)S(1)}, f32[128,256]{1,0:T(8,128)S(1)}, u32[]{:S(2)}, u32[]{:S(2)}) collective-permute-start(f32[128,256]{1,0:T(8,128)S(1)} %add_add_fusion.5.refs_6_), channel_id=1, source_target_pairs={{0,3},{1,2},{2,1},{3,0},{4,7},{5,6},{6,5},{7,4},{8,11},{9,10},{10,... | collective-permute-start | bytes 393224 | tf_op jit(solution)/shard_map/ppermute | solution.py:38
  31.3 2.8 %shard_map.71 = (f32[32,128,256]{2,1,0:T(8,128)S(1)}, s32[64,128,128]{2,1,0:T(8,128)S(1)}) custom-call(s32[6,65]{1,0:T(8,128)S(4)} %get-tuple-element.69.refs_0_, f32[32,128,256]{2,1,0:T(8,128)S(1)} %get-tuple-element.70.refs_1_, bf16[64,256,128]{2,1,0:T(8,128)(2,1)S(1)} %get-tuple-element.82.refs_2_, bf16[64,256,128]{2,1,0:T(8,128)(2,1)S(1)} %get-tuple-element.83.refs_3_, ...), custom_call_target="tpu_custom_call" | custom-call | flops 2147483648 | bytes 16777216 | tf_op jit(solution)/shard_map/pallas_call | solution.py:305
  34.1 0.1 collective-permute-start.22
  34.2 1.5 %collective-permute-start.21 = (f32[128,256]{1,0:T(8,128)S(1)}, f32[128,256]{1,0:T(8,128)S(1)}, u32[]{:S(2)}, u32[]{:S(2)}) collective-permute-start(f32[128,256]{1,0:T(8,128)S(1)} %add_add_fusion.5.refs_6_), channel_id=1, source_target_pairs={{0,1},{1,0},{2,3},{3,2},{4,5},{5,4},{6,7},{7,6},{8,9},{9,8},{10,11... | collective-permute-start | bytes 393224 | tf_op jit(solution)/shard_map/ppermute | solution.py:38
  35.7 0.1 collective-permute-done.5
  35.8 0.8 collective-permute-done.6
  36.7 1.4 %collective-permute-start.16 = (f32[128,256]{1,0:T(8,128)S(1)}, f32[128,256]{1,0:T(8,128)S(1)}, u32[]{:S(2)}, u32[]{:S(2)}) collective-permute-start(f32[128,256]{1,0:T(8,128)S(1)} %add_add_fusion.4.refs_6_), channel_id=1, source_target_pairs={{0,3},{1,2},{2,1},{3,0},{4,7},{5,6},{6,5},{7,4},{8,11},{9,10},{10,... | collective-permute-start | bytes 393224 | tf_op jit(solution)/shard_map/ppermute | solution.py:38
  38.1 0.6 collective-permute-start.15
  38.7 1.6 %collective-permute-start.14 = (f32[128,256]{1,0:T(8,128)S(1)}, f32[128,256]{1,0:T(8,128)S(1)}, u32[]{:S(2)}, u32[]{:S(2)}) collective-permute-start(f32[128,256]{1,0:T(8,128)S(1)} %add_add_fusion.4.refs_6_), channel_id=1, source_target_pairs={{0,1},{1,0},{2,3},{3,2},{4,5},{5,4},{6,7},{7,6},{8,9},{9,8},{10,11... | collective-permute-start | bytes 393224 | tf_op jit(solution)/shard_map/ppermute | solution.py:38
  40.3 1.7 %collective-permute-done.22.refs_4_ = f32[128,256]{1,0:T(8,128)S(1)} collective-permute-done((f32[128,256]{1,0:T(8,128)S(1)}, f32[128,256]{1,0:T(8,128)S(1)}, u32[]{:S(2)}, u32[]{:S(2)}) %collective-permute-start.22) | collective-permute-done | bytes 131104 | tf_op jit(solution)/shard_map/ppermute | solution.py:38
  41.9 1.9 %shard_map.73 = (f32[128,256]{1,0:T(8,128)S(1)}, f32[128,256]{1,0:T(8,128)S(1)}, f32[128,256]{1,0:T(8,128)S(1)}, f32[128,256]{1,0:T(8,128)S(1)}, bf16[64,256,128...) custom-call(s32[6,65]{1,0:T(8,128)S(4)} %get-tuple-element.69.refs_0_, ...), custom_call_target="tpu_custom_call" | custom-call | flops 1073741824 | bytes 4194304 | tf_op jit(solution)/shard_map/pallas_call | solution.py:266
  43.8 0.1 collective-permute-start.24
  43.9 2.8 %collective-permute-start.25 = (f32[128,256]{1,0:T(8,128)S(1)}, f32[128,256]{1,0:T(8,128)S(1)}, u32[]{:S(2)}, u32[]{:S(2)}) collective-permute-start(f32[128,256]{1,0:T(8,128)S(1)} %get-tuple-element.99), channel_id=1, source_target_pairs={{0,5},{1,4},{2,7},{3,6},{4,9},{5,8},{6,11},{7,10},{8,13},{9,12},{1... | collective-permute-start | bytes 393224 | tf_op jit(solution)/shard_map/ppermute | solution.py:38
  46.8 0.4 collective-permute-start.27
  47.2 1.6 %shard_map.72 = (f32[128,256]{1,0:T(8,128)S(1)}, f32[128,256]{1,0:T(8,128)S(1)}, f32[128,256]{1,0:T(8,128)S(1)}, f32[128,256]{1,0:T(8,128)S(1)}, bf16[64,256,128...) custom-call(s32[6,65]{1,0:T(8,128)S(4)} %get-tuple-element.69.refs_0_, ...), custom_call_target="tpu_custom_call" | custom-call | flops 1073741824 | bytes 4194304 | tf_op jit(solution)/shard_map/pallas_call | solution.py:266
  48.8 1.9 %collective-permute-start.17 = (f32[128,256]{1,0:T(8,128)S(1)}, f32[128,256]{1,0:T(8,128)S(1)}, u32[]{:S(2)}, u32[]{:S(2)}) collective-permute-start(f32[128,256]{1,0:T(8,128)S(1)} %get-tuple-element.93), channel_id=1, source_target_pairs={{0,7},{1,6},{2,5},{3,4},{4,11},{5,10},{6,9},{7,8},{8,15},{9,14},{1... | collective-permute-start | bytes 393224 | tf_op jit(solution)/shard_map/ppermute | solution.py:38
  50.7 1.4 %collective-permute-done.24 = f32[128,256]{1,0:T(8,128)S(1)} collective-permute-done((f32[128,256]{1,0:T(8,128)S(1)}, f32[128,256]{1,0:T(8,128)S(1)}, u32[]{:S(2)}, u32[]{:S(2)}) %collective-permute-start.24) | collective-permute-done | bytes 131104 | tf_op jit(solution)/shard_map/ppermute | solution.py:38
  52.1 0.6 collective-permute-done.25
  52.6 2.3 %collective-permute-start.19 = (f32[128,256]{1,0:T(8,128)S(1)}, f32[128,256]{1,0:T(8,128)S(1)}, u32[]{:S(2)}, u32[]{:S(2)}) collective-permute-start(f32[128,256]{1,0:T(8,128)S(1)} %get-tuple-element.95), channel_id=1, source_target_pairs={{0,6},{1,7},{2,4},{3,5},{4,10},{5,11},{6,8},{7,9},{8,14},{9,15},{1... | collective-permute-start | bytes 393224 | tf_op jit(solution)/shard_map/ppermute | solution.py:38
  55.0 0.0 collective-permute-start.20
  55.0 1.8 %collective-permute-start.37 = (f32[128,256]{1,0:T(8,128)S(1)}, f32[128,256]{1,0:T(8,128)S(1)}, u32[]{:S(2)}, u32[]{:S(2)}) collective-permute-start(f32[128,256]{1,0:T(8,128)S(1)} %add_add_fusion.3.refs_6_), channel_id=1, source_target_pairs={{0,3},{1,2},{2,1},{3,0},{4,7},{5,6},{6,5},{7,4},{8,11},{9,10},{10,... | collective-permute-start | bytes 393224 | tf_op jit(solution)/shard_map/ppermute | solution.py:38
  56.8 2.4 %shard_map.74 = (f32[32,128,256]{2,1,0:T(8,128)S(1)}, s32[64,128,128]{2,1,0:T(8,128)S(1)}) custom-call(s32[6,65]{1,0:T(8,128)S(4)} %get-tuple-element.69.refs_0_, f32[32,128,256]{2,1,0:T(8,128)S(1)} %get-tuple-element.87.refs_1_, bf16[64,256,128]{2,1,0:T(8,128)(2,1)S(1)} %get-tuple-element.104.refs_2_, bf16[64,256,128]{2,1,0:T(8,128)(2,1)S(1)} %get-tuple-element.105.refs_3_, ...), custom_call_target="tpu_custom_call" | custom-call | flops 2147483648 | bytes 16777216 | tf_op jit(solution)/shard_map/pallas_call | solution.py:305
  59.2 1.7 %collective-permute-start.36 = (f32[128,256]{1,0:T(8,128)S(1)}, f32[128,256]{1,0:T(8,128)S(1)}, u32[]{:S(2)}, u32[]{:S(2)}) collective-permute-start(f32[128,256]{1,0:T(8,128)S(1)} %add_add_fusion.3.refs_6_), channel_id=1, source_target_pairs={{0,2},{1,3},{2,0},{3,1},{4,6},{5,7},{6,4},{7,5},{8,10},{9,11},{10,... | collective-permute-start | bytes 393224 | tf_op jit(solution)/shard_map/ppermute | solution.py:38
  60.9 0.8 collective-permute-start.35
  61.7 0.2 collective-permute-done.19
  61.9 2.4 %collective-permute-start.30 = (f32[128,256]{1,0:T(8,128)S(1)}, f32[128,256]{1,0:T(8,128)S(1)}, u32[]{:S(2)}, u32[]{:S(2)}) collective-permute-start(f32[128,256]{1,0:T(8,128)S(1)} %add_add_fusion.2.refs_6_), channel_id=1, source_target_pairs={{0,3},{1,2},{2,1},{3,0},{4,7},{5,6},{6,5},{7,4},{8,11},{9,10},{10,... | collective-permute-start | bytes 393224 | tf_op jit(solution)/shard_map/ppermute | solution.py:38
  64.3 0.7 collective-permute-start.29
  65.0 0.5 collective-permute-start.28
  65.5 0.6 collective-permute-done.36.refs_4_
  66.1 1.6 %shard_map.76 = (f32[128,256]{1,0:T(8,128)S(1)}, f32[128,256]{1,0:T(8,128)S(1)}, f32[128,256]{1,0:T(8,128)S(1)}, f32[128,256]{1,0:T(8,128)S(1)}, bf16[64,256,128...) custom-call(s32[6,65]{1,0:T(8,128)S(4)} %get-tuple-element.69.refs_0_, ...), custom_call_target="tpu_custom_call" | custom-call | flops 1073741824 | bytes 4194304 | tf_op jit(solution)/shard_map/pallas_call | solution.py:266
  67.8 2.4 %collective-permute-start.38 = (f32[128,256]{1,0:T(8,128)S(1)}, f32[128,256]{1,0:T(8,128)S(1)}, u32[]{:S(2)}, u32[]{:S(2)}) collective-permute-start(f32[128,256]{1,0:T(8,128)S(1)} %get-tuple-element.120), channel_id=1, source_target_pairs={{0,7},{1,6},{2,5},{3,4},{4,11},{5,10},{6,9},{7,8},{8,15},{9,14},{1... | collective-permute-start | bytes 393224 | tf_op jit(solution)/shard_map/ppermute | solution.py:38
  70.2 1.4 %collective-permute-start.39 = (f32[128,256]{1,0:T(8,128)S(1)}, f32[128,256]{1,0:T(8,128)S(1)}, u32[]{:S(2)}, u32[]{:S(2)}) collective-permute-start(f32[128,256]{1,0:T(8,128)S(1)} %get-tuple-element.121), channel_id=1, source_target_pairs={{0,5},{1,4},{2,7},{3,6},{4,9},{5,8},{6,11},{7,10},{8,13},{9,12},{1... | collective-permute-start | bytes 393224 | tf_op jit(solution)/shard_map/ppermute | solution.py:38
  71.6 0.3 collective-permute-start.40
  71.8 0.3 collective-permute-done.29.refs_4_
  72.1 1.2 %collective-permute-start.41 = (f32[128,256]{1,0:T(8,128)S(1)}, f32[128,256]{1,0:T(8,128)S(1)}, u32[]{:S(2)}, u32[]{:S(2)}) collective-permute-start(f32[128,256]{1,0:T(8,128)S(1)} %get-tuple-element.123), channel_id=1, source_target_pairs={{0,4},{1,5},{2,6},{3,7},{4,8},{5,9},{6,10},{7,11},{8,12},{9,13},{1... | collective-permute-start | bytes 393224 | tf_op jit(solution)/shard_map/ppermute | solution.py:38
  73.3 2.4 %shard_map.75 = (f32[128,256]{1,0:T(8,128)S(1)}, f32[128,256]{1,0:T(8,128)S(1)}, f32[128,256]{1,0:T(8,128)S(1)}, f32[128,256]{1,0:T(8,128)S(1)}, bf16[64,256,128...) custom-call(s32[6,65]{1,0:T(8,128)S(4)} %get-tuple-element.69.refs_0_, ...), custom_call_target="tpu_custom_call" | custom-call | flops 1073741824 | bytes 4194304 | tf_op jit(solution)/shard_map/pallas_call | solution.py:266
  75.8 2.4 %collective-permute-start.31 = (f32[128,256]{1,0:T(8,128)S(1)}, f32[128,256]{1,0:T(8,128)S(1)}, u32[]{:S(2)}, u32[]{:S(2)}) collective-permute-start(f32[128,256]{1,0:T(8,128)S(1)} %get-tuple-element.115), channel_id=1, source_target_pairs={{0,7},{1,6},{2,5},{3,4},{4,11},{5,10},{6,9},{7,8},{8,15},{9,14},{1... | collective-permute-start | bytes 393224 | tf_op jit(solution)/shard_map/ppermute | solution.py:38
  78.2 0.6 collective-permute-start.32
  78.7 1.4 %collective-permute-start.33 = (f32[128,256]{1,0:T(8,128)S(1)}, f32[128,256]{1,0:T(8,128)S(1)}, u32[]{:S(2)}, u32[]{:S(2)}) collective-permute-start(f32[128,256]{1,0:T(8,128)S(1)} %get-tuple-element.117), channel_id=1, source_target_pairs={{0,6},{1,7},{2,4},{3,5},{4,10},{5,11},{6,8},{7,9},{8,14},{9,15},{1... | collective-permute-start | bytes 393224 | tf_op jit(solution)/shard_map/ppermute | solution.py:38
  80.1 1.2 %collective-permute-done.41 = f32[128,256]{1,0:T(8,128)S(1)} collective-permute-done((f32[128,256]{1,0:T(8,128)S(1)}, f32[128,256]{1,0:T(8,128)S(1)}, u32[]{:S(2)}, u32[]{:S(2)}) %collective-permute-start.41) | collective-permute-done | bytes 131104 | tf_op jit(solution)/shard_map/ppermute | solution.py:38
  81.3 4.5 %shard_map.77 = f32[32,128,256]{2,1,0:T(8,128)} custom-call(s32[6,65]{1,0:T(8,128)S(4)} %get-tuple-element.69.refs_0_, f32[32,128,256]{2,1,0:T(8,128)S(1)} %get-tuple-element.109.refs_1_, bf16[64,256,128]{2,1,0:T(8,128)(2,1)S(1)} %get-tuple-element.126.refs_2_, bf16[64,256,128]{2,1,0:T(8,128)(2,1)S(1)} %get-tuple-element.127.refs_3_, ...), custom_call_target="tpu_custom_call" | custom-call | flops 2147483648 | bytes 16777216 | tf_op jit(solution)/shard_map/pallas_call | solution.py:305
  85.9 2.0 %collective-permute-done.33 = f32[128,256]{1,0:T(8,128)S(1)} collective-permute-done((f32[128,256]{1,0:T(8,128)S(1)}, f32[128,256]{1,0:T(8,128)S(1)}, u32[]{:S(2)}, u32[]{:S(2)}) %collective-permute-start.33) | collective-permute-done | bytes 131104 | tf_op jit(solution)/shard_map/ppermute | solution.py:38
  87.9 0.2 collective-permute-done.34
  88.1 0.7 pad_maximum_fusion
  (38 shorter events, 0.3 us)
Async XLA Ops:
  1.6 12.4 %collective-permute-start.9 = (f32[128,256]{1,0:T(8,128)S(1)}, f32[128,256]{1,0:T(8,128)S(1)}, u32[]{:S(2)}, u32[]{:S(2)}) collective-permute-start(f32[128,256]{1,0:T(8,128)S(1)} %get-tuple-element.136.refs_6_), channel_id=1, source_target_pairs={{0,3},{1,2},{2,1},{3,0},{4,7},{5,6},{6,5},{7,4},{8,11},{9,10},{10,... | collective-permute-start | bytes 393224 | tf_op jit(solution)/shard_map/ppermute | solution.py:38
  5.6 9.2 %collective-permute-start.8 = (f32[128,256]{1,0:T(8,128)S(1)}, f32[128,256]{1,0:T(8,128)S(1)}, u32[]{:S(2)}, u32[]{:S(2)}) collective-permute-start(f32[128,256]{1,0:T(8,128)S(1)} %get-tuple-element.136.refs_6_), channel_id=1, source_target_pairs={{0,2},{1,3},{2,0},{3,1},{4,6},{5,7},{6,4},{7,5},{8,10},{9,11},{10,... | collective-permute-start | bytes 393224 | tf_op jit(solution)/shard_map/ppermute | solution.py:38
  6.1 8.7 %collective-permute-start.7 = (f32[128,256]{1,0:T(8,128)S(1)}, f32[128,256]{1,0:T(8,128)S(1)}, u32[]{:S(2)}, u32[]{:S(2)}) collective-permute-start(f32[128,256]{1,0:T(8,128)S(1)} %get-tuple-element.136.refs_6_), channel_id=1, source_target_pairs={{0,1},{1,0},{2,3},{3,2},{4,5},{5,4},{6,7},{7,6},{8,9},{9,8},{10,11... | collective-permute-start | bytes 393224 | tf_op jit(solution)/shard_map/ppermute | solution.py:38
  6.2 14.1 %collective-permute-start.2 = (f32[128,256]{1,0:T(8,128)S(1)}, f32[128,256]{1,0:T(8,128)S(1)}, u32[]{:S(2)}, u32[]{:S(2)}) collective-permute-start(f32[128,256]{1,0:T(8,128)S(1)} %get-tuple-element.137.refs_6_), channel_id=1, source_target_pairs={{0,3},{1,2},{2,1},{3,0},{4,7},{5,6},{6,5},{7,4},{8,11},{9,10},{10,... | collective-permute-start | bytes 393224 | tf_op jit(solution)/shard_map/ppermute | solution.py:38
  9.1 11.3 %collective-permute-start.1 = (f32[128,256]{1,0:T(8,128)S(1)}, f32[128,256]{1,0:T(8,128)S(1)}, u32[]{:S(2)}, u32[]{:S(2)}) collective-permute-start(f32[128,256]{1,0:T(8,128)S(1)} %get-tuple-element.137.refs_6_), channel_id=1, source_target_pairs={{0,2},{1,3},{2,0},{3,1},{4,6},{5,7},{6,4},{7,5},{8,10},{9,11},{10,... | collective-permute-start | bytes 393224 | tf_op jit(solution)/shard_map/ppermute | solution.py:38
  14.0 7.1 %collective-permute-start = (f32[128,256]{1,0:T(8,128)S(1)}, f32[128,256]{1,0:T(8,128)S(1)}, u32[]{:S(2)}, u32[]{:S(2)}) collective-permute-start(f32[128,256]{1,0:T(8,128)S(1)} %get-tuple-element.137.refs_6_), channel_id=1, source_target_pairs={{0,1},{1,0},{2,3},{3,2},{4,5},{5,4},{6,7},{7,6},{8,9},{9,8},{10,11... | collective-permute-start | bytes 393224 | tf_op jit(solution)/shard_map/ppermute | solution.py:38
  16.5 10.0 %collective-permute-start.10 = (f32[128,256]{1,0:T(8,128)S(1)}, f32[128,256]{1,0:T(8,128)S(1)}, u32[]{:S(2)}, u32[]{:S(2)}) collective-permute-start(f32[128,256]{1,0:T(8,128)S(1)} %get-tuple-element.76), channel_id=1, source_target_pairs={{0,7},{1,6},{2,5},{3,4},{4,11},{5,10},{6,9},{7,8},{8,15},{9,14},{1... | collective-permute-start | bytes 393224 | tf_op jit(solution)/shard_map/ppermute | solution.py:38
  17.0 10.3 %collective-permute-start.11 = (f32[128,256]{1,0:T(8,128)S(1)}, f32[128,256]{1,0:T(8,128)S(1)}, u32[]{:S(2)}, u32[]{:S(2)}) collective-permute-start(f32[128,256]{1,0:T(8,128)S(1)} %get-tuple-element.77), channel_id=1, source_target_pairs={{0,5},{1,4},{2,7},{3,6},{4,9},{5,8},{6,11},{7,10},{8,13},{9,12},{1... | collective-permute-start | bytes 393224 | tf_op jit(solution)/shard_map/ppermute | solution.py:38
  20.3 7.7 %collective-permute-start.12 = (f32[128,256]{1,0:T(8,128)S(1)}, f32[128,256]{1,0:T(8,128)S(1)}, u32[]{:S(2)}, u32[]{:S(2)}) collective-permute-start(f32[128,256]{1,0:T(8,128)S(1)} %get-tuple-element.78), channel_id=1, source_target_pairs={{0,6},{1,7},{2,4},{3,5},{4,10},{5,11},{6,8},{7,9},{8,14},{9,15},{1... | collective-permute-start | bytes 393224 | tf_op jit(solution)/shard_map/ppermute | solution.py:38
  20.4 9.0 %collective-permute-start.13 = (f32[128,256]{1,0:T(8,128)S(1)}, f32[128,256]{1,0:T(8,128)S(1)}, u32[]{:S(2)}, u32[]{:S(2)}) collective-permute-start(f32[128,256]{1,0:T(8,128)S(1)} %get-tuple-element.79), channel_id=1, source_target_pairs={{0,4},{1,5},{2,6},{3,7},{4,8},{5,9},{6,10},{7,11},{8,12},{9,13},{1... | collective-permute-start | bytes 393224 | tf_op jit(solution)/shard_map/ppermute | solution.py:38
  24.1 10.0 %collective-permute-start.3 = (f32[128,256]{1,0:T(8,128)S(1)}, f32[128,256]{1,0:T(8,128)S(1)}, u32[]{:S(2)}, u32[]{:S(2)}) collective-permute-start(f32[128,256]{1,0:T(8,128)S(1)} %get-tuple-element.72), channel_id=1, source_target_pairs={{0,7},{1,6},{2,5},{3,4},{4,11},{5,10},{6,9},{7,8},{8,15},{9,14},{1... | collective-permute-start | bytes 393224 | tf_op jit(solution)/shard_map/ppermute | solution.py:38
  26.5 7.7 %collective-permute-start.4 = (f32[128,256]{1,0:T(8,128)S(1)}, f32[128,256]{1,0:T(8,128)S(1)}, u32[]{:S(2)}, u32[]{:S(2)}) collective-permute-start(f32[128,256]{1,0:T(8,128)S(1)} %get-tuple-element.73), channel_id=1, source_target_pairs={{0,5},{1,4},{2,7},{3,6},{4,9},{5,8},{6,11},{7,10},{8,13},{9,12},{1... | collective-permute-start | bytes 393224 | tf_op jit(solution)/shard_map/ppermute | solution.py:38
  27.4 8.5 %collective-permute-start.5 = (f32[128,256]{1,0:T(8,128)S(1)}, f32[128,256]{1,0:T(8,128)S(1)}, u32[]{:S(2)}, u32[]{:S(2)}) collective-permute-start(f32[128,256]{1,0:T(8,128)S(1)} %get-tuple-element.74), channel_id=1, source_target_pairs={{0,6},{1,7},{2,4},{3,5},{4,10},{5,11},{6,8},{7,9},{8,14},{9,15},{1... | collective-permute-start | bytes 393224 | tf_op jit(solution)/shard_map/ppermute | solution.py:38
  28.0 8.7 %collective-permute-start.6 = (f32[128,256]{1,0:T(8,128)S(1)}, f32[128,256]{1,0:T(8,128)S(1)}, u32[]{:S(2)}, u32[]{:S(2)}) collective-permute-start(f32[128,256]{1,0:T(8,128)S(1)} %get-tuple-element.75), channel_id=1, source_target_pairs={{0,4},{1,5},{2,6},{3,7},{4,8},{5,9},{6,10},{7,11},{8,12},{9,13},{1... | collective-permute-start | bytes 393224 | tf_op jit(solution)/shard_map/ppermute | solution.py:38
  29.4 9.3 %collective-permute-start.23 = (f32[128,256]{1,0:T(8,128)S(1)}, f32[128,256]{1,0:T(8,128)S(1)}, u32[]{:S(2)}, u32[]{:S(2)}) collective-permute-start(f32[128,256]{1,0:T(8,128)S(1)} %add_add_fusion.5.refs_6_), channel_id=1, source_target_pairs={{0,3},{1,2},{2,1},{3,0},{4,7},{5,6},{6,5},{7,4},{8,11},{9,10},{10,... | collective-permute-start | bytes 393224 | tf_op jit(solution)/shard_map/ppermute | solution.py:38
  34.1 7.8 %collective-permute-start.22 = (f32[128,256]{1,0:T(8,128)S(1)}, f32[128,256]{1,0:T(8,128)S(1)}, u32[]{:S(2)}, u32[]{:S(2)}) collective-permute-start(f32[128,256]{1,0:T(8,128)S(1)} %add_add_fusion.5.refs_6_), channel_id=1, source_target_pairs={{0,2},{1,3},{2,0},{3,1},{4,6},{5,7},{6,4},{7,5},{8,10},{9,11},{10,... | collective-permute-start | bytes 393224 | tf_op jit(solution)/shard_map/ppermute | solution.py:38
  34.2 7.7 %collective-permute-start.21 = (f32[128,256]{1,0:T(8,128)S(1)}, f32[128,256]{1,0:T(8,128)S(1)}, u32[]{:S(2)}, u32[]{:S(2)}) collective-permute-start(f32[128,256]{1,0:T(8,128)S(1)} %add_add_fusion.5.refs_6_), channel_id=1, source_target_pairs={{0,1},{1,0},{2,3},{3,2},{4,5},{5,4},{6,7},{7,6},{8,9},{9,8},{10,11... | collective-permute-start | bytes 393224 | tf_op jit(solution)/shard_map/ppermute | solution.py:38
  36.7 10.1 %collective-permute-start.16 = (f32[128,256]{1,0:T(8,128)S(1)}, f32[128,256]{1,0:T(8,128)S(1)}, u32[]{:S(2)}, u32[]{:S(2)}) collective-permute-start(f32[128,256]{1,0:T(8,128)S(1)} %add_add_fusion.4.refs_6_), channel_id=1, source_target_pairs={{0,3},{1,2},{2,1},{3,0},{4,7},{5,6},{6,5},{7,4},{8,11},{9,10},{10,... | collective-permute-start | bytes 393224 | tf_op jit(solution)/shard_map/ppermute | solution.py:38
  38.1 8.7 %collective-permute-start.15 = (f32[128,256]{1,0:T(8,128)S(1)}, f32[128,256]{1,0:T(8,128)S(1)}, u32[]{:S(2)}, u32[]{:S(2)}) collective-permute-start(f32[128,256]{1,0:T(8,128)S(1)} %add_add_fusion.4.refs_6_), channel_id=1, source_target_pairs={{0,2},{1,3},{2,0},{3,1},{4,6},{5,7},{6,4},{7,5},{8,10},{9,11},{10,... | collective-permute-start | bytes 393224 | tf_op jit(solution)/shard_map/ppermute | solution.py:38
  38.7 8.5 %collective-permute-start.14 = (f32[128,256]{1,0:T(8,128)S(1)}, f32[128,256]{1,0:T(8,128)S(1)}, u32[]{:S(2)}, u32[]{:S(2)}) collective-permute-start(f32[128,256]{1,0:T(8,128)S(1)} %add_add_fusion.4.refs_6_), channel_id=1, source_target_pairs={{0,1},{1,0},{2,3},{3,2},{4,5},{5,4},{6,7},{7,6},{8,9},{9,8},{10,11... | collective-permute-start | bytes 393224 | tf_op jit(solution)/shard_map/ppermute | solution.py:38
  43.8 8.2 %collective-permute-start.24 = (f32[128,256]{1,0:T(8,128)S(1)}, f32[128,256]{1,0:T(8,128)S(1)}, u32[]{:S(2)}, u32[]{:S(2)}) collective-permute-start(f32[128,256]{1,0:T(8,128)S(1)} %get-tuple-element.98), channel_id=1, source_target_pairs={{0,7},{1,6},{2,5},{3,4},{4,11},{5,10},{6,9},{7,8},{8,15},{9,14},{1... | collective-permute-start | bytes 393224 | tf_op jit(solution)/shard_map/ppermute | solution.py:38
  43.9 8.7 %collective-permute-start.25 = (f32[128,256]{1,0:T(8,128)S(1)}, f32[128,256]{1,0:T(8,128)S(1)}, u32[]{:S(2)}, u32[]{:S(2)}) collective-permute-start(f32[128,256]{1,0:T(8,128)S(1)} %get-tuple-element.99), channel_id=1, source_target_pairs={{0,5},{1,4},{2,7},{3,6},{4,9},{5,8},{6,11},{7,10},{8,13},{9,12},{1... | collective-permute-start | bytes 393224 | tf_op jit(solution)/shard_map/ppermute | solution.py:38
  46.8 8.2 %collective-permute-start.26 = (f32[128,256]{1,0:T(8,128)S(1)}, f32[128,256]{1,0:T(8,128)S(1)}, u32[]{:S(2)}, u32[]{:S(2)}) collective-permute-start(f32[128,256]{1,0:T(8,128)S(1)} %get-tuple-element.100), channel_id=1, source_target_pairs={{0,6},{1,7},{2,4},{3,5},{4,10},{5,11},{6,8},{7,9},{8,14},{9,15},{1... | collective-permute-start | bytes 393224 | tf_op jit(solution)/shard_map/ppermute | solution.py:38
  46.8 8.2 %collective-permute-start.27 = (f32[128,256]{1,0:T(8,128)S(1)}, f32[128,256]{1,0:T(8,128)S(1)}, u32[]{:S(2)}, u32[]{:S(2)}) collective-permute-start(f32[128,256]{1,0:T(8,128)S(1)} %get-tuple-element.101), channel_id=1, source_target_pairs={{0,4},{1,5},{2,6},{3,7},{4,8},{5,9},{6,10},{7,11},{8,12},{9,13},{1... | collective-permute-start | bytes 393224 | tf_op jit(solution)/shard_map/ppermute | solution.py:38
  48.8 10.4 %collective-permute-start.17 = (f32[128,256]{1,0:T(8,128)S(1)}, f32[128,256]{1,0:T(8,128)S(1)}, u32[]{:S(2)}, u32[]{:S(2)}) collective-permute-start(f32[128,256]{1,0:T(8,128)S(1)} %get-tuple-element.93), channel_id=1, source_target_pairs={{0,7},{1,6},{2,5},{3,4},{4,11},{5,10},{6,9},{7,8},{8,15},{9,14},{1... | collective-permute-start | bytes 393224 | tf_op jit(solution)/shard_map/ppermute | solution.py:38
  52.1 8.8 %collective-permute-start.18 = (f32[128,256]{1,0:T(8,128)S(1)}, f32[128,256]{1,0:T(8,128)S(1)}, u32[]{:S(2)}, u32[]{:S(2)}) collective-permute-start(f32[128,256]{1,0:T(8,128)S(1)} %get-tuple-element.94), channel_id=1, source_target_pairs={{0,5},{1,4},{2,7},{3,6},{4,9},{5,8},{6,11},{7,10},{8,13},{9,12},{1... | collective-permute-start | bytes 393224 | tf_op jit(solution)/shard_map/ppermute | solution.py:38
  52.6 9.2 %collective-permute-start.19 = (f32[128,256]{1,0:T(8,128)S(1)}, f32[128,256]{1,0:T(8,128)S(1)}, u32[]{:S(2)}, u32[]{:S(2)}) collective-permute-start(f32[128,256]{1,0:T(8,128)S(1)} %get-tuple-element.95), channel_id=1, source_target_pairs={{0,6},{1,7},{2,4},{3,5},{4,10},{5,11},{6,8},{7,9},{8,14},{9,15},{1... | collective-permute-start | bytes 393224 | tf_op jit(solution)/shard_map/ppermute | solution.py:38
  55.0 6.9 %collective-permute-start.20 = (f32[128,256]{1,0:T(8,128)S(1)}, f32[128,256]{1,0:T(8,128)S(1)}, u32[]{:S(2)}, u32[]{:S(2)}) collective-permute-start(f32[128,256]{1,0:T(8,128)S(1)} %get-tuple-element.96), channel_id=1, source_target_pairs={{0,4},{1,5},{2,6},{3,7},{4,8},{5,9},{6,10},{7,11},{8,12},{9,13},{1... | collective-permute-start | bytes 393224 | tf_op jit(solution)/shard_map/ppermute | solution.py:38
  55.0 10.0 %collective-permute-start.37 = (f32[128,256]{1,0:T(8,128)S(1)}, f32[128,256]{1,0:T(8,128)S(1)}, u32[]{:S(2)}, u32[]{:S(2)}) collective-permute-start(f32[128,256]{1,0:T(8,128)S(1)} %add_add_fusion.3.refs_6_), channel_id=1, source_target_pairs={{0,3},{1,2},{2,1},{3,0},{4,7},{5,6},{6,5},{7,4},{8,11},{9,10},{10,... | collective-permute-start | bytes 393224 | tf_op jit(solution)/shard_map/ppermute | solution.py:38
  59.2 6.9 %collective-permute-start.36 = (f32[128,256]{1,0:T(8,128)S(1)}, f32[128,256]{1,0:T(8,128)S(1)}, u32[]{:S(2)}, u32[]{:S(2)}) collective-permute-start(f32[128,256]{1,0:T(8,128)S(1)} %add_add_fusion.3.refs_6_), channel_id=1, source_target_pairs={{0,2},{1,3},{2,0},{3,1},{4,6},{5,7},{6,4},{7,5},{8,10},{9,11},{10,... | collective-permute-start | bytes 393224 | tf_op jit(solution)/shard_map/ppermute | solution.py:38
  60.9 5.2 %collective-permute-start.35 = (f32[128,256]{1,0:T(8,128)S(1)}, f32[128,256]{1,0:T(8,128)S(1)}, u32[]{:S(2)}, u32[]{:S(2)}) collective-permute-start(f32[128,256]{1,0:T(8,128)S(1)} %add_add_fusion.3.refs_6_), channel_id=1, source_target_pairs={{0,1},{1,0},{2,3},{3,2},{4,5},{5,4},{6,7},{7,6},{8,9},{9,8},{10,11... | collective-permute-start | bytes 393224 | tf_op jit(solution)/shard_map/ppermute | solution.py:38
  61.9 9.6 %collective-permute-start.30 = (f32[128,256]{1,0:T(8,128)S(1)}, f32[128,256]{1,0:T(8,128)S(1)}, u32[]{:S(2)}, u32[]{:S(2)}) collective-permute-start(f32[128,256]{1,0:T(8,128)S(1)} %add_add_fusion.2.refs_6_), channel_id=1, source_target_pairs={{0,3},{1,2},{2,1},{3,0},{4,7},{5,6},{6,5},{7,4},{8,11},{9,10},{10,... | collective-permute-start | bytes 393224 | tf_op jit(solution)/shard_map/ppermute | solution.py:38
  64.3 7.8 %collective-permute-start.29 = (f32[128,256]{1,0:T(8,128)S(1)}, f32[128,256]{1,0:T(8,128)S(1)}, u32[]{:S(2)}, u32[]{:S(2)}) collective-permute-start(f32[128,256]{1,0:T(8,128)S(1)} %add_add_fusion.2.refs_6_), channel_id=1, source_target_pairs={{0,2},{1,3},{2,0},{3,1},{4,6},{5,7},{6,4},{7,5},{8,10},{9,11},{10,... | collective-permute-start | bytes 393224 | tf_op jit(solution)/shard_map/ppermute | solution.py:38
  65.0 8.3 %collective-permute-start.28 = (f32[128,256]{1,0:T(8,128)S(1)}, f32[128,256]{1,0:T(8,128)S(1)}, u32[]{:S(2)}, u32[]{:S(2)}) collective-permute-start(f32[128,256]{1,0:T(8,128)S(1)} %add_add_fusion.2.refs_6_), channel_id=1, source_target_pairs={{0,1},{1,0},{2,3},{3,2},{4,5},{5,4},{6,7},{7,6},{8,9},{9,8},{10,11... | collective-permute-start | bytes 393224 | tf_op jit(solution)/shard_map/ppermute | solution.py:38
  67.8 10.4 %collective-permute-start.38 = (f32[128,256]{1,0:T(8,128)S(1)}, f32[128,256]{1,0:T(8,128)S(1)}, u32[]{:S(2)}, u32[]{:S(2)}) collective-permute-start(f32[128,256]{1,0:T(8,128)S(1)} %get-tuple-element.120), channel_id=1, source_target_pairs={{0,7},{1,6},{2,5},{3,4},{4,11},{5,10},{6,9},{7,8},{8,15},{9,14},{1... | collective-permute-start | bytes 393224 | tf_op jit(solution)/shard_map/ppermute | solution.py:38
  70.2 8.6 %collective-permute-start.39 = (f32[128,256]{1,0:T(8,128)S(1)}, f32[128,256]{1,0:T(8,128)S(1)}, u32[]{:S(2)}, u32[]{:S(2)}) collective-permute-start(f32[128,256]{1,0:T(8,128)S(1)} %get-tuple-element.121), channel_id=1, source_target_pairs={{0,5},{1,4},{2,7},{3,6},{4,9},{5,8},{6,11},{7,10},{8,13},{9,12},{1... | collective-permute-start | bytes 393224 | tf_op jit(solution)/shard_map/ppermute | solution.py:38
  71.6 8.6 %collective-permute-start.40 = (f32[128,256]{1,0:T(8,128)S(1)}, f32[128,256]{1,0:T(8,128)S(1)}, u32[]{:S(2)}, u32[]{:S(2)}) collective-permute-start(f32[128,256]{1,0:T(8,128)S(1)} %get-tuple-element.122), channel_id=1, source_target_pairs={{0,6},{1,7},{2,4},{3,5},{4,10},{5,11},{6,8},{7,9},{8,14},{9,15},{1... | collective-permute-start | bytes 393224 | tf_op jit(solution)/shard_map/ppermute | solution.py:38
  72.1 9.2 %collective-permute-start.41 = (f32[128,256]{1,0:T(8,128)S(1)}, f32[128,256]{1,0:T(8,128)S(1)}, u32[]{:S(2)}, u32[]{:S(2)}) collective-permute-start(f32[128,256]{1,0:T(8,128)S(1)} %get-tuple-element.123), channel_id=1, source_target_pairs={{0,4},{1,5},{2,6},{3,7},{4,8},{5,9},{6,10},{7,11},{8,12},{9,13},{1... | collective-permute-start | bytes 393224 | tf_op jit(solution)/shard_map/ppermute | solution.py:38
  75.8 10.1 %collective-permute-start.31 = (f32[128,256]{1,0:T(8,128)S(1)}, f32[128,256]{1,0:T(8,128)S(1)}, u32[]{:S(2)}, u32[]{:S(2)}) collective-permute-start(f32[128,256]{1,0:T(8,128)S(1)} %get-tuple-element.115), channel_id=1, source_target_pairs={{0,7},{1,6},{2,5},{3,4},{4,11},{5,10},{6,9},{7,8},{8,15},{9,14},{1... | collective-permute-start | bytes 393224 | tf_op jit(solution)/shard_map/ppermute | solution.py:38
  78.2 7.7 %collective-permute-start.32 = (f32[128,256]{1,0:T(8,128)S(1)}, f32[128,256]{1,0:T(8,128)S(1)}, u32[]{:S(2)}, u32[]{:S(2)}) collective-permute-start(f32[128,256]{1,0:T(8,128)S(1)} %get-tuple-element.116), channel_id=1, source_target_pairs={{0,5},{1,4},{2,7},{3,6},{4,9},{5,8},{6,11},{7,10},{8,13},{9,12},{1... | collective-permute-start | bytes 393224 | tf_op jit(solution)/shard_map/ppermute | solution.py:38
  78.7 9.1 %collective-permute-start.33 = (f32[128,256]{1,0:T(8,128)S(1)}, f32[128,256]{1,0:T(8,128)S(1)}, u32[]{:S(2)}, u32[]{:S(2)}) collective-permute-start(f32[128,256]{1,0:T(8,128)S(1)} %get-tuple-element.117), channel_id=1, source_target_pairs={{0,6},{1,7},{2,4},{3,5},{4,10},{5,11},{6,8},{7,9},{8,14},{9,15},{1... | collective-permute-start | bytes 393224 | tf_op jit(solution)/shard_map/ppermute | solution.py:38
  80.1 7.9 %collective-permute-start.34 = (f32[128,256]{1,0:T(8,128)S(1)}, f32[128,256]{1,0:T(8,128)S(1)}, u32[]{:S(2)}, u32[]{:S(2)}) collective-permute-start(f32[128,256]{1,0:T(8,128)S(1)} %get-tuple-element.118), channel_id=1, source_target_pairs={{0,4},{1,5},{2,6},{3,7},{4,8},{5,9},{6,10},{7,11},{8,12},{9,13},{1... | collective-permute-start | bytes 393224 | tf_op jit(solution)/shard_map/ppermute | solution.py:38
